TPU v7x, 32 devices: a whole 2x2x4 slice. The times are simulated.
32 devices in a mesh: dp: 4 (over z), ctx: 4 (over y, x), tensor: 2 (over core).
Axes of the slice: x: 2, y: 2, z: 4, core: 2. Of those that a mesh axis runs over, the one named last changes fastest.
Arguments:
- tokens: bfloat16 [12288, 1152], P(('dp', 'ctx')), may hold values from -6 to 6
- out_cotangent: bfloat16 [12288, 1152], P(('dp', 'ctx')), may hold values from -6 to 6
- lengths: int32 [4, 4], P('dp'), may hold values from 1 to 2688, as said below
- norm_gains: float32 [1152, 4], P(('dp', 'ctx')), may hold values from 0.5 to 1.5
- gain_first: float32 [1152, 4], P(('dp', 'ctx')), may hold values from -112 to 112
- gain_second: float32 [1152, 4], P(('dp', 'ctx')), may hold values from 1474.56 to 5775.36
- head_gains: float32 [256, 2], P(('dp', 'ctx')), may hold values from 0.5 to 1.5
- head_first: float32 [256, 2], P(('dp', 'ctx')), may hold values from -224 to 224
- head_second: float32 [256, 2], P(('dp', 'ctx')), may hold values from 5898.24 to 23101.44
- query_weight: float32 [1152, 1024], P(('dp', 'ctx'), 'tensor'), may hold values from -0.1875 to 0.1875
- query_first: float32 [1152, 1024], P(('dp', 'ctx'), 'tensor'), may hold values from -112 to 112
- query_second: float32 [1152, 1024], P(('dp', 'ctx'), 'tensor'), may hold values from 1474.56 to 5775.36
- keyval_weight: float32 [1152, 512], P(('dp', 'ctx')), may hold values from -0.1875 to 0.1875
- keyval_first: float32 [1152, 512], P(('dp', 'ctx')), may hold values from -224 to 224
- keyval_second: float32 [1152, 512], P(('dp', 'ctx')), may hold values from 5898.24 to 23101.44
- output_weight: float32 [1152, 1024], P(('dp', 'ctx'), 'tensor'), may hold values from -0.1875 to 0.1875
- output_first: float32 [1152, 1024], P(('dp', 'ctx'), 'tensor'), may hold values from -112 to 112
- output_second: float32 [1152, 1024], P(('dp', 'ctx'), 'tensor'), may hold values from 1351.68 to 5406.72
- gate_up: float32 [1152, 2, 6912], P(('dp', 'ctx'), None, 'tensor'), may hold values from -0.1875 to 0.1875
- gate_first: float32 [1152, 2, 6912], P(('dp', 'ctx'), None, 'tensor'), may hold values from -32 to 32
- gate_second: float32 [1152, 2, 6912], P(('dp', 'ctx'), None, 'tensor'), may hold values from 114.2784 to 454.656
- down_weight: float32 [1152, 6912], P(('dp', 'ctx'), 'tensor'), may hold values from -0.078125 to 0.078125
- down_first: float32 [1152, 6912], P(('dp', 'ctx'), 'tensor'), may hold values from -64 to 64
- down_second: float32 [1152, 6912], P(('dp', 'ctx'), 'tensor'), may hold values from 646.3488 to 2580.48
Outputs:
- result: bfloat16 [12288, 1152], P(('dp', 'ctx'))
- input_grad: float32 [12288, 1152], P(('dp', 'ctx'))
- gains_new: float32 [1152, 4], P(('dp', 'ctx'))
- gain_first_new: float32 [1152, 4], P(('dp', 'ctx'))
- gain_second_new: float32 [1152, 4], P(('dp', 'ctx'))
- heads_new: float32 [256, 2], P(('dp', 'ctx'))
- head_first_new: float32 [256, 2], P(('dp', 'ctx'))
- head_second_new: float32 [256, 2], P(('dp', 'ctx'))
- query_new: float32 [1152, 1024], P(('dp', 'ctx'), 'tensor')
- query_first_new: float32 [1152, 1024], P(('dp', 'ctx'), 'tensor')
- query_second_new: float32 [1152, 1024], P(('dp', 'ctx'), 'tensor')
- keyval_new: float32 [1152, 512], P(('dp', 'ctx'))
- keyval_first_new: float32 [1152, 512], P(('dp', 'ctx'))
- keyval_second_new: float32 [1152, 512], P(('dp', 'ctx'))
- output_new: float32 [1152, 1024], P(('dp', 'ctx'), 'tensor')
- output_first_new: float32 [1152, 1024], P(('dp', 'ctx'), 'tensor')
- output_second_new: float32 [1152, 1024], P(('dp', 'ctx'), 'tensor')
- gate_new: float32 [1152, 2, 6912], P(('dp', 'ctx'), None, 'tensor')
- gate_first_new: float32 [1152, 2, 6912], P(('dp', 'ctx'), None, 'tensor')
- gate_second_new: float32 [1152, 2, 6912], P(('dp', 'ctx'), None, 'tensor')
- down_new: float32 [1152, 6912], P(('dp', 'ctx'), 'tensor')
- down_first_new: float32 [1152, 6912], P(('dp', 'ctx'), 'tensor')
- down_second_new: float32 [1152, 6912], P(('dp', 'ctx'), 'tensor')
Inputs may be any that keep to these rules, and one draw needn't show every extreme that they name: `lengths`: each row sums to 3072; exactly one entry of each row is 2688, the others sum to 384.
All inputs are finite; a program needn't handle non-finite values.
Results may differ from a plain program's by a relative error of at most 0.019.
The roundings to bfloat16 on the way count: a program that leaves them out, or rounds other values in their place, can miss the bound.
Values may be sent and summed in bfloat16 or wider, within the bound.
A program may use at most 256 MiB of HBM per device.

v0:
```python
import jax
import jax.numpy as jnp
import numpy as np
from jax import lax
from jax.sharding import PartitionSpec as P

D = 1152
HQ = 4
HD = 256
FF = 6912
WIN = 512
STEP = 10


norm_eps = 1e-06
beta_one = 0.9
beta_two = 0.95
adam_eps = 1e-08
decay_rate = 0.1
rope_base = 10000.0


def from_behind(block, axis, distance):
    devices = range(lax.axis_size(axis))
    route = [(i - distance, i) for i in devices if i - distance in devices]
    return lax.ppermute(block, axis, route)


def in_blocks(array, dim, length):
    shape = array.shape
    tiles = array.reshape(*shape[:dim], length, shape[dim] // length, *shape[dim + 1 :])
    return jnp.moveaxis(tiles, dim, 0)


def sent_and_summed(array, axis, dim):
    tiles = in_blocks(array, dim, lax.axis_size(axis))
    arrived = lax.all_to_all(tiles, axis, split_axis=0, concat_axis=0, tiled=True)
    return arrived.astype(jnp.float32).sum(axis=0)


def token_layout(lengths, places):
    stop_at = jnp.cumsum(lengths)
    start_at = stop_at - lengths
    segment = jnp.sum((places[:, None] >= stop_at[None, :]).astype(jnp.int32), axis=1)
    owned_by = segment[:, None] == jnp.arange(lengths.shape[0], dtype=jnp.int32)[None, :]
    seg_begin = jnp.sum(jnp.where(owned_by, start_at[None, :], 0), axis=1)
    return (segment, places - seg_begin)


def rope_tables(position):
    half_dim = HD // 2
    exponent = jnp.arange(half_dim, dtype=jnp.float32) * (2.0 / HD)
    inverse = jnp.power(jnp.float32(rope_base), -exponent)
    angles = position.astype(jnp.float32)[:, None] * inverse[None, :]
    return (jnp.cos(angles), jnp.sin(angles))


def rotate(values, cosine_table, sine_table):
    half_dim = values.shape[-1] // 2
    lower_part = values[..., :half_dim]
    upper_part = values[..., half_dim:]
    return jnp.concatenate(
        [
            lower_part * cosine_table - upper_part * sine_table,
            upper_part * cosine_table + lower_part * sine_table,
        ],
        axis=-1,
    )


def rms_norm(values, gain_row):
    scale = lax.rsqrt(jnp.mean(values * values, axis=-1, keepdims=True) + norm_eps)
    return values * scale * gain_row


def activate(gate_pair):
    return jax.nn.gelu(gate_pair[:, 0], approximate=True) * gate_pair[:, 1]


def contract_rows(left_side, right_side):
    return lax.dot_general(
        left_side, right_side, (((0,), (0,)), ((), ())), preferred_element_type=jnp.float32
    )


def contract_columns(left_side, right_side):
    return lax.dot_general(
        left_side, right_side, (((1,), (1,)), ((), ())), preferred_element_type=jnp.float32
    )


def adam_step(weight_value, gradient, first_moment, second_moment, step_rate, decay_factor):
    first_moment = beta_one * first_moment + (1.0 - beta_one) * gradient
    second_moment = beta_two * second_moment + (1.0 - beta_two) * gradient * gradient
    first_hat = first_moment / (1.0 - beta_one**STEP)
    second_hat = second_moment / (1.0 - beta_two**STEP)
    update = first_hat / (jnp.sqrt(second_hat) + adam_eps)
    return (
        weight_value - step_rate * (update + decay_factor * weight_value),
        first_moment,
        second_moment,
    )


def on_device(
    tokens,
    out_cotangent,
    lengths,
    norm_gains,
    gain_first,
    gain_second,
    head_gains,
    head_first,
    head_second,
    query_weight,
    query_first,
    query_second,
    keyval_weight,
    keyval_first,
    keyval_second,
    output_weight,
    output_first,
    output_second,
    gate_up,
    gate_first,
    gate_second,
    down_weight,
    down_first,
    down_second,
):
    row_count = tokens.shape[0]
    group_devices = lax.axis_size("ctx")
    ctx_place = lax.axis_index("ctx")
    score_scale = HD ** (-0.5)
    far_count = min((WIN - 1) // row_count + 1, group_devices - 1)
    distances = list(range(far_count, 0, -1))
    row_takes = [min(row_count, WIN - (distance - 1) * row_count) for distance in distances]
    offset_parts = [
        np.arange(row_count - rows_now, row_count) - distance * row_count
        for distance, rows_now in zip(distances, row_takes)
    ]
    offset_parts.append(np.arange(row_count))
    key_offsets = jnp.asarray(np.concatenate(offset_parts).astype(np.int32))
    key_count = int(sum(row_takes)) + row_count
    start_row = ctx_place * row_count
    query_places = start_row + jnp.arange(row_count, dtype=jnp.int32)
    key_places = (start_row + key_offsets).astype(jnp.int32)
    query_segment, query_position = token_layout(lengths[0], query_places)
    key_segment = token_layout(lengths[0], key_places)[0]
    query_cosine, query_sine = rope_tables(query_position)
    allowed = (
        (key_places[None, :] >= 0)
        & (query_segment[:, None] == key_segment[None, :])
        & (key_places[None, :] <= query_places[:, None])
        & (query_places[:, None] - key_places[None, :] < WIN)
    )
    gains_low = norm_gains.astype(jnp.bfloat16)
    heads_low = head_gains.astype(jnp.bfloat16)
    query_low = query_weight.astype(jnp.bfloat16)
    keyval_low = keyval_weight.astype(jnp.bfloat16)
    output_low = output_weight.astype(jnp.bfloat16)
    gate_low = gate_up.astype(jnp.bfloat16)
    down_low = down_weight.astype(jnp.bfloat16)
    full_query, full_keyval, full_output, full_gate, full_down, full_gains, full_heads = (
        lax.all_gather(query_low, ("dp", "ctx"), axis=0, tiled=True),
        lax.all_gather(keyval_low, ("dp", "ctx"), axis=0, tiled=True),
        lax.all_gather(output_low, ("dp", "ctx"), axis=0, tiled=True),
        lax.all_gather(gate_low, ("dp", "ctx"), axis=0, tiled=True),
        lax.all_gather(down_low, ("dp", "ctx"), axis=0, tiled=True),
        lax.all_gather(gains_low, ("dp", "ctx"), axis=0, tiled=True),
        lax.all_gather(heads_low, ("dp", "ctx"), axis=0, tiled=True),
    )
    gains_full = full_gains.astype(jnp.float32)
    heads_full = full_heads.astype(jnp.float32)
    inputs = tokens.astype(jnp.float32)
    normed_exact, norm_one_back = jax.vjp(rms_norm, inputs, gains_full[:, 0])
    normed_one = normed_exact.astype(jnp.bfloat16)
    query_lin = jnp.dot(normed_one, full_query, preferred_element_type=jnp.float32)
    keyval_lin = jnp.dot(normed_one, full_keyval, preferred_element_type=jnp.float32)
    head_count = query_lin.shape[1] // HD
    query_normed, query_norm_back = jax.vjp(
        rms_norm, query_lin.reshape(row_count, head_count, HD), heads_full[:, 0]
    )
    key_normed, key_norm_back = jax.vjp(rms_norm, keyval_lin[:, :HD], heads_full[:, 1])
    query_rot = rotate(query_normed, query_cosine[:, None, :], query_sine[:, None, :]).astype(
        jnp.bfloat16
    )
    key_rot = rotate(key_normed, query_cosine, query_sine)
    keyval_rot = jnp.concatenate([key_rot, keyval_lin[:, HD:]], axis=1).astype(jnp.bfloat16)
    key_pieces = []
    for distance, rows_now in zip(distances, row_takes):
        key_pieces.append(from_behind(keyval_rot[row_count - rows_now :], "ctx", distance))
    key_list = jnp.concatenate(key_pieces + [keyval_rot], axis=0)
    key_all = key_list[:, :HD]
    value_all = key_list[:, HD:]
    scores = (
        jnp.einsum("qhd,kd->hqk", query_rot, key_all, preferred_element_type=jnp.float32)
        * score_scale
    )
    masked = jnp.where(allowed[None], scores, -1e30)
    row_max = jnp.max(masked, axis=-1, keepdims=True)
    exp_values = jnp.exp(masked - row_max)
    row_total = jnp.sum(exp_values, axis=-1, keepdims=True)
    prob_values = exp_values / row_total
    log_total = row_max + jnp.log(row_total)
    attended = jnp.einsum(
        "hqk,kd->qhd",
        prob_values.astype(jnp.bfloat16),
        value_all,
        preferred_element_type=jnp.float32,
    )
    attended_low = attended.astype(jnp.bfloat16).reshape(row_count, head_count * HD)
    branch_raw = lax.psum(
        contract_columns(attended_low, full_output).astype(jnp.bfloat16), "tensor"
    ).astype(jnp.float32)
    branch, post_one_back = jax.vjp(rms_norm, branch_raw, gains_full[:, 1])
    middle = inputs + branch
    normed_exact_two, norm_two_back = jax.vjp(rms_norm, middle, gains_full[:, 2])
    normed_two = normed_exact_two.astype(jnp.bfloat16)
    gate_lin = jnp.einsum("td,dcf->tcf", normed_two, full_gate, preferred_element_type=jnp.float32)
    hidden, activate_back = jax.vjp(activate, gate_lin)
    hidden_low = hidden.astype(jnp.bfloat16)
    mlp_raw = lax.psum(
        contract_columns(hidden_low, full_down).astype(jnp.bfloat16), "tensor"
    ).astype(jnp.float32)
    mlp_out, post_two_back = jax.vjp(rms_norm, mlp_raw, gains_full[:, 3])
    result = (middle + mlp_out).astype(jnp.bfloat16)
    kept_weights = lax.optimization_barrier(
        ((query_low, keyval_low, output_low, gate_low, down_low), result)
    )[0]
    kept_query, kept_keyval, kept_output, kept_gate, kept_down = kept_weights
    full_query, full_keyval, full_output, full_gate, full_down = (
        lax.all_gather(kept_query, ("dp", "ctx"), axis=0, tiled=True),
        lax.all_gather(kept_keyval, ("dp", "ctx"), axis=0, tiled=True),
        lax.all_gather(kept_output, ("dp", "ctx"), axis=0, tiled=True),
        lax.all_gather(kept_gate, ("dp", "ctx"), axis=0, tiled=True),
        lax.all_gather(kept_down, ("dp", "ctx"), axis=0, tiled=True),
    )
    cotangent_f = out_cotangent.astype(jnp.float32)
    mlp_pre_grad, gain_three_grad = post_two_back(cotangent_f)
    mlp_raw_low = mlp_pre_grad.astype(jnp.bfloat16)
    hidden_grad = jnp.dot(mlp_raw_low, full_down, preferred_element_type=jnp.float32)
    gate_grad = activate_back(hidden_grad)[0].astype(jnp.bfloat16)
    normed_two_part = jnp.einsum(
        "tcf,dcf->td", gate_grad, full_gate, preferred_element_type=jnp.float32
    )
    normed_two_grad = lax.psum(normed_two_part.astype(jnp.bfloat16), "tensor").astype(jnp.float32)
    gate_term = jnp.einsum("td,tcf->dcf", normed_two, gate_grad, preferred_element_type=jnp.float32)
    down_term = contract_rows(mlp_raw_low, hidden_low)
    mlp_reduced = lax.psum_scatter(
        jnp.concatenate([gate_term, down_term[:, None, :]], axis=1),
        ("dp", "ctx"),
        scatter_dimension=0,
        tiled=True,
    )
    gate_reduced = mlp_reduced[:, :2]
    down_reduced = mlp_reduced[:, 2]
    middle_part, gain_two_grad = norm_two_back(normed_two_grad)
    middle_grad = cotangent_f + middle_part
    branch_pre_grad, gain_one_grad = post_one_back(middle_grad)
    branch_low = branch_pre_grad.astype(jnp.bfloat16)
    output_w_grad = contract_rows(branch_low, attended_low)
    attended_grad = (
        jnp.dot(branch_low, full_output, preferred_element_type=jnp.float32)
        .astype(jnp.bfloat16)
        .reshape(row_count, head_count, HD)
    )
    scores_again = (
        jnp.einsum("qhd,kd->hqk", query_rot, key_all, preferred_element_type=jnp.float32)
        * score_scale
    )
    prob_again = jnp.exp(jnp.where(allowed[None], scores_again, -1e30) - log_total)
    probs_grad = jnp.einsum(
        "qhd,kd->hqk", attended_grad, value_all, preferred_element_type=jnp.float32
    )
    value_grad_all = jnp.einsum(
        "hqk,qhd->kd",
        prob_again.astype(jnp.bfloat16),
        attended_grad,
        preferred_element_type=jnp.float32,
    )
    row_delta = jnp.sum(prob_again * probs_grad, axis=-1, keepdims=True)
    score_grad = (prob_again * (probs_grad - row_delta)).astype(jnp.bfloat16)
    query_rot_grad = (
        jnp.einsum("hqk,kd->qhd", score_grad, key_all, preferred_element_type=jnp.float32)
        * score_scale
    )
    key_grad_all = (
        jnp.einsum("hqk,qhd->kd", score_grad, query_rot, preferred_element_type=jnp.float32)
        * score_scale
    )
    keyval_grad_all = jnp.concatenate([key_grad_all, value_grad_all], axis=1)
    own_grad = keyval_grad_all[key_count - row_count :]
    cursor = 0
    for distance, rows_now in zip(distances, row_takes):
        returned = from_behind(
            keyval_grad_all[cursor : cursor + rows_now].astype(jnp.bfloat16), "ctx", -distance
        ).astype(jnp.float32)
        own_grad = own_grad.at[row_count - rows_now :].add(returned)
        cursor = cursor + rows_now
    query_normed_grad = rotate(query_rot_grad, query_cosine[:, None, :], -query_sine[:, None, :])
    query_pre_grad, head_zero_part = query_norm_back(query_normed_grad)
    query_lin_grad = query_pre_grad.reshape(row_count, head_count * HD).astype(jnp.bfloat16)
    normed_one_part = contract_columns(query_lin_grad, full_query)
    normed_one_sum, keyval_grad_sum, head_zero_grad = (
        lax.psum(normed_one_part.astype(jnp.bfloat16), "tensor").astype(jnp.float32),
        lax.psum(own_grad.astype(jnp.bfloat16), "tensor").astype(jnp.float32),
        lax.psum(head_zero_part.astype(jnp.bfloat16), "tensor").astype(jnp.float32),
    )
    key_normed_grad = rotate(keyval_grad_sum[:, :HD], query_cosine, -query_sine)
    key_pre_grad, head_one_grad = key_norm_back(key_normed_grad)
    keyval_lin_grad = jnp.concatenate([key_pre_grad, keyval_grad_sum[:, HD:]], axis=1).astype(
        jnp.bfloat16
    )
    normed_one_grad = normed_one_sum + contract_columns(keyval_lin_grad, full_keyval)
    query_w_grad = contract_rows(normed_one, query_lin_grad)
    keyval_w_grad = contract_rows(normed_one, keyval_lin_grad)
    input_part, gain_zero_grad = norm_one_back(normed_one_grad)
    input_grad = middle_grad + input_part
    gains_grad = jnp.stack([gain_zero_grad, gain_one_grad, gain_two_grad, gain_three_grad], axis=1)
    heads_grad = jnp.stack([head_zero_grad, head_one_grad], axis=1)
    query_reduced, keyval_reduced, output_reduced, gains_reduced, heads_reduced = (
        sent_and_summed(query_w_grad.astype(jnp.bfloat16), ("dp", "ctx"), 0),
        sent_and_summed(keyval_w_grad.astype(jnp.bfloat16), ("dp", "ctx"), 0),
        sent_and_summed(output_w_grad.astype(jnp.bfloat16), ("dp", "ctx"), 0),
        sent_and_summed(gains_grad.astype(jnp.bfloat16), ("dp", "ctx"), 0),
        sent_and_summed(heads_grad.astype(jnp.bfloat16), ("dp", "ctx"), 0),
    )
    gains_new, gain_first_new, gain_second_new = adam_step(
        norm_gains, gains_reduced, gain_first, gain_second, 0.5, 0.0
    )
    heads_new, head_first_new, head_second_new = adam_step(
        head_gains, heads_reduced, head_first, head_second, 0.5, 0.0
    )
    query_new, query_first_new, query_second_new = adam_step(
        query_weight, query_reduced, query_first, query_second, D ** (-0.5), decay_rate
    )
    keyval_new, keyval_first_new, keyval_second_new = adam_step(
        keyval_weight, keyval_reduced, keyval_first, keyval_second, D ** (-0.5), decay_rate
    )
    output_new, output_first_new, output_second_new = adam_step(
        output_weight, output_reduced, output_first, output_second, (HQ * HD) ** (-0.5), decay_rate
    )
    gate_new, gate_first_new, gate_second_new = adam_step(
        gate_up, gate_reduced, gate_first, gate_second, D ** (-0.5), decay_rate
    )
    down_new, down_first_new, down_second_new = adam_step(
        down_weight, down_reduced, down_first, down_second, FF ** (-0.5), decay_rate
    )
    return (
        result,
        input_grad,
        gains_new,
        gain_first_new,
        gain_second_new,
        heads_new,
        head_first_new,
        head_second_new,
        query_new,
        query_first_new,
        query_second_new,
        keyval_new,
        keyval_first_new,
        keyval_second_new,
        output_new,
        output_first_new,
        output_second_new,
        gate_new,
        gate_first_new,
        gate_second_new,
        down_new,
        down_first_new,
        down_second_new,
    )


def solution(mesh):
    placed = (
        P(("dp", "ctx"), None),
        P(("dp", "ctx"), None),
        P("dp", None),
        P(("dp", "ctx"), None),
        P(("dp", "ctx"), None),
        P(("dp", "ctx"), None),
        P(("dp", "ctx"), None),
        P(("dp", "ctx"), None),
        P(("dp", "ctx"), None),
        P(("dp", "ctx"), "tensor"),
        P(("dp", "ctx"), "tensor"),
        P(("dp", "ctx"), "tensor"),
        P(("dp", "ctx"), None),
        P(("dp", "ctx"), None),
        P(("dp", "ctx"), None),
        P(("dp", "ctx"), "tensor"),
        P(("dp", "ctx"), "tensor"),
        P(("dp", "ctx"), "tensor"),
        P(("dp", "ctx"), None, "tensor"),
        P(("dp", "ctx"), None, "tensor"),
        P(("dp", "ctx"), None, "tensor"),
        P(("dp", "ctx"), "tensor"),
        P(("dp", "ctx"), "tensor"),
        P(("dp", "ctx"), "tensor"),
    )
    return jax.shard_map(
        on_device,
        mesh=mesh,
        in_specs=placed,
        out_specs=(
            P(("dp", "ctx"), None),
            P(("dp", "ctx"), None),
            P(("dp", "ctx"), None),
            P(("dp", "ctx"), None),
            P(("dp", "ctx"), None),
            P(("dp", "ctx"), None),
            P(("dp", "ctx"), None),
            P(("dp", "ctx"), None),
            P(("dp", "ctx"), "tensor"),
            P(("dp", "ctx"), "tensor"),
            P(("dp", "ctx"), "tensor"),
            P(("dp", "ctx"), None),
            P(("dp", "ctx"), None),
            P(("dp", "ctx"), None),
            P(("dp", "ctx"), "tensor"),
            P(("dp", "ctx"), "tensor"),
            P(("dp", "ctx"), "tensor"),
            P(("dp", "ctx"), None, "tensor"),
            P(("dp", "ctx"), None, "tensor"),
            P(("dp", "ctx"), None, "tensor"),
            P(("dp", "ctx"), "tensor"),
            P(("dp", "ctx"), "tensor"),
            P(("dp", "ctx"), "tensor"),
        ),
        check_vma=False,
    )
```

profile of v0, /device:TPU:9, one launch (start us, length us, event | category | flops | bytes accessed | tf_op | source)
XLA Modules:
  0.0 1840.1 jit_solution(6868812776451276003)
XLA Ops:
  19.5 27.5 %all-gather.1 = bf16[16,16,2]{1,2,0:T(2,128)(2,1)S(1)} all-gather(bf16[1,16,2]{1,2,0:T(2,128)(2,1)S(1)} %convert_bitcast_fusion.1), channel_id=1, replica_groups=mesh['dp'=4,'ctx'=4,'tensor'=2] {'dp','ctx'}, dimensions={0}, use_global_device_ids=true | all-gather | bytes 1088 | tf_op jit(solution)/shard_map/all_gather | solution.py:171
  47.1 28.4 %all-gather = bf16[16,72,4]{1,2,0:T(4,128)(2,1)S(1)} all-gather(bf16[1,72,4]{1,2,0:T(4,128)(2,1)S(1)} %convert_bitcast_fusion), channel_id=1, replica_groups=mesh['dp'=4,'ctx'=4,'tensor'=2] {'dp','ctx'}, dimensions={0}, use_global_device_ids=true | all-gather | bytes 9792 | tf_op jit(solution)/shard_map/all_gather | solution.py:170
  82.7 42.3 %all-gather.15.cloned.1.call-done = bf16[1152,512]{1,0:T(8,128)(2,1)} async-done(((bf16[72,512]{1,0:T(8,128)(2,1)}), bf16[1152,512]{1,0:T(8,128)(2,1)}) %all-gather.15.cloned.1.call-update) | async-done | bytes 1179664 | tf_op jit(solution)/shard_map/all_gather | solution.py:165
  157.6 25.8 %all-gather.17.cloned.1.call-done = bf16[1152,512]{1,0:T(8,128)(2,1)} async-done(((bf16[72,512]{1,0:T(8,128)(2,1)}), bf16[1152,512]{1,0:T(8,128)(2,1)}) %all-gather.17.cloned.1.call-update) | async-done | bytes 1179664 | tf_op jit(solution)/shard_map/all_gather | solution.py:167
  191.1 18.7 %all-reduce.8.cloned.1.call-done = bf16[768,1152]{1,0:T(8,128)(2,1)} async-done(((bf16[768,1152]{1,0:T(8,128)(2,1)}), bf16[768,1152]{1,0:T(8,128)(2,1)}) %all-reduce.8.cloned.1.call-update) | async-done | bytes 1769488 | tf_op jit(solution)/shard_map/psum | solution.py:213
  215.5 179.9 %all-gather.19.cloned.1.call-done = bf16[1152,2,3456]{2,0,1:T(8,128)(2,1)} async-done(((bf16[72,2,3456]{2,0,1:T(8,128)(2,1)}), bf16[1152,2,3456]{2,0,1:T(8,128)(2,1)}) %all-gather.19.cloned.1.call-update) | async-done | bytes 15925264 | tf_op jit(solution)/shard_map/all_gather | solution.py:168
  395.3 21.2 %fusion.80 = f32[768,2,3456]{2,0,1:T(8,128)} fusion(bf16[1152,2,3456]{2,0,1:T(8,128)(2,1)} %all-gather.19.cloned.1.call-done, f32[1152]{0:T(1024)} %get-tuple-element.171, f32[768]{0:T(1024)S(1)} %fusion.85, bf16[768,1152]{1,0:T(8,128)(2,1)S(1)} %copy-done, bf16[768,1152]{1,0:T(8,128)(2,1)S(1)} %copy-done.1, f32[1152]{0:T(1024)S(1)} %get-tuple-element.172, ...), kind=kOutput, calls=%fused_computation.183 | convolution fusion | flops 12237668352 | bytes 40713216 | tf_op jit(solution)/shard_map/td,dcf->tcf/dot_general | solution.py:220
  416.5 11.3 multiply_convert_fusion
  427.8 78.4 %all-gather.21.cloned.1.call-done = bf16[1152,3456]{1,0:T(8,128)(2,1)} async-done(((bf16[72,3456]{1,0:T(8,128)(2,1)}), bf16[1152,3456]{1,0:T(8,128)(2,1)}) %all-gather.21.cloned.1.call-update) | async-done | bytes 7962640 | tf_op jit(solution)/shard_map/all_gather | solution.py:169
  506.2 12.5 convolution_convert_fusion
  518.8 21.8 %all-reduce.10.cloned.1.call-done = bf16[768,1152]{1,0:T(8,128)(2,1)} async-done(((bf16[768,1152]{1,0:T(8,128)(2,1)}), bf16[768,1152]{1,0:T(8,128)(2,1)}) %all-reduce.10.cloned.1.call-update) | async-done | bytes 1769488 | tf_op jit(solution)/shard_map/psum | solution.py:223
  551.0 105.0 %all-gather.23.cloned.1.call-done = bf16[1152,3456]{1,0:T(8,128)(2,1)} async-done(((bf16[72,3456]{1,0:T(8,128)(2,1)}), bf16[1152,3456]{1,0:T(8,128)(2,1)}) %all-gather.23.cloned.1.call-update) | async-done | bytes 7962640 | tf_op jit(solution)/shard_map/all_gather | solution.py:237
  656.0 23.3 %multiply_bitcast_fusion = (f32[768,1,3456]{2,0,1:T(8,128)}, f32[768,1,3456]{2,0,1:T(8,128)}) fusion(f32[768,2,3456]{2,0,1:T(8,128)} %fusion.80, bf16[1152,3456]{1,0:T(8,128)(2,1)} %all-gather.23.cloned.1.call-done, bf16[768,1152]{1,0:T(8,128)(2,1)} %param.28, bf16[768,1152]{1,0:T(8,128)(2,1)} %all-reduce.10.cloned.1.call-done, ...), kind=kOutput, calls=%fused_computation.14 | convolution fusion | flops 6180765696 | bytes 53979648 | tf_op jit(solution)/shard_map/dot_general | solution.py:242
  679.3 161.8 %all-gather.25.cloned.1.call-done = bf16[1152,2,3456]{2,0,1:T(8,128)(2,1)} async-done(((bf16[72,2,3456]{2,0,1:T(8,128)(2,1)}), bf16[1152,2,3456]{2,0,1:T(8,128)(2,1)}) %all-gather.25.cloned.1.call-update) | async-done | bytes 15925264 | tf_op jit(solution)/shard_map/all_gather | solution.py:236
  841.1 20.3 %fusion.42 = bf16[768,1152]{1,0:T(8,128)(2,1)} fusion(bf16[1152,2,3456]{2,0,1:T(8,128)(2,1)} %all-gather.25.cloned.1.call-done, f32[768,1,3456]{2,0,1:T(8,128)} %get-tuple-element.199, f32[768,1,3456]{2,0,1:T(8,128)} %get-tuple-element.198), kind=kOutput, calls=%fused_computation.84 | convolution fusion | flops 12242092032 | bytes 38928384 | tf_op jit(solution)/shard_map/tcf,dcf->td/dot_general | solution.py:244
  867.0 16.5 all-reduce.12.cloned.1.call-done
  894.8 46.8 %all-gather.27.cloned.1.call-done = bf16[1152,512]{1,0:T(8,128)(2,1)} async-done(((bf16[72,512]{1,0:T(8,128)(2,1)}), bf16[1152,512]{1,0:T(8,128)(2,1)}) %all-gather.27.cloned.1.call-update) | async-done | bytes 1179664 | tf_op jit(solution)/shard_map/all_gather | solution.py:235
  944.8 7.7 fusion.7
  952.6 7.0 fusion.9
  982.5 18.9 %all-gather.29.cloned.1.call-done = bf16[1152,512]{1,0:T(8,128)(2,1)} async-done(((bf16[72,512]{1,0:T(8,128)(2,1)}), bf16[1152,512]{1,0:T(8,128)(2,1)}) %all-gather.29.cloned.1.call-update) | async-done | bytes 1179664 | tf_op jit(solution)/shard_map/all_gather | solution.py:233
  1008.6 13.4 convolution_bitcast_fusion
  1022.0 24.9 %fusion.54 = f32[1152,2,3456]{2,0,1:T(8,128)} fusion(f32[768,1,3456]{2,0,1:T(8,128)} %get-tuple-element.199, f32[768,1,3456]{2,0,1:T(8,128)} %get-tuple-element.198, f32[1152]{0:T(1024)S(1)} %copy-done.37, f32[768]{0:T(1024)S(1)} %fusion.85, bf16[768,1152]{1,0:T(8,128)(2,1)S(1)} %copy-done, bf16[768,1152]{1,0:T(8,128)(2,1)S(1)} %copy-done.1, ...), kind=kOutput, calls=%fused_computation.123 | convolution fusion | flops 12248285184 | bytes 56638464 | tf_op jit(solution)/shard_map/td,tcf->dcf/dot_general | solution.py:248
  1046.9 33.2 %pad_maximum_fusion = f32[1152,3,3456]{2,0,1:T(8,128)} fusion(f32[1152,1,3456]{2,0,1:T(8,128)} %convolution_bitcast_fusion, f32[1152,2,3456]{2,0,1:T(8,128)} %fusion.54), kind=kLoop, calls=%fused_computation | loop fusion | flops 11943936 | bytes 95551488 | tf_op jit(solution)/shard_map/concatenate | solution.py:251
  1093.4 37.6 %all-to-all-done.4 = bf16[16,72,512]{2,1,0:T(8,128)(2,1)S(1)} async-done(((bf16[16,72,512]{2,1,0:T(8,128)(2,1)}), bf16[16,72,512]{2,1,0:T(8,128)(2,1)S(1)}, u32[]{:S(2)}, u32[]{:S(2)}) %all-to-all-start.4) | async-done | bytes 1179680 | tf_op jit(solution)/shard_map/all_to_all | solution.py:37
  1131.0 6.6 all-to-all-start.2
  1138.1 10.1 psum.47
  1160.3 5.8 fusion.26
  1166.2 24.3 %all-to-all-done.2 = bf16[16,72,512]{2,1,0:T(8,128)(2,1)} async-done(((bf16[16,72,512]{2,1,0:T(8,128)(2,1)}), bf16[16,72,512]{2,1,0:T(8,128)(2,1)}, u32[]{:S(2)}, u32[]{:S(2)}) %all-to-all-start.2) | async-done | bytes 1179680 | tf_op jit(solution)/shard_map/all_to_all | solution.py:37
  1190.5 7.7 all-to-all-start.1
  1220.2 5.9 fusion.35
  1227.4 40.9 %all-to-all-done.3 = bf16[16,72,512]{2,1,0:T(8,128)(2,1)S(1)} async-done(((bf16[16,72,512]{2,1,0:T(8,128)(2,1)}), bf16[16,72,512]{2,1,0:T(8,128)(2,1)S(1)}, u32[]{:S(2)}, u32[]{:S(2)}) %all-to-all-start.3) | async-done | bytes 1179680 | tf_op jit(solution)/shard_map/all_to_all | solution.py:37
  1269.3 549.1 %reduce-scatter.2.cloned.1.call-done = f32[72,3,3456]{2,0,1:T(8,128)} async-done(((f32[1152,3,3456]{2,0,1:T(8,128)}), f32[72,3,3456]{2,0,1:T(8,128)}) %reduce-scatter.2.cloned.1.call-update) | async-done | bytes 2986000 | tf_op jit(solution)/shard_map/reduce_scatter | solution.py:250
  (324 shorter events, 190.4 us)
Async XLA Ops:
  7.2 71.8 %copy-start = (bf16[768,1152]{1,0:T(8,128)(2,1)S(1)}, bf16[768,1152]{1,0:T(8,128)(2,1)}, u32[]{:S(2)}) copy-start(bf16[768,1152]{1,0:T(8,128)(2,1)} %param.27) | copy-start | bytes 5308420
  7.2 71.8 %all-gather.13.cloned.1.call-start = ((), (), s32[]{:S(2)}) async-start(), calls=%async_computation.6 | async-start | bytes 1253376 | tf_op jit(solution)/shard_map/all_gather | solution.py:166
  8.9 116.0 %all-gather.15.cloned.1.call-start = ((), (), s32[]{:S(2)}) async-start(), calls=%async_computation.7 | async-start | bytes 1253376 | tf_op jit(solution)/shard_map/all_gather | solution.py:165
  10.6 172.8 %all-gather.17.cloned.1.call-start = ((), (), s32[]{:S(2)}) async-start(), calls=%async_computation.8 | async-start | bytes 1253376 | tf_op jit(solution)/shard_map/all_gather | solution.py:167
  12.2 197.6 %all-reduce.8.cloned.1.call-start = ((), (), s32[]{:S(2)}) async-start(), calls=%async_computation.9 | async-start | bytes 3538944 | tf_op jit(solution)/shard_map/psum | solution.py:213
  19.0 106.0 %copy-start.69 = (f32[768]{0:T(1024)}, f32[768]{0:T(1024)S(1)}, u32[]{:S(2)}) copy-start(f32[768]{0:T(1024)S(1)} %fusion.82) | copy-start | bytes 9220
  19.1 110.4 %copy-start.58 = (f32[768]{0:T(1024)}, f32[768]{0:T(1024)S(1)}, u32[]{:S(2)}) copy-start(f32[768]{0:T(1024)S(1)} %subtract_convert_fusion.1) | copy-start | bytes 9220
  47.1 82.3 %copy-start.67 = (f32[256,1]{0,1:T(1,128)}, f32[256,1]{0,1:T(1,128)S(1)}, u32[]{:S(2)}) copy-start(f32[256,1]{0,1:T(1,128)S(1)} %get-tuple-element.218) | copy-start | bytes 3076
  47.1 94.4 %copy-start.73 = (f32[256,1]{0,1:T(1,128)}, f32[256,1]{0,1:T(1,128)S(1)}, u32[]{:S(2)}) copy-start(f32[256,1]{0,1:T(1,128)S(1)} %get-tuple-element.219) | copy-start | bytes 3076
  76.3 48.7 %copy-start.60 = (f32[1152]{0:T(1024)}, f32[1152]{0:T(1024)S(1)}, u32[]{:S(2)}) copy-start(f32[1152]{0:T(1024)S(1)} %get-tuple-element.173) | copy-start | bytes 13828
  135.5 13.5 collective-permute-start
  187.1 208.2 %all-gather.19.cloned.1.call-start = ((), (), s32[]{:S(2)}) async-start(), calls=%async_computation.10 | async-start | bytes 16920576 | tf_op jit(solution)/shard_map/all_gather | solution.py:168
  189.9 316.3 %all-gather.21.cloned.1.call-start = ((), (), s32[]{:S(2)}) async-start(), calls=%async_computation.11 | async-start | bytes 8460288 | tf_op jit(solution)/shard_map/all_gather | solution.py:169
  190.8 349.8 %all-reduce.10.cloned.1.call-start = ((), (), s32[]{:S(2)}) async-start(), calls=%async_computation.12 | async-start | bytes 3538944 | tf_op jit(solution)/shard_map/psum | solution.py:223
  209.8 185.5 %copy-start.1 = (bf16[768,1152]{1,0:T(8,128)(2,1)S(1)}, bf16[768,1152]{1,0:T(8,128)(2,1)}, u32[]{:S(2)}) copy-start(bf16[768,1152]{1,0:T(8,128)(2,1)} %all-reduce.8.cloned.1.call-done) | copy-start | bytes 5308420
  518.7 137.3 %all-gather.23.cloned.1.call-start = ((), (), s32[]{:S(2)}) async-start(), calls=%async_computation.13 | async-start | bytes 8460288 | tf_op jit(solution)/shard_map/all_gather | solution.py:237
  548.5 292.6 %all-gather.25.cloned.1.call-start = ((), (), s32[]{:S(2)}) async-start(), calls=%async_computation.14 | async-start | bytes 16920576 | tf_op jit(solution)/shard_map/all_gather | solution.py:236
  549.2 334.2 %all-reduce.12.cloned.1.call-start = ((), (), s32[]{:S(2)}) async-start(), calls=%async_computation.15 | async-start | bytes 3538944 | tf_op jit(solution)/shard_map/psum | solution.py:247
  861.5 80.2 %all-gather.27.cloned.1.call-start = ((), (), s32[]{:S(2)}) async-start(), calls=%async_computation.16 | async-start | bytes 1253376 | tf_op jit(solution)/shard_map/all_gather | solution.py:235
  862.2 139.3 %all-gather.29.cloned.1.call-start = ((), (), s32[]{:S(2)}) async-start(), calls=%async_computation.17 | async-start | bytes 1253376 | tf_op jit(solution)/shard_map/all_gather | solution.py:233
  866.8 284.9 %all-reduce.14.cloned.1.call-start = ((), (), s32[]{:S(2)}) async-start(), calls=%async_computation.20 | async-start | bytes 5111808 | tf_op jit(solution)/shard_map/psum | solution.py:306
  967.9 37.7 %collective-permute-start.1 = (bf16[512,512]{0,1:T(8,128)(2,1)}, bf16[512,512]{0,1:T(8,128)(2,1)}, u32[]{:S(2)}, u32[]{:S(2)}) collective-permute-start(bf16[512,512]{0,1:T(8,128)(2,1)} %fusion.59), channel_id=1, source_target_pairs={{2,0},{4,2},{6,4},{3,1},{5,3},{7,5},{10,8},{12,10},{14,12},{11,9},... | collective-permute-start | bytes 1572872 | tf_op jit(solution)/shard_map/ppermute | solution.py:26
  1007.6 152.8 %all-gather.31.cloned.1.call-start = ((), (), s32[]{:S(2)}) async-start(), calls=%async_computation.18 | async-start | bytes 1253376 | tf_op jit(solution)/shard_map/all_gather | solution.py:234
  1008.1 810.2 %reduce-scatter.2.cloned.1.call-start = ((), (), s32[]{:S(2)}) async-start(), calls=%async_computation.19 | async-start | bytes 50761728 | tf_op jit(solution)/shard_map/reduce_scatter | solution.py:250
  1084.8 46.2 %all-to-all-start.4 = ((bf16[16,72,512]{2,1,0:T(8,128)(2,1)}), bf16[16,72,512]{2,1,0:T(8,128)(2,1)S(1)}, u32[]{:S(2)}, u32[]{:S(2)}) async-start(bf16[16,72,512]{2,1,0:T(8,128)(2,1)} %bitcast.151), calls=%async_computation.4 | async-start | bytes 2359296 | tf_op jit(solution)/shard_map/all_to_all | solution.py:37
  1089.9 60.0 %copy-start.32 = (f32[72,512]{1,0:T(8,128)S(1)}, f32[72,512]{1,0:T(8,128)}, u32[]{:S(2)}) copy-start(f32[72,512]{1,0:T(8,128)} %param.42) | copy-start | bytes 442372
  1131.0 59.5 %all-to-all-start.2 = ((bf16[16,72,512]{2,1,0:T(8,128)(2,1)}), bf16[16,72,512]{2,1,0:T(8,128)(2,1)}, u32[]{:S(2)}, u32[]{:S(2)}) async-start(bf16[16,72,512]{2,1,0:T(8,128)(2,1)} %bitcast.149), calls=%async_computation.2 | async-start | bytes 2359296 | tf_op jit(solution)/shard_map/all_to_all | solution.py:37
  1190.5 12.9 all-to-all-start.1
  1203.5 9.7 all-to-all-start
  1213.1 55.1 %all-to-all-start.3 = ((bf16[16,72,512]{2,1,0:T(8,128)(2,1)}), bf16[16,72,512]{2,1,0:T(8,128)(2,1)S(1)}, u32[]{:S(2)}, u32[]{:S(2)}) async-start(bf16[16,72,512]{2,1,0:T(8,128)(2,1)} %bitcast.150), calls=%async_computation.3 | async-start | bytes 2359296 | tf_op jit(solution)/shard_map/all_to_all | solution.py:37
  1220.2 48.2 %copy-start.34 = (f32[72,512]{1,0:T(8,128)S(1)}, f32[72,512]{1,0:T(8,128)}, u32[]{:S(2)}) copy-start(f32[72,512]{1,0:T(8,128)} %param.39) | copy-start | bytes 442372
  1220.2 48.2 %copy-start.44 = (f32[72,512]{1,0:T(8,128)S(1)}, f32[72,512]{1,0:T(8,128)}, u32[]{:S(2)}) copy-start(f32[72,512]{1,0:T(8,128)} %param.40) | copy-start | bytes 442372
  (75 other events, 861.1 us)
Sparse Core Ops, SparseCore 0:
  11.4 55.1 all-gather.12
  69.9 54.9 all-gather.14
  128.3 55.0 all-gather.16
  187.3 22.4 all-reduce.7
  213.4 181.8 all-gather.18
  398.8 107.3 all-gather.20
  518.8 21.7 all-reduce.9
  548.6 107.3 all-gather.22
  659.4 181.7 all-gather.24
  861.6 21.8 all-reduce.11
  887.2 54.3 all-gather.26
  945.3 56.1 all-gather.28
  1007.7 23.9 all-reduce.13
  1034.8 54.3 all-gather.30
  1095.2 723.0 reduce-scatter.1
where the time goes:
time: 1850 us; the launch traced here: 1840 us
  waiting for transfers between devices  1380 us (75%)
  matrix products  168 us (9%)
  other arithmetic  137 us (7%)
  blocking collectives  66.1 us (4%)
  starting transfers between devices  35.7 us (2%)
  local copies, waits for them, and re-layouts  35.1 us (2%)
    reduce_scatter x1, waiting for transfers between devices, on_device(): lax.psum_scatter(jnp.concatenate([gate_term, down_term[:, None, :]], axis...  549 us
    all_gather x1, waiting for transfers between devices, on_device(): lax.all_gather(gate_low, ('dp', 'ctx'), axis=0, tiled=True)  180 us
    all_gather x1, waiting for transfers between devices, on_device(): lax.all_gather(kept_gate, ('dp', 'ctx'), axis=0, tiled=True)  162 us
    all_to_all x5, waiting for transfers between devices, sent_and_summed(): lax.all_to_all(tiles, axis, split_axis=0, concat_axis=0, tiled=True)  110 us
    all_gather x1, waiting for transfers between devices, on_device(): lax.all_gather(kept_down, ('dp', 'ctx'), axis=0, tiled=True)  105 us
    all_gather x1, waiting for transfers between devices, on_device(): lax.all_gather(down_low, ('dp', 'ctx'), axis=0, tiled=True)  78.4 us
    all_gather x1, waiting for transfers between devices, on_device(): lax.all_gather(kept_output, ('dp', 'ctx'), axis=0, tiled=True)  46.8 us
    all_gather x1, waiting for transfers between devices, on_device(): lax.all_gather(query_low, ('dp', 'ctx'), axis=0, tiled=True)  42.3 us
  transfers between devices with their start and end apart: 22, of which 18 were waited for; matrix products, arithmetic and copies ran while one was open for 15% of the time, Pallas kernels for 0%

commit v1 on v0

v1 whole, which is shorter than its diff:
```python
import functools

import jax
import jax.numpy as jnp
import numpy as np
from jax import lax
from jax.experimental import pallas as pl
from jax.experimental.pallas import tpu as pltpu
from jax.sharding import PartitionSpec as P

D = 1152
HQ = 4
HD = 256
FF = 6912
WIN = 512
STEP = 10


norm_eps = 1e-06
beta_one = 0.9
beta_two = 0.95
adam_eps = 1e-08
decay_rate = 0.1
rope_base = 10000.0
GELU_SCALE = float(np.sqrt(2.0 / np.pi))
MESH = pl.DeviceIdType.MESH


def from_behind(block, axis, distance):
    devices = range(lax.axis_size(axis))
    route = [(i - distance, i) for i in devices if i - distance in devices]
    return lax.ppermute(block, axis, route)


def from_partner(block, axis, bits):
    return lax.ppermute(block, axis, [(i ^ bits, i) for i in range(lax.axis_size(axis))])


def along_line(tiles, axis):
    n = lax.axis_size(axis)
    if n > 4:
        return lax.all_to_all(tiles, axis, split_axis=0, concat_axis=0, tiled=True)
    place = lax.axis_index(axis)
    arrived = [lax.dynamic_index_in_dim(tiles, place, 0, keepdims=False)]
    for shift in range(1, n):
        tile = lax.dynamic_index_in_dim(tiles, lax.rem(place + shift, n), 0, keepdims=False)
        arrived.append(lax.ppermute(tile, axis, [(i, (i + shift) % n) for i in range(n)]))
    return jnp.stack(arrived)


def core_ordered(own, other):
    first = lax.axis_index("tensor") == 0
    return jnp.concatenate([jnp.where(first, own, other), jnp.where(first, other, own)], axis=0)


def half_of(array, dim):
    size = array.shape[dim] // 2
    return lax.dynamic_slice_in_dim(array, lax.axis_index("tensor") * size, size, axis=dim)


def half_not_of(array, dim):
    size = array.shape[dim] // 2
    return lax.dynamic_slice_in_dim(array, (1 - lax.axis_index("tensor")) * size, size, axis=dim)


def token_layout(lengths, places):
    stop_at = jnp.cumsum(lengths)
    start_at = stop_at - lengths
    segment = jnp.sum((places[:, None] >= stop_at[None, :]).astype(jnp.int32), axis=1)
    owned_by = segment[:, None] == jnp.arange(lengths.shape[0], dtype=jnp.int32)[None, :]
    seg_begin = jnp.sum(jnp.where(owned_by, start_at[None, :], 0), axis=1)
    return (segment, places - seg_begin)


def rope_tables(position):
    half_dim = HD // 2
    exponent = jnp.arange(half_dim, dtype=jnp.float32) * (2.0 / HD)
    inverse = jnp.power(jnp.float32(rope_base), -exponent)
    angles = position.astype(jnp.float32)[:, None] * inverse[None, :]
    return (jnp.cos(angles), jnp.sin(angles))


def rotate(values, cosine_table, sine_table):
    half_dim = values.shape[-1] // 2
    lower_part = values[..., :half_dim]
    upper_part = values[..., half_dim:]
    return jnp.concatenate(
        [
            lower_part * cosine_table - upper_part * sine_table,
            upper_part * cosine_table + lower_part * sine_table,
        ],
        axis=-1,
    )


def rms_norm(values, gain_row):
    scale = lax.rsqrt(jnp.mean(values * values, axis=-1, keepdims=True) + norm_eps)
    return values * scale * gain_row


def contract_rows(left_side, right_side):
    return lax.dot_general(
        left_side, right_side, (((0,), (0,)), ((), ())), preferred_element_type=jnp.float32
    )


def contract_columns(left_side, right_side):
    return lax.dot_general(
        left_side, right_side, (((1,), (1,)), ((), ())), preferred_element_type=jnp.float32
    )


def adam_step(weight_value, gradient, first_moment, second_moment, step_rate, decay_factor):
    first_moment = beta_one * first_moment + (1.0 - beta_one) * gradient
    second_moment = beta_two * second_moment + (1.0 - beta_two) * gradient * gradient
    first_hat = first_moment / (1.0 - beta_one**STEP)
    second_hat = second_moment / (1.0 - beta_two**STEP)
    update = first_hat / (jnp.sqrt(second_hat) + adam_eps)
    return (
        weight_value - step_rate * (update + decay_factor * weight_value),
        first_moment,
        second_moment,
    )


def places():
    return lax.axis_index("dp"), lax.axis_index("ctx"), lax.axis_index("tensor")


def plane_partners():
    dp, ctx, core = places()
    beside = ctx + 1 - 2 * lax.rem(ctx, 2)
    across = lax.rem(ctx + 2, 4)
    return (dp, beside, core), (dp, across, core), (dp, 3 - ctx, core), (dp, ctx, 1 - core)


def enter(n_dp, line):
    dp, ctx, core = places()
    barrier = pltpu.get_barrier_semaphore()

    def greet(device):
        pl.semaphore_signal(barrier, inc=1, device_id=device, device_id_type=MESH)

    for device in plane_partners():
        greet(device)
    if line:
        pl.when(dp < n_dp - 1)(lambda: greet((dp + 1, ctx, core)))
        pl.when(dp > 0)(lambda: greet((dp - 1, ctx, core)))
    ends = jnp.minimum(dp, 1) + jnp.minimum(n_dp - 1 - dp, 1) if line else 0
    pl.semaphore_wait(barrier, 4 + ends)


def in_columns(count, body):
    whole = count // 256

    def one(i, carry):
        body(pl.multiple_of(i * 256, 256), 256)
        return carry

    lax.fori_loop(0, whole, one, 0)
    if count % 256:
        body(whole * 256, count % 256)


def in_rows(count, body, start):
    size = 64

    def one(i, carry):
        return body(pl.multiple_of(i * size, size), size, carry)

    return lax.fori_loop(0, count // size, one, start)


def turned(values, cosine, sine):
    half_dim = values.shape[-1] // 2
    lower, upper = values[:, :half_dim], values[:, half_dim:]
    return jnp.concatenate([lower * cosine - upper * sine, upper * cosine + lower * sine], axis=1)


def scale_of(values):
    return lax.rsqrt(jnp.mean(values * values, axis=1, keepdims=True) + norm_eps)


def attend_kernel(
    n_dp,
    owned_heads,
    tokens,
    cosine,
    sine,
    lowest,
    attn_pack,
    mlp_pack,
    mlp_full,
    attn_full,
    gain_rows,
    head_rows,
    normed_out,
    lin,
    query_out,
    keyval_out,
    attended,
    log_total,
    branch_out,
    middle_out,
    normed_two,
    slots,
    wide_slots,
    keyval,
    partial,
    core_send,
    core_take,
    own_sem,
    mlp_plane_send,
    mlp_plane_recv,
    mlp_line_send,
    mlp_line_recv,
    attn_line_send,
    attn_line_recv,
    attn_plane_send,
    attn_plane_recv,
    keyval_send,
    keyval_recv,
):
    dp, ctx, core = places()
    x_dev, y_dev, far_dev, core_dev = plane_partners()
    plane = ((dp, ctx, core), x_dev, y_dev, far_dev)
    f32, bf16 = jnp.float32, jnp.bfloat16
    row_count, width = tokens.shape
    half = row_count // 2
    owned = attn_pack.shape[0]
    behind = keyval.shape[1] - row_count
    next_dev = (dp, ctx + 1, core)
    enter(n_dp, True)

    def remote(source, target, send, recv, device):
        return pltpu.make_async_remote_copy(
            src_ref=source, dst_ref=target, send_sem=send, recv_sem=recv, device_id=device,
            device_id_type=MESH,
        )

    def line_block(way, step, k):
        origin = dp - step if way == 0 else dp + step
        return origin * 4 + plane[k][1]

    def can_take(way, step):
        return dp >= step if way == 0 else dp <= n_dp - 1 - step

    def can_give(way):
        return dp < n_dp - 1 if way == 0 else dp > 0

    def line_dev(way):
        return (dp + 1, ctx, core) if way == 0 else (dp - 1, ctx, core)

    def mlp_hop(way, step, k):
        block = mlp_full.at[line_block(way, step, k)]
        index = (way * n_dp + step) * 4 + k
        return remote(block, block, mlp_line_send.at[index], mlp_line_recv.at[index], line_dev(way))

    def mlp_came(way, step, k):
        block = mlp_full.at[line_block(way, step, k)]
        index = (way * n_dp + step - 1) * 4 + k
        return remote(block, block, mlp_line_send.at[index], mlp_line_recv.at[index], line_dev(way))

    def attn_hop(way, step):
        block = slots.at[line_block(way, step, 0)]
        index = way * n_dp + step
        return remote(block, block, attn_line_send.at[index], attn_line_recv.at[index], line_dev(way))

    def attn_came(way, step):
        block = slots.at[line_block(way, step, 0)]
        index = way * n_dp + step - 1
        return remote(block, block, attn_line_send.at[index], attn_line_recv.at[index], line_dev(way))

    def each(step, act, give):
        for way in range(2):
            if give:
                fits = can_give(way) & can_take(way, step) if step else can_give(way)
            else:
                fits = can_take(way, step)
            pl.when(fits)(functools.partial(act, way))

    def attn_plane(way, step, side, came=False):
        from_k = {1: 0, 2: 0, 3: 1 if step % 2 == 0 else 2}[side]
        device = {1: x_dev, 2: y_dev, 3: y_dev if step % 2 == 0 else x_dev}[side]
        block = slots.at[line_block(way, step, side if came else from_k)]
        index = (way * n_dp + step) * 4 + side
        return remote(block, block, attn_plane_send.at[index], attn_plane_recv.at[index], device)

    own_attn = pltpu.make_async_copy(attn_pack, slots.at[dp * 4 + ctx], own_sem.at[0])
    own_mlp = pltpu.make_async_copy(mlp_pack.at[ctx], mlp_full.at[dp * 4 + ctx], own_sem.at[1])
    own_attn.start()
    own_mlp.start()
    own_attn.wait()
    each(0, lambda way: attn_hop(way, 0).start(), True)
    for side in (1, 2):
        attn_plane(0, 0, side).start()
    own_mlp.wait()
    each(0, lambda way: mlp_hop(way, 0, 0).start(), True)

    def mlp_plane(k, came=False):
        return remote(
            mlp_pack.at[plane[k][1]],
            mlp_full.at[dp * 4 + (plane[k][1] if came else ctx)],
            mlp_plane_send.at[k],
            mlp_plane_recv.at[k],
            plane[k],
        )

    for k in (1, 2, 3):
        mlp_plane(k).start()

    def came(way, step):
        attn_came(way, step).wait_recv()

    def hand_on(way, step):
        for side in (1, 2):
            attn_plane(way, step, side).start()

    for step in range(1, n_dp):
        each(step, lambda way: came(way, step), False)
        each(step, lambda way: attn_hop(way, step).start(), True)
        each(step, lambda way: hand_on(way, step), False)
    order = [(0, 0)] + [(way, step) for step in range(1, n_dp) for way in range(2)]

    def relay(way, step):
        for side in (1, 2):
            attn_plane(way, step, side, True).wait_recv()
        attn_plane(way, step, 3).start()

    def relayed(way, step):
        attn_plane(way, step, 3, True).wait_recv()

    def where_held(way, step, act):
        if step:
            pl.when(can_take(way, step))(lambda: act(way, step))
        else:
            act(way, step)

    for way, step in order:
        where_held(way, step, relay)

    def mlp_first(k):
        mlp_plane(k, True).wait_recv()
        each(0, lambda way: mlp_hop(way, 0, k).start(), True)

    def mlp_next(step, k):
        each(step, lambda way: mlp_came(way, step, k).wait_recv(), False)
        if step < n_dp - 1:
            each(step, lambda way: mlp_hop(way, step, k).start(), True)

    events = [functools.partial(mlp_first, k) for k in (1, 2, 3)] + [
        functools.partial(mlp_next, step, k) for step in range(1, n_dp) for k in range(4)
    ]
    events.reverse()

    def move(count):
        for _ in range(min(count, len(events))):
            events.pop()()

    move(2)
    for way, step in order:
        where_held(way, step, relayed)
    move(2)

    for block in range(n_dp * 4):
        wide_slots[block * owned : (block + 1) * owned, :] = slots[block].astype(f32)

    def narrow(first, size, carry):
        at = pl.ds(first, size)
        attn_full[at] = wide_slots[at].astype(bf16)
        return carry

    in_rows(width, narrow, 0)
    pick = lax.broadcasted_iota(jnp.int32, (8, 128), 0) == lax.broadcasted_iota(
        jnp.int32, (8, 128), 1
    )
    small = contract_columns(pick.astype(f32).astype(bf16), attn_full[:, 1280:1408])
    gain_rows[...] = small
    row_of = lax.broadcasted_iota(jnp.int32, (width, HD), 0)
    head_of = lax.broadcasted_iota(jnp.int32, (width, HD), 1)
    shift = owned_heads.bit_length() - 1
    chosen = row_of == (head_of >> shift) * owned + (head_of & (owned_heads - 1))
    heads = jnp.dot(
        small.astype(bf16), chosen.astype(f32).astype(bf16), preferred_element_type=f32
    )
    head_rows[...] = heads

    def normalize(first, size, carry):
        at = pl.ds(first, size)
        values = tokens[at].astype(f32)
        normed_out[at] = (values * scale_of(values) * gain_rows[0:1]).astype(bf16)
        return carry

    in_rows(row_count, normalize, 0)

    def project(start, size):
        lin[:, pl.ds(start, size)] = jnp.dot(
            normed_out[...], attn_full[:, pl.ds(start, size)], preferred_element_type=f32
        )

    in_columns(3 * HD, project)
    move(1)

    def turn_keyval(first, size, carry):
        at = pl.ds(first, size)
        values = lin[at, 2 * HD : 3 * HD]
        keys = turned(values * scale_of(values) * head_rows[5:6], cosine[at], sine[at])
        mine = jnp.where(core == 0, keys, values).astype(bf16)
        keyval[core, pl.ds(pl.multiple_of(first + behind, 64), size)] = mine
        return carry

    in_rows(row_count, turn_keyval, 0)
    own_rows, last_rows = pl.ds(behind, row_count), pl.ds(row_count, behind)
    past_rows = pl.ds(0, behind)

    def to_core(came=False):
        block = keyval.at[1 - core if came else core, own_rows]
        return remote(block, block, keyval_send.at[0], keyval_recv.at[0], core_dev)

    def past_to_core(came=False):
        block = keyval.at[1 - core if came else core, past_rows]
        return remote(block, block, keyval_send.at[2], keyval_recv.at[2], core_dev)

    to_next = remote(
        keyval.at[core, last_rows],
        keyval.at[core, past_rows],
        keyval_send.at[1],
        keyval_recv.at[1],
        next_dev,
    )
    pl.when(ctx < 3)(to_next.start)
    to_core().start()

    def turn_query(first, size, carry):
        at = pl.ds(first, size)
        for head in range(2):
            values = lin[at, head * HD : (head + 1) * HD]
            normal = values * scale_of(values) * head_rows[4:5]
            query_out[head, at] = turned(normal, cosine[at], sine[at]).astype(bf16)
        return carry

    in_rows(row_count, turn_query, 0)

    @pl.when(ctx > 0)
    def _():
        to_next.wait_recv()
        past_to_core().start()
        past_to_core(True).wait_recv()

    @pl.when(ctx == 0)
    def _():
        keyval[:, 0:behind] = jnp.zeros((2, behind, HD), bf16)

    to_core(True).wait_recv()
    move(2)

    block_rows = 256
    reach = block_rows + behind

    def attend(first, head):
        at = pl.ds(first, block_rows)
        near = pl.ds(first, reach)
        scores = contract_columns(query_out[head, at], keyval[0, near]) * HD ** (-0.5)
        key_at = first + lax.broadcasted_iota(jnp.int32, (block_rows, reach), 1)
        query_at = first + behind + lax.broadcasted_iota(jnp.int32, (block_rows, reach), 0)
        scores = jnp.where((key_at >= lowest[at]) & (key_at <= query_at), scores, -1e30)
        row_max = jnp.max(scores, axis=1, keepdims=True)
        values = jnp.exp(scores - row_max)
        row_total = jnp.sum(values, axis=1, keepdims=True)
        probs = (values / row_total).astype(bf16)
        log_total[head, at] = row_max + jnp.log(row_total)
        out = jnp.dot(probs, keyval[1, near], preferred_element_type=f32)
        attended[at, head * HD : (head + 1) * HD] = out.astype(bf16)

    for block in range(row_count // block_rows):
        for head in range(2):
            attend(block * block_rows, head)
        move(1)

    def outward(start, size):
        partial[:, pl.ds(start, size)] = contract_columns(
            attended[...], attn_full[pl.ds(start, size), 3 * HD : 5 * HD]
        )

    in_columns(width, outward)

    def give_half(first, size, carry):
        at = pl.ds(pl.multiple_of((1 - core) * half + first, 64), size)
        core_send[pl.ds(first, size)] = partial[at].astype(bf16)
        return carry

    in_rows(half, give_half, 0)
    exchange = remote(core_send, core_take, keyval_send.at[3], keyval_recv.at[3], core_dev)
    exchange.start()
    exchange.wait_recv()

    def finish(first, size, carry):
        at = pl.ds(first, size)
        whole_at = pl.ds(pl.multiple_of(core * half + first, 64), size)
        branch = partial[whole_at] + core_take[at].astype(f32)
        branch_out[at] = branch
        middle = tokens[whole_at].astype(f32) + branch * scale_of(branch) * gain_rows[1:2]
        middle_out[at] = middle
        normed_two[at] = (middle * scale_of(middle) * gain_rows[2:3]).astype(bf16)
        return carry

    in_rows(half, finish, 0)
    keyval_out[...] = keyval[...]
    move(len(events))

    exchange.wait_send()
    to_core().wait_send()
    pl.when(ctx < 3)(to_next.wait_send)
    pl.when(ctx > 0)(past_to_core().wait_send)
    for k in (1, 2, 3):
        mlp_plane(k).wait_send()
    for step in range(n_dp - 1):
        each(step, lambda way: attn_hop(way, step).wait_send(), True)
        for k in range(4):
            each(step, lambda way: mlp_hop(way, step, k).wait_send(), True)

    def left(way, step):
        for side in (1, 2, 3):
            attn_plane(way, step, side).wait_send()

    for way, step in order:
        where_held(way, step, left)


def attend_call(n_dp, owned_heads, behind, tokens, cosine, sine, lowest, attn_pack, mlp_pack):
    row_count, width = tokens.shape
    half = row_count // 2
    owned, attn_cols = attn_pack.shape
    blocks = n_dp * 4
    f32, bf16 = jnp.float32, jnp.bfloat16
    vmem = pl.BlockSpec(memory_space=pltpu.VMEM)
    anywhere = pl.BlockSpec(memory_space=pl.ANY)

    def array(dtype, *shape):
        return jax.ShapeDtypeStruct(shape, dtype)

    dma = pltpu.SemaphoreType.DMA
    return pl.pallas_call(
        functools.partial(attend_kernel, n_dp, owned_heads),
        out_shape=(
            array(bf16, blocks, owned, mlp_pack.shape[2]),
            array(bf16, width, attn_cols),
            array(f32, 8, width),
            array(f32, 8, HD),
            array(bf16, row_count, width),
            array(f32, row_count, 3 * HD),
            array(bf16, 2, row_count, HD),
            array(bf16, 2, behind + row_count, HD),
            array(bf16, row_count, 2 * HD),
            array(f32, 2, row_count, 1),
            array(f32, half, width),
            array(f32, half, width),
            array(bf16, half, width),
        ),
        in_specs=[vmem] * 4 + [anywhere] * 2,
        out_specs=(anywhere,) + (vmem,) * 12,
        scratch_shapes=[
            pltpu.VMEM((blocks, owned, attn_cols), bf16),
            pltpu.VMEM((width, attn_cols), f32),
            pltpu.VMEM((2, behind + row_count, HD), bf16),
            pltpu.VMEM((row_count, width), f32),
            pltpu.VMEM((half, width), bf16),
            pltpu.VMEM((half, width), bf16),
            dma((2,)),
            dma((4,)),
            dma((4,)),
            dma((8 * n_dp,)),
            dma((8 * n_dp,)),
            dma((2 * n_dp,)),
            dma((2 * n_dp,)),
            dma((8 * n_dp,)),
            dma((8 * n_dp,)),
            dma((4,)),
            dma((4,)),
        ],
        compiler_params=pltpu.CompilerParams(
            collective_id=1, has_side_effects=True, vmem_limit_bytes=60 * 2**20
        ),
        cost_estimate=pl.CostEstimate(
            flops=4 * 10**9, bytes_accessed=30 * 2**20, transcendentals=2 * 10**6
        ),
        name="attend",
    )(tokens, cosine, sine, lowest, attn_pack, mlp_pack)


def mlp_kernel(
    normed,
    middle,
    cotangent,
    gain,
    weights,
    result,
    back_sum,
    gain_sum,
    rows_out,
    grads_out,
    hidden_out,
    gate_out,
    rows,
    grads,
    hidden,
    pair,
    total,
    waiting,
    core_send,
    core_take,
    plane_send,
    plane_take,
    send_sem,
    recv_sem,
    out_sem,
):
    half = normed.shape[0]
    h = half // 2
    width = normed.shape[1]
    hid = hidden.shape[2]
    step_rows = 2 * half
    part_a, part_b = pl.ds(0, h), pl.ds(h, h)
    x_dev, y_dev, _, core_dev = plane_partners()
    f32, bf16 = jnp.float32, jnp.bfloat16

    enter(1, False)

    def remote(source, target, index, device):
        return pltpu.make_async_remote_copy(
            src_ref=source,
            dst_ref=target,
            send_sem=send_sem.at[index],
            recv_sem=recv_sem.at[index],
            device_id=device,
            device_id_type=MESH,
        )

    def gather_copies(buffer, base):
        def piece(step, side):
            return buffer.at[step, 0, side]

        return [
            remote(piece(0, part_a), piece(1, part_a), base, x_dev),
            remote(piece(0, part_b), piece(1, part_b), base + 1, y_dev),
            remote(piece(0, part_b), piece(2, part_b), base + 2, x_dev),
            remote(piece(0, part_a), piece(2, part_a), base + 3, y_dev),
            remote(piece(1, part_a), piece(3, part_a), base + 4, y_dev),
            remote(piece(1, part_b), piece(3, part_b), base + 5, x_dev),
        ] + [
            remote(buffer.at[step, 0], buffer.at[step, 1], base + 6 + step, core_dev)
            for step in range(4)
        ]

    def scatter_copies(base):
        return [
            remote(plane_send.at[0, part_a], plane_take.at[0, part_a], base, y_dev),
            remote(plane_send.at[0, part_b], plane_take.at[0, part_b], base + 1, x_dev),
            remote(plane_send.at[1, part_a], plane_take.at[1, part_a], base + 2, y_dev),
            remote(plane_send.at[1, part_b], plane_take.at[1, part_b], base + 3, x_dev),
            remote(plane_send.at[2, part_a], plane_take.at[2, part_a], base + 4, x_dev),
            remote(plane_send.at[2, part_b], plane_take.at[2, part_b], base + 5, y_dev),
        ] + [
            remote(core_send.at[step % 2], core_take.at[step], base + 6 + step, core_dev)
            for step in range(4)
        ]

    def out_copy(buffer, target, step, index):
        return pltpu.make_async_copy(
            buffer.at[step],
            target.at[step],
            out_sem.at[index * 4 + step],
        )

    def gather_step(copies, step):
        if step == 0:
            for copy in copies[:4]:
                copy.start()
        elif step == 1:
            copies[0].wait_recv()
            copies[1].wait_recv()
            copies[4].start()
            copies[5].start()
        else:
            copies[2 * step - 2].wait_recv()
            copies[2 * step - 1].wait_recv()
        copies[6 + step].start()
        copies[6 + step].wait_recv()

    def scatter_step(copies, step, left, first):
        kept = (total, waiting, back_sum, back_sum)[step]
        slot = core_send.at[step % 2]
        if step >= 2:
            copies[6 + step - 2].wait_send()

        def body(start, size):
            product = contract_columns(
                left[step], weights[pl.ds(start, size), first : first + left.shape[2]]
            )
            kept[:, pl.ds(start, size)] = product[:half]
            slot[:, pl.ds(start, size)] = product[half:].astype(bf16)

        in_columns(width, body)
        copies[6 + step].start()
        copies[6 + step].wait_recv()
        summed = kept[...] + core_take[step].astype(f32)
        if step < 2:
            kept[...] = summed
        else:
            plane_send[step - 2] = summed.astype(bf16)
            copies[2 * step - 4].start()
            copies[2 * step - 3].start()

    def scatter_end(copies):
        copies[2].wait_recv()
        copies[3].wait_recv()
        plane_send[2] = (waiting[...] + plane_take[1].astype(f32)).astype(bf16)
        copies[4].start()
        copies[5].start()

    def scatter_total(at):
        return total[at] + plane_take[0, at].astype(f32) + plane_take[2, at].astype(f32)

    def scatter_wait(copies):
        for index in (0, 1, 4, 5):
            copies[index].wait_recv()

    def sent(copies):
        for copy in copies:
            copy.wait_send()

    rows[0, 0] = normed[...]
    gather = gather_copies(rows, 0)
    scatter = scatter_copies(10)
    for step in range(4):
        gather_step(gather, step)
        out_copy(rows, rows_out, step, 0).start()

        def activate(j, carry):
            at = pl.multiple_of(j * 256, 256)
            lin = jnp.dot(
                rows[step].reshape(step_rows, width),
                weights[:, pl.ds(at, 256)],
                preferred_element_type=f32,
            )
            gate, up = lin[:, :128], lin[:, 128:]
            square = gate * gate
            curve = jnp.tanh(GELU_SCALE * gate * (1.0 + 0.044715 * square))
            gelu = 0.5 * gate * (1.0 + curve)
            slope = 0.5 * (1.0 + curve) + 0.5 * GELU_SCALE * gate * (1.0 - curve * curve) * (
                1.0 + 3 * 0.044715 * square
            )
            at_half = pl.multiple_of(j * 128, 128)
            hidden[step, :, pl.ds(at_half, 128)] = (gelu * up).astype(bf16)
            pair[step, :, pl.ds(at, 128)] = (slope * up).astype(bf16)
            pair[step, :, pl.ds(pl.multiple_of(at + 128, 128), 128)] = gelu.astype(bf16)
            return carry

        lax.fori_loop(0, hid // 128, activate, 0)
        out_copy(hidden, hidden_out, step, 1).start()
        scatter_step(scatter, step, hidden, 2 * hid)
    scatter_end(scatter)
    sent(gather)
    scatter_wait(scatter)
    sent(scatter[:6] + scatter[8:])

    def norm_rows(first, size, gain_total):
        at = pl.ds(first, size)
        raw = scatter_total(at)
        scale = lax.rsqrt(jnp.mean(raw * raw, axis=1, keepdims=True) + norm_eps)
        normal = raw * scale
        result[at] = (middle[at] + normal * gain[...]).astype(bf16)
        cotangents = cotangent[at].astype(f32)
        scaled = cotangents * gain[...]
        inner = jnp.mean(raw * scaled, axis=1, keepdims=True)
        back = scale * scaled - raw * (scale * scale * scale * inner)
        grads[0, 0, at] = back.astype(bf16)
        return gain_total + jnp.sum(cotangents * normal, axis=0, keepdims=True)

    gain_sum[...] = in_rows(half, norm_rows, jnp.zeros((1, width), f32))

    gather = gather_copies(grads, 20)
    scatter = scatter_copies(30)
    for step in range(4):
        gather_step(gather, step)
        out_copy(grads, grads_out, step, 2).start()

        def unfold(start, size):
            hidden_grad = jnp.dot(
                grads[step].reshape(step_rows, width),
                weights[:, pl.ds(pl.multiple_of(2 * hid + start, 128), size)],
                preferred_element_type=f32,
            )
            for tile in range(size // 128):
                piece = hidden_grad[:, tile * 128 : (tile + 1) * 128]
                for side in range(2):
                    at = pl.ds(pl.multiple_of(2 * start + (2 * tile + side) * 128, 128), 128)
                    pair[step, :, at] = (pair[step, :, at].astype(f32) * piece).astype(bf16)

        in_columns(hid, unfold)
        out_copy(pair, gate_out, step, 3).start()
        scatter_step(scatter, step, pair, 0)
    scatter_end(scatter)
    sent(gather)
    scatter_wait(scatter)

    def finish_rows(first, size, carry):
        at = pl.ds(first, size)
        back_sum[at] = scatter_total(at)
        return carry

    in_rows(half, finish_rows, 0)
    sent(scatter[:6] + scatter[8:])
    for step in range(4):
        for index, (buffer, target) in enumerate(
            ((rows, rows_out), (hidden, hidden_out), (grads, grads_out), (pair, gate_out))
        ):
            out_copy(buffer, target, step, index).wait()


def mlp_call(normed, middle, cotangent, gain, weights):
    half, width = normed.shape
    hid = weights.shape[1] // 3
    count = 8 * half
    f32, bf16 = jnp.float32, jnp.bfloat16
    vmem = pl.BlockSpec(memory_space=pltpu.VMEM)
    anywhere = pl.BlockSpec(memory_space=pl.ANY)
    outs = pl.pallas_call(
        mlp_kernel,
        out_shape=(
            jax.ShapeDtypeStruct((half, width), bf16),
            jax.ShapeDtypeStruct((half, width), f32),
            jax.ShapeDtypeStruct((1, width), f32),
            jax.ShapeDtypeStruct((4, 2, half, width), bf16),
            jax.ShapeDtypeStruct((4, 2, half, width), bf16),
            jax.ShapeDtypeStruct((4, 2 * half, hid), bf16),
            jax.ShapeDtypeStruct((4, 2 * half, 2 * hid), bf16),
        ),
        in_specs=[vmem] * 5,
        out_specs=(vmem, vmem, vmem, anywhere, anywhere, anywhere, anywhere),
        scratch_shapes=[
            pltpu.VMEM((4, 2, half, width), bf16),
            pltpu.VMEM((4, 2, half, width), bf16),
            pltpu.VMEM((4, 2 * half, hid), bf16),
            pltpu.VMEM((4, 2 * half, 2 * hid), bf16),
            pltpu.VMEM((half, width), f32),
            pltpu.VMEM((half, width), f32),
            pltpu.VMEM((2, half, width), bf16),
            pltpu.VMEM((4, half, width), bf16),
            pltpu.VMEM((3, half, width), bf16),
            pltpu.VMEM((3, half, width), bf16),
            pltpu.SemaphoreType.DMA((40,)),
            pltpu.SemaphoreType.DMA((40,)),
            pltpu.SemaphoreType.DMA((16,)),
        ],
        compiler_params=pltpu.CompilerParams(
            collective_id=0, has_side_effects=True, vmem_limit_bytes=62 * 2**20
        ),
        cost_estimate=pl.CostEstimate(
            flops=2 * count * width * hid * 6, bytes_accessed=60 * 2**20, transcendentals=count * hid
        ),
        name="feed_forward",
    )(normed, middle, cotangent, gain, weights)
    return outs[:3] + tuple(array.reshape(count, array.shape[-1]) for array in outs[3:])


def on_device(
    tokens,
    out_cotangent,
    lengths,
    norm_gains,
    gain_first,
    gain_second,
    head_gains,
    head_first,
    head_second,
    query_weight,
    query_first,
    query_second,
    keyval_weight,
    keyval_first,
    keyval_second,
    output_weight,
    output_first,
    output_second,
    gate_up,
    gate_first,
    gate_second,
    down_weight,
    down_first,
    down_second,
):
    bf16, f32 = jnp.bfloat16, jnp.float32
    row_count = tokens.shape[0]
    owned = query_weight.shape[0]
    owned_heads = head_gains.shape[0]
    n_dp, n_ctx = lax.axis_size("dp"), lax.axis_size("ctx")
    half_ff = gate_up.shape[2]
    wide = -(-half_ff // (n_ctx * 128)) * 128
    behind = WIN
    ctx_place = lax.axis_index("ctx")
    core_first = lax.axis_index("tensor") == 0
    score_scale = HD ** (-0.5)

    head_columns = jnp.pad(head_gains, ((0, owned - owned_heads), (0, 0)))
    small = jnp.concatenate([norm_gains, head_columns], axis=1).astype(bf16)
    attn_pack = jnp.concatenate(
        [
            query_weight.astype(bf16),
            half_of(keyval_weight, 1).astype(bf16),
            output_weight.astype(bf16),
            jnp.pad(small, ((0, 0), (0, 122))),
        ],
        axis=1,
    )
    cols = query_weight.shape[1]

    def in_parts(array):
        padded = jnp.pad(array.astype(bf16), ((0, 0), (0, n_ctx * wide - half_ff)))
        return padded.reshape(owned, n_ctx, wide // 128, 128)

    gate_parts = jnp.stack([in_parts(gate_up[:, side]) for side in range(2)], axis=3)
    mlp_pack = jnp.concatenate(
        [
            gate_parts.reshape(owned, n_ctx, 2 * wide),
            in_parts(down_weight).reshape(owned, n_ctx, wide),
        ],
        axis=2,
    )
    mlp_pack = jnp.moveaxis(mlp_pack, 1, 0)

    start_row = ctx_place * row_count
    row_index = jnp.arange(row_count, dtype=jnp.int32)
    query_position = token_layout(lengths[0], start_row + row_index)[1]
    query_cosine, query_sine = rope_tables(query_position)
    lowest = jnp.maximum(row_index - query_position + behind, row_index + 1)[:, None]
    (
        mlp_full,
        attn_full,
        gain_rows,
        head_rows,
        normed_one,
        lin,
        query_rot,
        keyval_all,
        attended_low,
        log_total,
        branch_raw,
        middle,
        normed_two_half,
    ) = attend_call(
        n_dp, owned_heads, behind, tokens, query_cosine, query_sine, lowest, attn_pack, mlp_pack
    )
    key_count = behind + row_count
    head_count = cols // HD
    full_query = attn_full[:, :cols]
    half_keyval = attn_full[:, cols : cols + HD]
    full_output = attn_full[:, cols + HD : 2 * cols + HD]
    query_norm_back = jax.vjp(
        rms_norm, lin[:, :cols].reshape(row_count, head_count, HD), head_rows[4]
    )[1]
    key_norm_back = jax.vjp(rms_norm, lin[:, cols:], head_rows[5])[1]
    key_all, value_all = keyval_all[0], keyval_all[1]
    post_one_back = jax.vjp(rms_norm, branch_raw, gain_rows[1])[1]
    norm_two_back = jax.vjp(rms_norm, middle, gain_rows[2])[1]
    inputs_half = half_of(tokens, 0).astype(f32)
    key_index = jnp.arange(key_count, dtype=jnp.int32)[None, :]
    allowed = (key_index >= lowest) & (key_index <= row_index[:, None] + behind)

    def core_summed(partial):
        arrived = from_partner(half_not_of(partial, 0).astype(bf16), "tensor", 1)
        return half_of(partial, 0) + arrived.astype(f32)

    cotangent_half = half_of(out_cotangent, 0)
    (
        result_half,
        normed_two_grad,
        gain_three_part,
        normed_two,
        mlp_raw_low,
        hidden_low,
        gate_grad,
    ) = mlp_call(
        normed_two_half,
        middle,
        cotangent_half,
        gain_rows[3:4],
        mlp_full.reshape(n_dp * n_ctx * owned, 3 * wide),
    )
    gain_three_grad = gain_three_part[0]
    cotangent_half = cotangent_half.astype(f32)
    result = core_ordered(result_half, from_partner(result_half, "tensor", 1))
    def exchanged(tiles):
        return lax.all_to_all(tiles, ("dp", "ctx"), split_axis=0, concat_axis=0, tiled=True)

    def to_owners(term):
        arrived = exchanged(term.astype(bf16).reshape(n_dp * n_ctx, owned, term.shape[1]))
        return arrived.reshape(n_dp, n_ctx, owned, term.shape[1]).astype(f32).sum(axis=0)

    def from_parts(tiles):
        return jnp.moveaxis(tiles, 0, 1).reshape(owned, n_ctx * wide)[:, :half_ff]

    down_reduced = from_parts(to_owners(contract_rows(mlp_raw_low, hidden_low)))
    gate_arrived = to_owners(contract_rows(normed_two, gate_grad))
    gate_arrived = gate_arrived.reshape(n_ctx, owned, wide // 128, 2, 128)
    gate_reduced = jnp.stack(
        [from_parts(gate_arrived[:, :, :, side].reshape(n_ctx, owned, wide)) for side in range(2)],
        axis=1,
    )

    middle_part, gain_two_grad = norm_two_back(normed_two_grad)
    middle_grad = cotangent_half + middle_part
    branch_pre_grad, gain_one_grad = post_one_back(middle_grad)
    branch_half = branch_pre_grad.astype(bf16)
    branch_low = core_ordered(branch_half, from_partner(branch_half, "tensor", 1))
    output_w_grad = contract_rows(branch_low, attended_low)
    attended_grad = (
        jnp.dot(branch_low, full_output, preferred_element_type=f32)
        .astype(bf16)
        .reshape(row_count, head_count, HD)
    )
    scores_again = (
        jnp.einsum("hqd,kd->hqk", query_rot, key_all, preferred_element_type=f32) * score_scale
    )
    prob_again = jnp.exp(jnp.where(allowed[None], scores_again, -1e30) - log_total)
    probs_grad = jnp.einsum("qhd,kd->hqk", attended_grad, value_all, preferred_element_type=f32)
    value_grad_all = jnp.einsum(
        "hqk,qhd->kd", prob_again.astype(bf16), attended_grad, preferred_element_type=f32
    )
    row_delta = jnp.sum(prob_again * probs_grad, axis=-1, keepdims=True)
    score_grad = (prob_again * (probs_grad - row_delta)).astype(bf16)
    query_rot_grad = (
        jnp.einsum("hqk,kd->qhd", score_grad, key_all, preferred_element_type=f32) * score_scale
    )
    key_grad_all = (
        jnp.einsum("hqk,hqd->kd", score_grad, query_rot, preferred_element_type=f32) * score_scale
    )
    grad_mine = jnp.where(core_first, key_grad_all, value_grad_all)
    grad_other = jnp.where(core_first, value_grad_all, key_grad_all)
    grad_mine = grad_mine + from_partner(grad_other.astype(bf16), "tensor", 1).astype(f32)
    returned = from_behind(grad_mine[:behind].astype(bf16), "ctx", -1).astype(f32)
    own_grad = grad_mine[behind:].at[row_count - behind :].add(returned)
    query_normed_grad = rotate(query_rot_grad, query_cosine[:, None, :], -query_sine[:, None, :])
    query_pre_grad, head_zero_part = query_norm_back(query_normed_grad)
    query_lin_grad = query_pre_grad.reshape(row_count, head_count * HD).astype(bf16)
    key_pre_grad, head_one_part = key_norm_back(rotate(own_grad, query_cosine, -query_sine))
    keyval_lin_grad = jnp.where(core_first, key_pre_grad, own_grad).astype(bf16)
    head_one_part = jnp.where(core_first, head_one_part, 0.0)
    normed_one_grad = core_summed(
        contract_columns(query_lin_grad, full_query) + contract_columns(keyval_lin_grad, half_keyval)
    )
    query_w_grad = contract_rows(normed_one, query_lin_grad)
    keyval_w_grad = contract_rows(normed_one, keyval_lin_grad)
    norm_one_back = jax.vjp(rms_norm, inputs_half, gain_rows[0])[1]
    input_part, gain_zero_grad = norm_one_back(normed_one_grad)
    input_half = middle_grad + input_part
    input_grad = core_ordered(input_half, from_partner(input_half, "tensor", 1))

    gains_part = jnp.stack([gain_zero_grad, gain_one_grad, gain_two_grad, gain_three_grad], axis=1)
    heads_part = jnp.stack([head_zero_part, head_one_part], axis=1)
    heads_part = jnp.pad(
        heads_part.reshape(-1, owned_heads, 2), ((0, 0), (0, owned - owned_heads), (0, 0))
    ).reshape(-1, 2)
    small_part = jnp.concatenate([gains_part, heads_part], axis=1)
    small_grad = small_part + from_partner(small_part, "tensor", 1)
    attn_grad = jnp.concatenate(
        [query_w_grad, keyval_w_grad, output_w_grad, jnp.pad(small_grad, ((0, 0), (0, 122)))], axis=1
    ).astype(bf16)
    attn_grad = jnp.moveaxis(attn_grad.reshape(n_dp, n_ctx, owned, -1), 1, 0)
    attn_arrived = along_line(attn_grad, "ctx").astype(f32).sum(axis=0).astype(bf16)
    attn_sum = along_line(attn_arrived, "dp").astype(f32).sum(axis=0)
    query_reduced = attn_sum[:, :cols]
    keyval_half = attn_sum[:, cols : cols + HD]
    output_reduced = attn_sum[:, cols + HD : 2 * cols + HD]
    keyval_not = from_partner(keyval_half, "tensor", 1)
    keyval_reduced = jnp.concatenate(
        [
            jnp.where(core_first, keyval_half, keyval_not),
            jnp.where(core_first, keyval_not, keyval_half),
        ],
        axis=1,
    )
    gains_reduced = attn_sum[:, 2 * cols + HD : 2 * cols + HD + 4]
    heads_reduced = attn_sum[:owned_heads, 2 * cols + HD + 4 : 2 * cols + HD + 6]

    gains_new, gain_first_new, gain_second_new = adam_step(
        norm_gains, gains_reduced, gain_first, gain_second, 0.5, 0.0
    )
    heads_new, head_first_new, head_second_new = adam_step(
        head_gains, heads_reduced, head_first, head_second, 0.5, 0.0
    )
    query_new, query_first_new, query_second_new = adam_step(
        query_weight, query_reduced, query_first, query_second, D ** (-0.5), decay_rate
    )
    keyval_new, keyval_first_new, keyval_second_new = adam_step(
        keyval_weight, keyval_reduced, keyval_first, keyval_second, D ** (-0.5), decay_rate
    )
    output_new, output_first_new, output_second_new = adam_step(
        output_weight, output_reduced, output_first, output_second, (HQ * HD) ** (-0.5), decay_rate
    )
    gate_new, gate_first_new, gate_second_new = adam_step(
        gate_up, gate_reduced, gate_first, gate_second, D ** (-0.5), decay_rate
    )
    down_new, down_first_new, down_second_new = adam_step(
        down_weight, down_reduced, down_first, down_second, FF ** (-0.5), decay_rate
    )
    return (
        result,
        input_grad,
        gains_new,
        gain_first_new,
        gain_second_new,
        heads_new,
        head_first_new,
        head_second_new,
        query_new,
        query_first_new,
        query_second_new,
        keyval_new,
        keyval_first_new,
        keyval_second_new,
        output_new,
        output_first_new,
        output_second_new,
        gate_new,
        gate_first_new,
        gate_second_new,
        down_new,
        down_first_new,
        down_second_new,
    )


def solution(mesh):
    placed = (
        P(("dp", "ctx"), None),
        P(("dp", "ctx"), None),
        P("dp", None),
        P(("dp", "ctx"), None),
        P(("dp", "ctx"), None),
        P(("dp", "ctx"), None),
        P(("dp", "ctx"), None),
        P(("dp", "ctx"), None),
        P(("dp", "ctx"), None),
        P(("dp", "ctx"), "tensor"),
        P(("dp", "ctx"), "tensor"),
        P(("dp", "ctx"), "tensor"),
        P(("dp", "ctx"), None),
        P(("dp", "ctx"), None),
        P(("dp", "ctx"), None),
        P(("dp", "ctx"), "tensor"),
        P(("dp", "ctx"), "tensor"),
        P(("dp", "ctx"), "tensor"),
        P(("dp", "ctx"), None, "tensor"),
        P(("dp", "ctx"), None, "tensor"),
        P(("dp", "ctx"), None, "tensor"),
        P(("dp", "ctx"), "tensor"),
        P(("dp", "ctx"), "tensor"),
        P(("dp", "ctx"), "tensor"),
    )
    return jax.shard_map(
        on_device,
        mesh=mesh,
        in_specs=placed,
        out_specs=(
            P(("dp", "ctx"), None),
            P(("dp", "ctx"), None),
            P(("dp", "ctx"), None),
            P(("dp", "ctx"), None),
            P(("dp", "ctx"), None),
            P(("dp", "ctx"), None),
            P(("dp", "ctx"), None),
            P(("dp", "ctx"), None),
            P(("dp", "ctx"), "tensor"),
            P(("dp", "ctx"), "tensor"),
            P(("dp", "ctx"), "tensor"),
            P(("dp", "ctx"), None),
            P(("dp", "ctx"), None),
            P(("dp", "ctx"), None),
            P(("dp", "ctx"), "tensor"),
            P(("dp", "ctx"), "tensor"),
            P(("dp", "ctx"), "tensor"),
            P(("dp", "ctx"), None, "tensor"),
            P(("dp", "ctx"), None, "tensor"),
            P(("dp", "ctx"), None, "tensor"),
            P(("dp", "ctx"), "tensor"),
            P(("dp", "ctx"), "tensor"),
            P(("dp", "ctx"), "tensor"),
        ),
        check_vma=False,
    )
```

time: 1850 us -> 626 us (0.34)
  waiting for transfers between devices: 1380 us -> 81.9 us
  Pallas kernels: 0 us -> 298 us
  matrix products: 168 us -> 54.5 us
  other arithmetic: 137 us -> 70.8 us
  blocking collectives: 66.1 us -> 0 us
  local copies, waits for them, and re-layouts: 35.1 us -> 64.7 us
    all_gather x10 -> x0, waiting for transfers between devices: 659 us -> none  [the longest x1 180 us: on_device(): lax.all_gather(gate_low, ('dp', 'ctx'), axis=0, tiled=True)]
    reduce_scatter x1 -> x0, waiting for transfers between devices: 549 us -> none  [on_device(): lax.psum_scatter(jnp.concatenate([gate_term, down_term[:, None, :]], axis...]
    pallas_call x0 -> x2, Pallas kernels: none -> 298 us  [the longest x1 155 us: mlp_call(): pl.pallas_call(mlp_kernel, out_shape=(jax.ShapeDtypeStruct((half, width),...]
    all_to_all x5 -> x2, waiting for transfers between devices: 110 us -> 0.01 us  [exchanged(): lax.all_to_all(tiles, ('dp', 'ctx'), split_axis=0, concat_axis=0, tiled=T...]
    dot_general x12 -> x5, matrix products: 112 us -> 13.7 us  [the longest x1 3.69 us: on_device(): jnp.einsum('hqk,kd->qhd', score_grad, key_all, preferred_element_type=f32)]
    ppermute x0 -> x13, waiting for transfers between devices: none -> 76.8 us  [the longest x6 76.8 us: along_line(): lax.ppermute(tile, axis, [(i, (i + shift) % n) for i in range(n)])]
    psum x4 -> x0, waiting for transfers between devices: 57 us -> none  [the longest x1 21.8 us: on_device(): lax.psum(contract_columns(hidden_low, full_down).astype(jnp.bfloat16), 't...]
    all_gather x2 -> x0, blocking collectives: 55.9 us -> none  [the longest x1 28.4 us: on_device(): lax.all_gather(gains_low, ('dp', 'ctx'), axis=0, tiled=True)]
  transfers between devices with their start and end apart: 22 -> 16, of which waited for: 18 -> 5; matrix products, arithmetic and copies ran while one was open for 15% -> 21% of each run, Pallas kernels for 0% -> 0%
where the time goes in v1:
time: 626 us; the launch traced here: 615 us
  Pallas kernels  298 us (48%)
  waiting for transfers between devices  81.9 us (13%)
  other arithmetic  70.8 us (11%)
  local copies, waits for them, and re-layouts  64.7 us (10%)
  matrix products  54.5 us (9%)
  starting transfers between devices  43.2 us (7%)
    pallas_call x1, Pallas kernels, mlp_call(): pl.pallas_call(mlp_kernel, out_shape=(jax.ShapeDtypeStruct((half, width),...  155 us
    pallas_call x1, Pallas kernels, attend_call(): pl.pallas_call(functools.partial(attend_kernel, n_dp, owned_heads), out_s...  143 us
    ppermute x6, waiting for transfers between devices, along_line(): lax.ppermute(tile, axis, [(i, (i + shift) % n) for i in range(n)])  76.8 us
    dot_general x5, matrix products, contract_rows(): lax.dot_general(left_side, right_side, (((0,), (0,)), ((), ())), preferre...  37.6 us
    unnamed x137, local copies, waits for them, and re-layouts  22.8 us
    ppermute x6, starting transfers between devices, along_line(): lax.ppermute(tile, axis, [(i, (i + shift) % n) for i in range(n)])  19.7 us
    all_to_all x2, starting transfers between devices, exchanged(): lax.all_to_all(tiles, ('dp', 'ctx'), split_axis=0, concat_axis=0, tiled=T...  13.2 us
  transfers between devices with their start and end apart: 16, of which 5 were waited for; matrix products, arithmetic and copies ran while one was open for 21% of the time, Pallas kernels for 0%

profile of v1, /device:TPU:9, one launch (start us, length us, event | category | flops | bytes accessed | tf_op | source)
XLA Modules:
  0.0 614.5 jit_solution(483609706897660863)
XLA Ops:
  12.3 2.6 fusion.45
  17.7 143.1 %attend.1 = (bf16[16,72,2688]{2,1,0:T(8,128)(2,1)}, bf16[1152,1408]{1,0:T(8,128)(2,1)}, f32[8,1152]{1,0:T(8,128)}, f32[8,256]{1,0:T(8,128)}, bf16[768,1152]{1,0:...) custom-call(bf16[768,1152]{1,0:T(8,128)(2,1)} %tokens.1, ...), custom_call_target="tpu_custom_call" | custom-call | flops 4000000000 | bytes 31457280 | tf_op jit(solution)/shard_map/attend/pallas_call | solution.py:543
  165.0 154.6 %feed_forward.1 = (bf16[384,1152]{1,0:T(8,128)(2,1)}, f32[384,1152]{1,0:T(8,128)}, f32[1,1152]{1,0:T(1,128)}, bf16[4,2,384,1152]{3,2,1,0:T(8,128)(2,1)}, bf16[4,...) custom-call(bf16[384,1152]{1,0:T(8,128)(2,1)} %get-tuple-element.55.normed, ...), custom_call_target="tpu_custom_call" | custom-call | flops 38050725888 | bytes 62914560 | tf_op jit(solution)/shard_map/feed_forward/pallas_call | solution.py:828
  319.7 2.7 multiply_reduce_fusion
  325.7 2.6 collective-permute-start.1
  328.3 10.7 %convolution_convert_fusion.1 = bf16[1152,896]{1,0:T(8,128)(2,1)} fusion(bf16[3072,1152]{1,0:T(8,128)(2,1)S(1)} %bitcast.167, bf16[3072,896]{1,0:T(8,128)(2,1)} %bitcast.169), kind=kOutput, calls=%fused_computation.15 | convolution fusion | flops 6342819840 | bytes 14647296 | tf_op jit(solution)/shard_map/dot_general | solution.py:102
  339.0 6.8 %all-to-all-start.1 = ((bf16[16,72,896]{2,1,0:T(8,128)(2,1)}), bf16[16,72,896]{2,1,0:T(8,128)(2,1)}, u32[]{:S(2)}, u32[]{:S(2)}) async-start(bf16[16,72,896]{2,1,0:T(8,128)(2,1)} %bitcast.148), calls=%async_computation.1 | async-start | bytes 4128768 | tf_op jit(solution)/shard_map/all_to_all | solution.py:994
  350.2 2.3 reshape.432
  361.0 19.6 %convolution_convert_fusion = bf16[1152,1792]{1,0:T(8,128)(2,1)} fusion(bf16[3072,1152]{1,0:T(8,128)(2,1)} %bitcast.166, bf16[3072,1792]{1,0:T(8,128)(2,1)} %bitcast.165), kind=kOutput, calls=%fused_computation.7 | convolution fusion | flops 12685639680 | bytes 22216704 | tf_op jit(solution)/shard_map/dot_general | solution.py:102
  385.8 3.2 convolution_convert_fusion.5
  390.4 3.1 fusion
  393.5 6.4 %fusion.2 = bf16[2,768,1280]{2,1,0:T(8,128)(2,1)} fusion(f32[2,768,1280]{2,1,0:T(8,128)S(1)} %get-tuple-element.356, f32[1280,768,2]{0,1,2:T(8,128)} %copy-done, f32[2,768]{1,0:T(2,128)S(1)} %get-tuple-element.355), kind=kLoop, calls=%fused_computation.5 | loop fusion | flops 5898240 | bytes 19666944 | tf_op jit(solution)/shard_map/convert_element_type | solution.py:1031
  399.9 3.7 multiply_bitcast_fusion
  404.9 2.6 select_convert_fusion
  420.8 3.5 multiply_reduce_fusion.6
  424.4 5.1 collective-permute-done.3
  446.5 2.7 fusion.18
  451.9 6.4 %all-to-all-start = ((bf16[16,72,1792]{2,1,0:T(8,128)(2,1)}), bf16[16,72,1792]{2,1,0:T(8,128)(2,1)}, u32[]{:S(2)}, u32[]{:S(2)}) async-start(bf16[16,72,1792]{2,1,0:T(8,128)(2,1)} %bitcast.139), calls=%async_computation | async-start | bytes 8257536 | tf_op jit(solution)/shard_map/all_to_all | solution.py:994
  458.2 3.0 convolution_convert_fusion.4
  473.8 17.8 %collective-permute-done.7 = bf16[4,72,1408]{2,1,0:T(8,128)(2,1)S(1)} collective-permute-done((bf16[4,72,1408]{2,1,0:T(8,128)(2,1)S(1)}, bf16[4,72,1408]{2,1,0:T(8,128)(2,1)S(1)}, u32[]{:S(2)}, u32[]{:S(2)}) %collective-permute-start.7) | collective-permute-done | bytes 811040 | tf_op jit(solution)/shard_map/ppermute | solution.py:47
  491.6 42.0 %collective-permute-done.8 = bf16[4,72,1408]{2,1,0:T(8,128)(2,1)S(1)} collective-permute-done((bf16[4,72,1408]{2,1,0:T(8,128)(2,1)S(1)}, bf16[4,72,1408]{2,1,0:T(8,128)(2,1)S(1)}, u32[]{:S(2)}, u32[]{:S(2)}) %collective-permute-start.8) | collective-permute-done | bytes 811040 | tf_op jit(solution)/shard_map/ppermute | solution.py:47
  534.0 14.9 %collective-permute-start.10 = (bf16[72,1408]{1,0:T(8,128)(2,1)S(1)}, bf16[72,1408]{1,0:T(8,128)(2,1)S(1)}, u32[]{:S(2)}, u32[]{:S(2)}) collective-permute-start(bf16[72,1408]{1,0:T(8,128)(2,1)S(1)} %get-tuple-element.337), channel_id=1, source_target_pairs={{0,8},{8,16},{16,24},{24,0},{1,9},{9,17},{17,25},{25,1},{2,10},{10... | collective-permute-start | bytes 608264 | tf_op jit(solution)/shard_map/ppermute | solution.py:47
  550.2 2.9 fusion.14
  554.8 12.6 %collective-permute-done.10 = bf16[72,1408]{1,0:T(8,128)(2,1)S(1)} collective-permute-done((bf16[72,1408]{1,0:T(8,128)(2,1)S(1)}, bf16[72,1408]{1,0:T(8,128)(2,1)S(1)}, u32[]{:S(2)}, u32[]{:S(2)}) %collective-permute-start.10) | collective-permute-done | bytes 202784 | tf_op jit(solution)/shard_map/ppermute | solution.py:47
  567.3 4.3 collective-permute-done.11
  574.5 2.3 multiply_subtract_fusion.4
  587.7 3.0 convert_reduce_fusion
  590.7 2.3 reshape.437
  593.0 8.1 %slice_reduce_fusion.1 = (f32[4,72,7,128]{3,2,1,0:T(8,128)S(1)}, f32[4,72,7,128]{3,2,1,0:T(8,128)S(1)}) fusion(f32[4,72,7,2,128]{4,3,2,1,0:T(2,128)} %reshape.437), kind=kLoop, calls=%fused_computation.74 | loop fusion | bytes 4128768 | tf_op jit(solution)/shard_map/slice | solution.py:1007
  607.4 2.3 copy.480
  609.7 2.3 copy.481
  612.0 2.3 copy.482
  (272 shorter events, 111.0 us)
Async XLA Ops:
  0.7 11.6 %copy-start.52 = (f32[128]{0:T(128)}, f32[128]{0:T(128)S(1)}, u32[]{:S(2)}) copy-start(f32[128]{0:T(128)S(1)} %negate_power_fusion) | copy-start | bytes 1540
  165.0 154.6 %copy-start.1 = (f32[384,1152]{1,0:T(8,128)S(1)}, f32[384,1152]{1,0:T(8,128)}, u32[]{:S(2)}) copy-start(f32[384,1152]{1,0:T(8,128)} %get-tuple-element.64) | copy-start | bytes 5308420
  325.7 58.4 %collective-permute-start.1 = (bf16[384,1152]{1,0:T(8,128)(2,1)}, bf16[384,1152]{1,0:T(8,128)(2,1)}, u32[]{:S(2)}, u32[]{:S(2)}) collective-permute-start(bf16[384,1152]{1,0:T(8,128)(2,1)} %fusion.13), channel_id=1, source_target_pairs={{1,0},{0,1},{3,2},{2,3},{5,4},{4,5},{7,6},{6,7},{9,8},{8,9},{11,10... | collective-permute-start | bytes 2654216 | tf_op jit(solution)/shard_map/ppermute | solution.py:36
  339.0 8.9 %copy-start.27 = (f32[768,128]{1,0:T(8,128)S(1)}, f32[768,128]{1,0:T(8,128)}, u32[]{:S(2)}) copy-start(f32[768,128]{1,0:T(8,128)} %get-tuple-element.352.cosine) | copy-start | bytes 1179652
  339.0 9.8 %copy-start.5 = (f32[768,768]{1,0:T(8,128)S(1)}, f32[768,768]{1,0:T(8,128)}, u32[]{:S(2)}) copy-start(f32[768,768]{1,0:T(8,128)} %get-tuple-element.67) | copy-start | bytes 7077892
  339.0 112.8 %all-to-all-start.1 = ((bf16[16,72,896]{2,1,0:T(8,128)(2,1)}), bf16[16,72,896]{2,1,0:T(8,128)(2,1)}, u32[]{:S(2)}, u32[]{:S(2)}) async-start(bf16[16,72,896]{2,1,0:T(8,128)(2,1)} %bitcast.148), calls=%async_computation.1 | async-start | bytes 4128768 | tf_op jit(solution)/shard_map/all_to_all | solution.py:994
  345.9 125.2 %collective-permute-start = (bf16[384,1152]{1,0:T(8,128)(2,1)}, bf16[384,1152]{1,0:T(8,128)(2,1)}, u32[]{:S(2)}, u32[]{:S(2)}) collective-permute-start(bf16[384,1152]{1,0:T(8,128)(2,1)} %get-tuple-element.59), channel_id=1, source_target_pairs={{1,0},{0,1},{3,2},{2,3},{5,4},{4,5},{7,6},{6,7},{9,8},{8,9},{11,10... | collective-permute-start | bytes 2654216 | tf_op jit(solution)/shard_map/ppermute | solution.py:36
  356.5 24.1 %copy-start.45 = (f32[384]{0:T(512)}, f32[384]{0:T(512)S(1)}, u32[]{:S(2)}) copy-start(f32[384]{0:T(512)S(1)} %fusion.15) | copy-start | bytes 4612
  361.0 19.6 %copy-start.39 = (f32[2,768,1]{2,1,0:T(8,128)S(1)}, f32[2,768,1]{2,1,0:T(8,128)}, u32[]{:S(2)}) copy-start(f32[2,768,1]{2,1,0:T(8,128)} %get-tuple-element.63) | copy-start | bytes 18436
  407.5 8.4 %collective-permute-start.2 = (bf16[1280,256]{1,0:T(8,128)(2,1)}, bf16[1280,256]{1,0:T(8,128)(2,1)S(1)}, u32[]{:S(2)}, u32[]{:S(2)}) collective-permute-start(bf16[1280,256]{1,0:T(8,128)(2,1)} %get-tuple-element.357), channel_id=1, source_target_pairs={{1,0},{0,1},{3,2},{2,3},{5,4},{4,5},{7,6},{6,7},{9,8},{8,9},{11,10... | collective-permute-start | bytes 1966088 | tf_op jit(solution)/shard_map/ppermute | solution.py:36
  419.5 10.0 %collective-permute-start.3 = (bf16[512,256]{1,0:T(8,128)(2,1)}, bf16[512,256]{1,0:T(8,128)(2,1)S(1)}, u32[]{:S(2)}, u32[]{:S(2)}) collective-permute-start(bf16[512,256]{1,0:T(8,128)(2,1)} %slice.220), channel_id=1, source_target_pairs={{2,0},{4,2},{6,4},{3,1},{5,3},{7,5},{10,8},{12,10},{14,12},{11,9},... | collective-permute-start | bytes 786440 | tf_op jit(solution)/shard_map/ppermute | solution.py:32
  420.8 8.7 %slice-start = ((f32[1280,256]{1,0:T(8,128)}), f32[768,256]{1,0:T(8,128)S(1)}, s32[]{:S(2)}) async-start(f32[1280,256]{1,0:T(8,128)} %copy-done.9), calls=%async_computation.2 | async-start | bytes 1572864 | tf_op jit(solution)/shard_map/slice | solution.py:1042
  424.4 6.9 %copy-start.49 = (f32[1,256]{1,0:T(1,128)S(1)}, f32[1,256]{1,0:T(1,128)}, u32[]{:S(2)}) copy-start(f32[1,256]{1,0:T(1,128)} %get-tuple-element.347) | copy-start | bytes 3076
  436.8 9.7 %collective-permute-start.4 = (bf16[384,1152]{1,0:T(8,128)(2,1)}, bf16[384,1152]{1,0:T(8,128)(2,1)}, u32[]{:S(2)}, u32[]{:S(2)}) collective-permute-start(bf16[384,1152]{1,0:T(8,128)(2,1)} %dynamic-slice_convert_fusion), channel_id=1, source_target_pairs={{1,0},{0,1},{3,2},{2,3},{5,4},{4,5},{7,6},{6,7},{9,8},{8,9},{11,10... | collective-permute-start | bytes 2654216 | tf_op jit(solution)/shard_map/ppermute | solution.py:36
  451.2 10.1 %collective-permute-start.6 = (f32[1152,6]{0,1:T(8,128)}, f32[1152,6]{0,1:T(8,128)}, u32[]{:S(2)}, u32[]{:S(2)}) collective-permute-start(f32[1152,6]{0,1:T(8,128)} %concatenate.61), channel_id=1, source_target_pairs={{1,0},{0,1},{3,2},{2,3},{5,4},{4,5},{7,6},{6,7},{9,8},{8,9},{11,10... | collective-permute-start | bytes 82952 | tf_op jit(solution)/shard_map/ppermute | solution.py:36
  451.9 135.9 %all-to-all-start = ((bf16[16,72,1792]{2,1,0:T(8,128)(2,1)}), bf16[16,72,1792]{2,1,0:T(8,128)(2,1)}, u32[]{:S(2)}, u32[]{:S(2)}) async-start(bf16[16,72,1792]{2,1,0:T(8,128)(2,1)} %bitcast.139), calls=%async_computation | async-start | bytes 8257536 | tf_op jit(solution)/shard_map/all_to_all | solution.py:994
  467.5 24.1 %collective-permute-start.7 = (bf16[4,72,1408]{2,1,0:T(8,128)(2,1)S(1)}, bf16[4,72,1408]{2,1,0:T(8,128)(2,1)S(1)}, u32[]{:S(2)}, u32[]{:S(2)}) collective-permute-start(bf16[4,72,1408]{2,1,0:T(8,128)(2,1)S(1)} %get-tuple-element.321), channel_id=1, source_target_pairs={{0,2},{2,4},{4,6},{6,0},{1,3},{3,5},{5,7},{7,1},{8,10},{10,12},{12... | collective-permute-start | bytes 2433032 | tf_op jit(solution)/shard_map/ppermute | solution.py:47
  468.7 64.9 %collective-permute-start.8 = (bf16[4,72,1408]{2,1,0:T(8,128)(2,1)S(1)}, bf16[4,72,1408]{2,1,0:T(8,128)(2,1)S(1)}, u32[]{:S(2)}, u32[]{:S(2)}) collective-permute-start(bf16[4,72,1408]{2,1,0:T(8,128)(2,1)S(1)} %get-tuple-element.323), channel_id=1, source_target_pairs={{0,4},{2,6},{4,0},{6,2},{1,5},{3,7},{5,1},{7,3},{8,12},{10,14},{12... | collective-permute-start | bytes 2433032 | tf_op jit(solution)/shard_map/ppermute | solution.py:47
  470.0 63.7 %collective-permute-start.9 = (bf16[4,72,1408]{2,1,0:T(8,128)(2,1)S(1)}, bf16[4,72,1408]{2,1,0:T(8,128)(2,1)S(1)}, u32[]{:S(2)}, u32[]{:S(2)}) collective-permute-start(bf16[4,72,1408]{2,1,0:T(8,128)(2,1)S(1)} %get-tuple-element.322), channel_id=1, source_target_pairs={{0,6},{2,0},{4,2},{6,4},{1,7},{3,1},{5,3},{7,5},{8,14},{10,8},{12,... | collective-permute-start | bytes 2433032 | tf_op jit(solution)/shard_map/ppermute | solution.py:47
  473.8 76.3 %copy-start.48 = (f32[384]{0:T(512)S(1)}, f32[384]{0:T(512)}, u32[]{:S(2)}) copy-start(f32[384]{0:T(512)} %fusion.53) | copy-start | bytes 4612
  533.7 16.5 %copy-start.3 = (f32[384,1152]{1,0:T(8,128)S(1)}, f32[384,1152]{1,0:T(8,128)}, u32[]{:S(2)}) copy-start(f32[384,1152]{1,0:T(8,128)} %copy-done.2) | copy-start | bytes 5308420
  533.7 16.5 %copy-start.18 = (bf16[768,1152]{1,0:T(8,128)(2,1)S(1)}, bf16[768,1152]{1,0:T(8,128)(2,1)}, u32[]{:S(2)}) copy-start(bf16[768,1152]{1,0:T(8,128)(2,1)} %tokens.1) | copy-start | bytes 5308420
  534.0 33.4 %collective-permute-start.10 = (bf16[72,1408]{1,0:T(8,128)(2,1)S(1)}, bf16[72,1408]{1,0:T(8,128)(2,1)S(1)}, u32[]{:S(2)}, u32[]{:S(2)}) collective-permute-start(bf16[72,1408]{1,0:T(8,128)(2,1)S(1)} %get-tuple-element.337), channel_id=1, source_target_pairs={{0,8},{8,16},{16,24},{24,0},{1,9},{9,17},{17,25},{25,1},{2,10},{10... | collective-permute-start | bytes 608264 | tf_op jit(solution)/shard_map/ppermute | solution.py:47
  548.9 22.8 %collective-permute-start.11 = (bf16[72,1408]{1,0:T(8,128)(2,1)S(1)}, bf16[72,1408]{1,0:T(8,128)(2,1)S(1)}, u32[]{:S(2)}, u32[]{:S(2)}) collective-permute-start(bf16[72,1408]{1,0:T(8,128)(2,1)S(1)} %get-tuple-element.336), channel_id=1, source_target_pairs={{0,16},{8,24},{16,0},{24,8},{1,17},{9,25},{17,1},{25,9},{2,18},{10... | collective-permute-start | bytes 608264 | tf_op jit(solution)/shard_map/ppermute | solution.py:47
  548.9 24.3 %copy-start.51 = (f32[72,4]{0,1:T(4,128)S(1)}, f32[72,4]{0,1:T(4,128)}, u32[]{:S(2)}) copy-start(f32[72,4]{0,1:T(4,128)} %param.29) | copy-start | bytes 3460
  548.9 24.3 %copy-start.54 = (f32[72,4]{0,1:T(4,128)S(1)}, f32[72,4]{0,1:T(4,128)}, u32[]{:S(2)}) copy-start(f32[72,4]{0,1:T(4,128)} %param.30) | copy-start | bytes 3460
  548.9 22.8 %collective-permute-start.12 = (bf16[72,1408]{1,0:T(8,128)(2,1)S(1)}, bf16[72,1408]{1,0:T(8,128)(2,1)S(1)}, u32[]{:S(2)}, u32[]{:S(2)}) collective-permute-start(bf16[72,1408]{1,0:T(8,128)(2,1)S(1)} %get-tuple-element.335), channel_id=1, source_target_pairs={{0,24},{8,0},{16,8},{24,16},{1,25},{9,1},{17,9},{25,17},{2,26},{10... | collective-permute-start | bytes 608264 | tf_op jit(solution)/shard_map/ppermute | solution.py:47
  553.1 30.9 %collective-permute-start.5 = (f32[384,1152]{1,0:T(8,128)}, f32[384,1152]{1,0:T(8,128)S(1)}, u32[]{:S(2)}, u32[]{:S(2)}) collective-permute-start(f32[384,1152]{1,0:T(8,128)} %fusion.14), channel_id=1, source_target_pairs={{1,0},{0,1},{3,2},{2,3},{5,4},{4,5},{7,6},{6,7},{9,8},{8,9},{11,10... | collective-permute-start | bytes 5308424 | tf_op jit(solution)/shard_map/ppermute | solution.py:36
  571.7 5.7 copy-start.41
  571.7 5.7 copy-start.42
  571.7 5.7 copy-start.43
  572.0 5.5 collective-permute-start.13
  (48 other events, 130.9 us)

commit v2 on v1

--- a/solution.py
+++ b/solution.py
@@ -26,26 +26,8 @@
 MESH = pl.DeviceIdType.MESH
 
 
-def from_behind(block, axis, distance):
-    devices = range(lax.axis_size(axis))
-    route = [(i - distance, i) for i in devices if i - distance in devices]
-    return lax.ppermute(block, axis, route)
-
-
 def from_partner(block, axis, bits):
     return lax.ppermute(block, axis, [(i ^ bits, i) for i in range(lax.axis_size(axis))])
-
-
-def along_line(tiles, axis):
-    n = lax.axis_size(axis)
-    if n > 4:
-        return lax.all_to_all(tiles, axis, split_axis=0, concat_axis=0, tiled=True)
-    place = lax.axis_index(axis)
-    arrived = [lax.dynamic_index_in_dim(tiles, place, 0, keepdims=False)]
-    for shift in range(1, n):
-        tile = lax.dynamic_index_in_dim(tiles, lax.rem(place + shift, n), 0, keepdims=False)
-        arrived.append(lax.ppermute(tile, axis, [(i, (i + shift) % n) for i in range(n)]))
-    return jnp.stack(arrived)
 
 
 def core_ordered(own, other):
@@ -56,11 +38,6 @@
 def half_of(array, dim):
     size = array.shape[dim] // 2
     return lax.dynamic_slice_in_dim(array, lax.axis_index("tensor") * size, size, axis=dim)
-
-
-def half_not_of(array, dim):
-    size = array.shape[dim] // 2
-    return lax.dynamic_slice_in_dim(array, (1 - lax.axis_index("tensor")) * size, size, axis=dim)
 
 
 def token_layout(lengths, places):
@@ -78,24 +55,6 @@
     inverse = jnp.power(jnp.float32(rope_base), -exponent)
     angles = position.astype(jnp.float32)[:, None] * inverse[None, :]
     return (jnp.cos(angles), jnp.sin(angles))
-
-
-def rotate(values, cosine_table, sine_table):
-    half_dim = values.shape[-1] // 2
-    lower_part = values[..., :half_dim]
-    upper_part = values[..., half_dim:]
-    return jnp.concatenate(
-        [
-            lower_part * cosine_table - upper_part * sine_table,
-            upper_part * cosine_table + lower_part * sine_table,
-        ],
-        axis=-1,
-    )
-
-
-def rms_norm(values, gain_row):
-    scale = lax.rsqrt(jnp.mean(values * values, axis=-1, keepdims=True) + norm_eps)
-    return values * scale * gain_row
 
 
 def contract_rows(left_side, right_side):
@@ -169,6 +128,43 @@
         return body(pl.multiple_of(i * size, size), size, carry)
 
     return lax.fori_loop(0, count // size, one, start)
+
+
+def gather_copies(remote, buffer, base):
+    x_dev, y_dev, _, core_dev = plane_partners()
+    h = buffer.shape[2] // 2
+    part_a, part_b = pl.ds(0, h), pl.ds(h, h)
+
+    def piece(step, side):
+        return buffer.at[step, 0, side]
+
+    return [
+        remote(piece(0, part_a), piece(1, part_a), base, x_dev),
+        remote(piece(0, part_b), piece(1, part_b), base + 1, y_dev),
+        remote(piece(0, part_b), piece(2, part_b), base + 2, x_dev),
+        remote(piece(0, part_a), piece(2, part_a), base + 3, y_dev),
+        remote(piece(1, part_a), piece(3, part_a), base + 4, y_dev),
+        remote(piece(1, part_b), piece(3, part_b), base + 5, x_dev),
+    ] + [
+        remote(buffer.at[step, 0], buffer.at[step, 1], base + 6 + step, core_dev)
+        for step in range(4)
+    ]
+
+
+def gather_step(copies, step):
+    if step == 0:
+        for copy in copies[:4]:
+            copy.start()
+    elif step == 1:
+        copies[0].wait_recv()
+        copies[1].wait_recv()
+        copies[4].start()
+        copies[5].start()
+    else:
+        copies[2 * step - 2].wait_recv()
+        copies[2 * step - 1].wait_recv()
+    copies[6 + step].start()
+    copies[6 + step].wait_recv()
 
 
 def turned(values, cosine, sine):
@@ -202,7 +198,7 @@
     log_total,
     branch_out,
     middle_out,
-    normed_two,
+    rows_out,
     slots,
     wide_slots,
     keyval,
@@ -220,6 +216,10 @@
     attn_plane_recv,
     keyval_send,
     keyval_recv,
+    rows,
+    rows_send,
+    rows_recv,
+    rows_sem,
 ):
     dp, ctx, core = places()
     x_dev, y_dev, far_dev, core_dev = plane_partners()
@@ -306,7 +306,7 @@
             plane[k],
         )
 
-    for k in (1, 2, 3):
+    for k in (1, 2):
         mlp_plane(k).start()
 
     def came(way, step):
@@ -316,10 +316,6 @@
         for side in (1, 2):
             attn_plane(way, step, side).start()
 
-    for step in range(1, n_dp):
-        each(step, lambda way: came(way, step), False)
-        each(step, lambda way: attn_hop(way, step).start(), True)
-        each(step, lambda way: hand_on(way, step), False)
     order = [(0, 0)] + [(way, step) for step in range(1, n_dp) for way in range(2)]
 
     def relay(way, step):
@@ -336,9 +332,6 @@
         else:
             act(way, step)
 
-    for way, step in order:
-        where_held(way, step, relay)
-
     def mlp_first(k):
         mlp_plane(k, True).wait_recv()
         each(0, lambda way: mlp_hop(way, 0, k).start(), True)
@@ -357,10 +350,23 @@
         for _ in range(min(count, len(events))):
             events.pop()()
 
-    move(2)
+    for step in range(1, n_dp):
+        each(step, lambda way: came(way, step), False)
+        each(step, lambda way: attn_hop(way, step).start(), True)
+        each(step, lambda way: hand_on(way, step), False)
+        if step == 1:
+            mlp_plane(3).start()
+        if step <= 3:
+            move(1)
+    if n_dp == 1:
+        mlp_plane(3).start()
+    move(max(0, 4 - n_dp) + 2)
+    for way, step in order:
+        where_held(way, step, relay)
+    move(1)
     for way, step in order:
         where_held(way, step, relayed)
-    move(2)
+    move(1)
 
     for block in range(n_dp * 4):
         wide_slots[block * owned : (block + 1) * owned, :] = slots[block].astype(f32)
@@ -501,12 +507,30 @@
         branch_out[at] = branch
         middle = tokens[whole_at].astype(f32) + branch * scale_of(branch) * gain_rows[1:2]
         middle_out[at] = middle
-        normed_two[at] = (middle * scale_of(middle) * gain_rows[2:3]).astype(bf16)
+        rows[0, 0, at] = (middle * scale_of(middle) * gain_rows[2:3]).astype(bf16)
         return carry
 
     in_rows(half, finish, 0)
-    keyval_out[...] = keyval[...]
+
+    def remote_rows(source, target, index, device):
+        return remote(source, target, rows_send.at[index], rows_recv.at[index], device)
+
+    gather = gather_copies(remote_rows, rows, 0)
+    outs = [
+        pltpu.make_async_copy(rows.at[step], rows_out.at[step], rows_sem.at[step])
+        for step in range(4)
+    ]
+    for step in range(4):
+        gather_step(gather, step)
+        outs[step].start()
+        if step == 0:
+            keyval_out[...] = keyval[...]
+        move(1)
     move(len(events))
+    for copy in gather:
+        copy.wait_send()
+    for copy in outs:
+        copy.wait()
 
     exchange.wait_send()
     to_core().wait_send()
@@ -555,10 +579,10 @@
             array(f32, 2, row_count, 1),
             array(f32, half, width),
             array(f32, half, width),
-            array(bf16, half, width),
+            array(bf16, 4, 2, half, width),
         ),
         in_specs=[vmem] * 4 + [anywhere] * 2,
-        out_specs=(anywhere,) + (vmem,) * 12,
+        out_specs=(anywhere,) + (vmem,) * 11 + (anywhere,),
         scratch_shapes=[
             pltpu.VMEM((blocks, owned, attn_cols), bf16),
             pltpu.VMEM((width, attn_cols), f32),
@@ -577,6 +601,10 @@
             dma((8 * n_dp,)),
             dma((4,)),
             dma((4,)),
+            pltpu.VMEM((4, 2, half, width), bf16),
+            dma((10,)),
+            dma((10,)),
+            dma((4,)),
         ],
         compiler_params=pltpu.CompilerParams(
             collective_id=1, has_side_effects=True, vmem_limit_bytes=60 * 2**20
@@ -589,22 +617,20 @@
 
 
 def mlp_kernel(
-    normed,
+    rows_in,
     middle,
     cotangent,
     gain,
-    weights,
+    weights_in,
     result,
     back_sum,
     gain_sum,
-    rows_out,
-    grads_out,
-    hidden_out,
-    gate_out,
+    weights_out,
     rows,
     grads,
     hidden,
     pair,
+    weights,
     total,
     waiting,
     core_send,
@@ -613,17 +639,23 @@
     plane_take,
     send_sem,
     recv_sem,
+    load_sem,
     out_sem,
 ):
-    half = normed.shape[0]
+    half, width = middle.shape
     h = half // 2
-    width = normed.shape[1]
     hid = hidden.shape[2]
     step_rows = 2 * half
     part_a, part_b = pl.ds(0, h), pl.ds(h, h)
     x_dev, y_dev, _, core_dev = plane_partners()
     f32, bf16 = jnp.float32, jnp.bfloat16
 
+    loads = [pltpu.make_async_copy(weights_in, weights, load_sem.at[4])] + [
+        pltpu.make_async_copy(rows_in.at[step], rows.at[step], load_sem.at[step])
+        for step in range(4)
+    ]
+    for load in (loads[0], loads[4], loads[3], loads[2], loads[1]):
+        load.start()
     enter(1, False)
 
     def remote(source, target, index, device):
@@ -635,22 +667,6 @@
             device_id=device,
             device_id_type=MESH,
         )
-
-    def gather_copies(buffer, base):
-        def piece(step, side):
-            return buffer.at[step, 0, side]
-
-        return [
-            remote(piece(0, part_a), piece(1, part_a), base, x_dev),
-            remote(piece(0, part_b), piece(1, part_b), base + 1, y_dev),
-            remote(piece(0, part_b), piece(2, part_b), base + 2, x_dev),
-            remote(piece(0, part_a), piece(2, part_a), base + 3, y_dev),
-            remote(piece(1, part_a), piece(3, part_a), base + 4, y_dev),
-            remote(piece(1, part_b), piece(3, part_b), base + 5, x_dev),
-        ] + [
-            remote(buffer.at[step, 0], buffer.at[step, 1], base + 6 + step, core_dev)
-            for step in range(4)
-        ]
 
     def scatter_copies(base):
         return [
@@ -665,33 +681,11 @@
             for step in range(4)
         ]
 
-    def out_copy(buffer, target, step, index):
-        return pltpu.make_async_copy(
-            buffer.at[step],
-            target.at[step],
-            out_sem.at[index * 4 + step],
-        )
-
-    def gather_step(copies, step):
-        if step == 0:
-            for copy in copies[:4]:
-                copy.start()
-        elif step == 1:
-            copies[0].wait_recv()
-            copies[1].wait_recv()
-            copies[4].start()
-            copies[5].start()
-        else:
-            copies[2 * step - 2].wait_recv()
-            copies[2 * step - 1].wait_recv()
-        copies[6 + step].start()
-        copies[6 + step].wait_recv()
-
-    def scatter_step(copies, step, left, first):
+    def scatter_step(copies, step, before, left, first):
         kept = (total, waiting, back_sum, back_sum)[step]
         slot = core_send.at[step % 2]
-        if step >= 2:
-            copies[6 + step - 2].wait_send()
+        if before is not None:
+            copies[6 + before].wait_send()
 
         def body(start, size):
             product = contract_columns(
@@ -729,12 +723,10 @@
         for copy in copies:
             copy.wait_send()
 
-    rows[0, 0] = normed[...]
-    gather = gather_copies(rows, 0)
-    scatter = scatter_copies(10)
-    for step in range(4):
-        gather_step(gather, step)
-        out_copy(rows, rows_out, step, 0).start()
+    scatter = scatter_copies(0)
+    loads[0].wait()
+    for step in (3, 2, 1, 0):
+        loads[1 + step].wait()
 
         def activate(j, carry):
             at = pl.multiple_of(j * 256, 256)
@@ -757,12 +749,11 @@
             return carry
 
         lax.fori_loop(0, hid // 128, activate, 0)
-        out_copy(hidden, hidden_out, step, 1).start()
-        scatter_step(scatter, step, hidden, 2 * hid)
-    scatter_end(scatter)
-    sent(gather)
+        scatter_step(scatter, step, step + 2 if step < 2 else None, hidden, 2 * hid)
+        if step == 1:
+            scatter_end(scatter)
     scatter_wait(scatter)
-    sent(scatter[:6] + scatter[8:])
+    sent(scatter[:8])
 
     def norm_rows(first, size, gain_total):
         at = pl.ds(first, size)
@@ -779,11 +770,10 @@
 
     gain_sum[...] = in_rows(half, norm_rows, jnp.zeros((1, width), f32))
 
-    gather = gather_copies(grads, 20)
-    scatter = scatter_copies(30)
+    gather = gather_copies(remote, grads, 10)
+    scatter = scatter_copies(20)
     for step in range(4):
         gather_step(gather, step)
-        out_copy(grads, grads_out, step, 2).start()
 
         def unfold(start, size):
             hidden_grad = jnp.dot(
@@ -798,10 +788,28 @@
                     pair[step, :, at] = (pair[step, :, at].astype(f32) * piece).astype(bf16)
 
         in_columns(hid, unfold)
-        out_copy(pair, gate_out, step, 3).start()
-        scatter_step(scatter, step, pair, 0)
+        scatter_step(scatter, step, step - 2 if step >= 2 else None, pair, 0)
+    sent(gather)
+
+    def weigh(first, right):
+        def one(i, carry):
+            at = pl.ds(pl.multiple_of(i * 384, 128), 384)
+            left = (rows if right is pair else grads)[:, :, :, at].reshape(8 * half, 384)
+            product = contract_rows(left, right[...].reshape(8 * half, right.shape[2]))
+            weights[at, first : first + right.shape[2]] = product.astype(bf16)
+            return carry
+
+        lax.fori_loop(0, width // 384, one, 0)
+        columns = pl.ds(first, right.shape[2])
+        copy = pltpu.make_async_copy(
+            weights.at[:, columns], weights_out.at[:, columns], out_sem.at[first // (2 * hid)]
+        )
+        copy.start()
+        return copy
+
+    down_out = weigh(2 * hid, hidden)
     scatter_end(scatter)
-    sent(gather)
+    gate_out = weigh(0, pair)
     scatter_wait(scatter)
 
     def finish_rows(first, size, carry):
@@ -811,57 +819,629 @@
 
     in_rows(half, finish_rows, 0)
     sent(scatter[:6] + scatter[8:])
-    for step in range(4):
-        for index, (buffer, target) in enumerate(
-            ((rows, rows_out), (hidden, hidden_out), (grads, grads_out), (pair, gate_out))
-        ):
-            out_copy(buffer, target, step, index).wait()
-
-
-def mlp_call(normed, middle, cotangent, gain, weights):
-    half, width = normed.shape
+    down_out.wait()
+    gate_out.wait()
+
+
+def mlp_call(rows, middle, cotangent, gain, weights):
+    half, width = middle.shape
     hid = weights.shape[1] // 3
     count = 8 * half
     f32, bf16 = jnp.float32, jnp.bfloat16
     vmem = pl.BlockSpec(memory_space=pltpu.VMEM)
     anywhere = pl.BlockSpec(memory_space=pl.ANY)
-    outs = pl.pallas_call(
+    return pl.pallas_call(
         mlp_kernel,
         out_shape=(
             jax.ShapeDtypeStruct((half, width), bf16),
             jax.ShapeDtypeStruct((half, width), f32),
             jax.ShapeDtypeStruct((1, width), f32),
-            jax.ShapeDtypeStruct((4, 2, half, width), bf16),
-            jax.ShapeDtypeStruct((4, 2, half, width), bf16),
-            jax.ShapeDtypeStruct((4, 2 * half, hid), bf16),
-            jax.ShapeDtypeStruct((4, 2 * half, 2 * hid), bf16),
+            jax.ShapeDtypeStruct((width, 3 * hid), bf16),
         ),
-        in_specs=[vmem] * 5,
-        out_specs=(vmem, vmem, vmem, anywhere, anywhere, anywhere, anywhere),
+        in_specs=[anywhere, vmem, vmem, vmem, anywhere],
+        out_specs=(vmem, vmem, vmem, anywhere),
         scratch_shapes=[
             pltpu.VMEM((4, 2, half, width), bf16),
             pltpu.VMEM((4, 2, half, width), bf16),
             pltpu.VMEM((4, 2 * half, hid), bf16),
             pltpu.VMEM((4, 2 * half, 2 * hid), bf16),
+            pltpu.VMEM((width, 3 * hid), bf16),
             pltpu.VMEM((half, width), f32),
             pltpu.VMEM((half, width), f32),
             pltpu.VMEM((2, half, width), bf16),
             pltpu.VMEM((4, half, width), bf16),
             pltpu.VMEM((3, half, width), bf16),
             pltpu.VMEM((3, half, width), bf16),
-            pltpu.SemaphoreType.DMA((40,)),
-            pltpu.SemaphoreType.DMA((40,)),
-            pltpu.SemaphoreType.DMA((16,)),
+            pltpu.SemaphoreType.DMA((30,)),
+            pltpu.SemaphoreType.DMA((30,)),
+            pltpu.SemaphoreType.DMA((5,)),
+            pltpu.SemaphoreType.DMA((2,)),
         ],
         compiler_params=pltpu.CompilerParams(
-            collective_id=0, has_side_effects=True, vmem_limit_bytes=62 * 2**20
+            collective_id=0, has_side_effects=True, vmem_limit_bytes=63 * 2**20
         ),
         cost_estimate=pl.CostEstimate(
-            flops=2 * count * width * hid * 6, bytes_accessed=60 * 2**20, transcendentals=count * hid
+            flops=2 * count * width * hid * 9, bytes_accessed=30 * 2**20, transcendentals=count * hid
         ),
         name="feed_forward",
-    )(normed, middle, cotangent, gain, weights)
-    return outs[:3] + tuple(array.reshape(count, array.shape[-1]) for array in outs[3:])
+    )(rows, middle, cotangent, gain, weights)
+
+
+def norm_back(values, gains, grads):
+    scale = scale_of(values)
+    normal = values * scale
+    scaled = grads * gains
+    inner = jnp.mean(values * scaled, axis=1, keepdims=True)
+    return scale * scaled - values * (scale * scale * scale * inner), grads * normal
+
+
+def retreat_kernel(
+    n_dp,
+    line,
+    owned_heads,
+    back_sum,
+    middle,
+    branch,
+    cotangent_in,
+    tokens_in,
+    cosine,
+    sine,
+    lowest,
+    gain_rows,
+    head_rows,
+    gain_three,
+    attn_full_in,
+    normed_one_in,
+    lin_in,
+    query_in,
+    keyval_in,
+    attended_in,
+    log_total,
+    mlp_grads,
+    input_out,
+    mlp_reduced,
+    attn_reduced,
+    line_slots,
+    attn_grads,
+    attn_blocks,
+    attn_plane_take,
+    attn_sums,
+    attn_slots,
+    branch_low,
+    attended_grad,
+    query_grad,
+    lin_grad,
+    keyval_grad,
+    keyval_send,
+    keyval_take,
+    past_take,
+    partial,
+    core_send,
+    core_take,
+    small_rows,
+    small_take,
+    line_send_sem,
+    line_recv_sem,
+    plane_send_sem,
+    plane_recv_sem,
+    attn_plane_send_sem,
+    attn_plane_recv_sem,
+    attn_line_send_sem,
+    attn_line_recv_sem,
+    core_send_sem,
+    core_recv_sem,
+    load_sem,
+    mlp_own,
+    cotangent,
+    tokens,
+    attn_full,
+    normed_one,
+    lin,
+    query,
+    keyval,
+    attended,
+):
+    dp, ctx, core = places()
+    x_dev, y_dev, far_dev, core_dev = plane_partners()
+    plane = ((dp, ctx, core), x_dev, y_dev, far_dev)
+    f32, bf16 = jnp.float32, jnp.bfloat16
+    row_count, width = tokens.shape
+    half = row_count // 2
+    owned, hid = mlp_grads.shape[1], mlp_grads.shape[2] // 3
+    behind = keyval.shape[1] - row_count
+    last_dp = line - 1
+    here_dp = dp if line > 1 else 0
+    sources = (
+        (cotangent_in, cotangent),
+        (attn_full_in, attn_full),
+        (query_in, query),
+        (keyval_in, keyval),
+        (mlp_grads, mlp_own),
+        (lin_in, lin),
+        (attended_in, attended),
+        (normed_one_in, normed_one),
+        (tokens_in, tokens),
+    )
+    held = [
+        pltpu.make_async_copy(source, target, load_sem.at[3 + index])
+        for index, (source, target) in enumerate(sources)
+    ]
+    loads = [
+        pltpu.make_async_copy(
+            source,
+            attn_grads.at[pl.ds(index * half, half), pl.ds(0, width)],
+            load_sem.at[index],
+        )
+        for index, source in enumerate((middle, branch, back_sum))
+    ]
+    for load in loads + held:
+        load.start()
+    enter(n_dp, line > 1)
+
+    def remote(source, target, send, recv, device):
+        return pltpu.make_async_remote_copy(
+            src_ref=source,
+            dst_ref=target,
+            send_sem=send,
+            recv_sem=recv,
+            device_id=device,
+            device_id_type=MESH,
+        )
+
+    def goal(way, far):
+        return dp + far if way == 0 else dp - far
+
+    def has_goal(way, far):
+        return dp + far <= last_dp if way == 0 else dp >= far
+
+    def is_first(way):
+        return dp == 0 if way == 0 else dp == last_dp
+
+    def not_first(way):
+        return dp > 0 if way == 0 else dp < last_dp
+
+    def line_dev(way):
+        return (dp + 1, ctx, core) if way == 0 else (dp - 1, ctx, core)
+
+    def slot_of(way, far, k):
+        return (way * last_dp + far - 1) * 4 + k
+
+    def own_mlp(place, k):
+        return mlp_own[place * 4 + plane[k][1]].astype(f32)
+
+    def first_hop(way, far, k):
+        slot = slot_of(way, far, k)
+        return remote(
+            mlp_grads.at[goal(way, far) * 4 + plane[k][1]],
+            line_slots.at[slot],
+            line_send_sem.at[slot],
+            line_recv_sem.at[slot],
+            line_dev(way),
+        )
+
+    def next_hop(way, far, k):
+        slot = slot_of(way, far, k)
+        return remote(
+            line_slots.at[slot_of(way, far + 1, k)],
+            line_slots.at[slot],
+            line_send_sem.at[slot],
+            line_recv_sem.at[slot],
+            line_dev(way),
+        )
+
+    def came(way, far, k):
+        slot = slot_of(way, far, k)
+        block = line_slots.at[slot]
+        remote(
+            block, block, line_send_sem.at[slot], line_recv_sem.at[slot], line_dev(way)
+        ).wait_recv()
+
+    turn = (3, 1, 2, 0)
+
+    def start_first(blocks):
+        def start(way):
+            for far, k in blocks:
+                first_hop(way, far, k).start()
+
+        for way in range(2):
+            if line > 1:
+                pl.when(is_first(way))(functools.partial(start, way))
+
+    start_first([(far, k) for far in range(last_dp, 1, -1) for k in turn])
+
+    def pass_on(way, far, k):
+        came(way, far + 1, k)
+        slot = slot_of(way, far + 1, k)
+        line_slots[slot] = (line_slots[slot].astype(f32) + own_mlp(goal(way, far), k)).astype(bf16)
+        next_hop(way, far, k).start()
+
+    def mlp_step(far, k):
+        for way in range(2):
+            pl.when(not_first(way) & has_goal(way, far))(functools.partial(pass_on, way, far, k))
+
+    def to_owner(k, came=False):
+        place = plane[k][1] if came else ctx
+        return remote(
+            line_slots.at[k], mlp_reduced.at[place], plane_send_sem.at[k], plane_recv_sem.at[k], plane[k]
+        )
+
+    own_done = pltpu.make_async_copy(line_slots.at[0], mlp_reduced.at[ctx], plane_send_sem.at[0])
+
+    def mlp_last(k):
+        if line > 1:
+            for way in range(2):
+                pl.when(not_first(way))(functools.partial(came, way, 1, k))
+        total = own_mlp(here_dp, k)
+        for way in range(2):
+            if line > 1:
+                arrived = line_slots[slot_of(way, 1, k)].astype(f32)
+                total = total + jnp.where(not_first(way), arrived, 0.0)
+        line_slots[k] = total.astype(bf16)
+        if k:
+            to_owner(k).start()
+        else:
+            own_done.start()
+
+    events = [
+        functools.partial(mlp_step, far, k) for far in range(line - 2, 0, -1) for k in turn
+    ] + [functools.partial(mlp_last, k) for k in turn]
+    events.reverse()
+
+    def move(count):
+        for _ in range(min(count, len(events))):
+            events.pop()()
+
+    for load in loads + held[:1]:
+        load.wait()
+
+    def loaded(index, first, size):
+        return attn_grads[pl.ds(pl.multiple_of(first + index * half, 64), size), 0:width]
+
+    def norms(first, size, carry):
+        at = pl.ds(first, size)
+        part, gain_two = norm_back(loaded(0, first, size), gain_rows[2:3], loaded(2, first, size))
+        middle_grad = cotangent[at].astype(f32) + part
+        input_out[at] = middle_grad
+        grad, gain_one = norm_back(loaded(1, first, size), gain_rows[1:2], middle_grad)
+        branch_low[pl.ds(pl.multiple_of(core * half + first, 64), size)] = grad.astype(bf16)
+        return (
+            carry[0] + jnp.sum(gain_one, axis=0, keepdims=True),
+            carry[1] + jnp.sum(gain_two, axis=0, keepdims=True),
+        )
+
+    nothing = jnp.zeros((1, width), f32)
+    small_rows[...] = jnp.zeros_like(small_rows)
+    gain_one, gain_two = in_rows(half, norms, (nothing, nothing))
+    small_rows[1:2] = gain_one
+    small_rows[2:3] = gain_two
+    small_rows[3:4] = gain_three[...]
+
+    def halves(came):
+        rows = pl.ds(pl.multiple_of((1 - core if came else core) * half, 64), half)
+        return remote(
+            branch_low.at[rows], branch_low.at[rows], core_send_sem.at[0], core_recv_sem.at[0], core_dev
+        )
+
+    halves(False).start()
+    halves(True).wait_recv()
+
+    def inward(start, size):
+        grad = jnp.dot(
+            branch_low[...],
+            attn_full[:, pl.ds(pl.multiple_of(3 * HD + start, 128), size)],
+            preferred_element_type=f32,
+        )
+        attended_grad[:, pl.ds(start, size)] = grad.astype(bf16)
+
+    held[1].wait()
+    in_columns(2 * HD, inward)
+
+    block_rows = 256
+    reach = block_rows + behind
+    keyval_grad[...] = jnp.zeros_like(keyval_grad)
+    for load in held[2:5]:
+        load.wait()
+
+    def retreat(first, head):
+        at = pl.ds(first, block_rows)
+        near = pl.ds(first, reach)
+        columns = slice(head * HD, (head + 1) * HD)
+        scores = contract_columns(query[head, at], keyval[0, near]) * HD ** (-0.5)
+        key_at = first + lax.broadcasted_iota(jnp.int32, (block_rows, reach), 1)
+        query_at = first + behind + lax.broadcasted_iota(jnp.int32, (block_rows, reach), 0)
+        scores = jnp.where((key_at >= lowest[at]) & (key_at <= query_at), scores, -1e30)
+        probs = jnp.exp(scores - log_total[head, at])
+        grads = attended_grad[at, columns]
+        probs_grad = contract_columns(grads, keyval[1, near])
+        delta = jnp.sum(probs * probs_grad, axis=1, keepdims=True)
+        score_grad = (probs * (probs_grad - delta)).astype(bf16)
+        query_grad[at, columns] = (
+            jnp.dot(score_grad, keyval[0, near], preferred_element_type=f32) * HD ** (-0.5)
+        )
+        keyval_grad[0, near] += contract_rows(score_grad, query[head, at]) * HD ** (-0.5)
+        keyval_grad[1, near] += contract_rows(probs.astype(bf16), grads)
+
+    for block in range(row_count // block_rows):
+        for head in range(2):
+            retreat(block * block_rows, head)
+    move(2)
+
+    keyval_send[0] = keyval_grad[1 - core].astype(bf16)
+    to_core = remote(
+        keyval_send.at[0], keyval_take, core_send_sem.at[1], core_recv_sem.at[1], core_dev
+    )
+    to_core.start()
+
+    def query_rows(first, size, carry):
+        at = pl.ds(first, size)
+        total = carry
+        for head in range(2):
+            columns = slice(head * HD, (head + 1) * HD)
+            grads = turned(query_grad[at, columns], cosine[at], -sine[at])
+            grad, gain = norm_back(lin[at, columns], head_rows[4:5], grads)
+            lin_grad[at, columns] = grad.astype(bf16)
+            total = total + jnp.sum(gain, axis=0, keepdims=True)
+        return total
+
+    for load in held[5:]:
+        load.wait()
+    head_zero = in_rows(row_count, query_rows, jnp.zeros((1, HD), f32))
+    move(1)
+    to_core.wait_recv()
+    keyval_grad[core] = keyval_grad[core] + keyval_take[...].astype(f32)
+    keyval_send[1, 0:behind] = keyval_grad[core, 0:behind].astype(bf16)
+    to_past = remote(
+        keyval_send.at[1, pl.ds(0, behind)],
+        past_take,
+        core_send_sem.at[2],
+        core_recv_sem.at[2],
+        (dp, ctx - 1, core),
+    )
+    pl.when(ctx > 0)(to_past.start)
+
+    def outward(start, size):
+        attn_grads[0:width, pl.ds(pl.multiple_of(3 * HD + start, 128), size)] = contract_rows(
+            branch_low[...], attended[:, pl.ds(start, size)]
+        )
+
+    in_columns(2 * HD, outward)
+
+    @pl.when(ctx < 3)
+    def _():
+        to_past.wait_recv()
+        late = pl.ds(row_count, behind)
+        keyval_grad[core, late] = keyval_grad[core, late] + past_take[...].astype(f32)
+
+    def keyval_rows(first, size, carry):
+        at = pl.ds(first, size)
+        values = keyval_grad[core, pl.ds(pl.multiple_of(first + behind, 64), size)]
+        grads = turned(values, cosine[at], -sine[at])
+        grad, gain = norm_back(lin[at, 2 * HD : 3 * HD], head_rows[5:6], grads)
+        lin_grad[at, 2 * HD : 3 * HD] = jnp.where(core == 0, grad, values).astype(bf16)
+        return carry + jnp.sum(gain, axis=0, keepdims=True)
+
+    head_one = in_rows(row_count, keyval_rows, jnp.zeros((1, HD), f32))
+    head_one = jnp.where(core == 0, head_one, 0.0)
+
+    def weigh(start, size):
+        attn_grads[0:width, pl.ds(start, size)] = contract_rows(
+            normed_one[...], lin_grad[:, pl.ds(start, size)]
+        )
+
+    in_columns(3 * HD, weigh)
+    move(1)
+    start_first([(1, k) for k in turn[:2]])
+
+    def back(start, size):
+        columns = pl.ds(start, size)
+        product = contract_columns(lin_grad[...], attn_full[columns, 0 : 3 * HD])
+        first, second = product[:half], product[half:]
+        partial[:, columns] = jnp.where(core == 0, first, second)
+        core_send[:, columns] = jnp.where(core == 0, second, first).astype(bf16)
+
+    in_columns(width, back)
+    exchange = remote(core_send, core_take, core_send_sem.at[3], core_recv_sem.at[3], core_dev)
+    exchange.start()
+    exchange.wait_recv()
+
+    def finish(first, size, carry):
+        at = pl.ds(first, size)
+        whole_at = pl.ds(pl.multiple_of(core * half + first, 64), size)
+        grads = partial[at] + core_take[at].astype(f32)
+        part, gain = norm_back(tokens[whole_at].astype(f32), gain_rows[0:1], grads)
+        input_out[at] = input_out[at] + part
+        return carry + jnp.sum(gain, axis=0, keepdims=True)
+
+    small_rows[0:1] = in_rows(half, finish, nothing)
+
+    row_of = lax.broadcasted_iota(jnp.int32, (width, HD), 0)
+    head_of = lax.broadcasted_iota(jnp.int32, (width, HD), 1)
+    shift = owned_heads.bit_length() - 1
+    chosen = row_of == (head_of >> shift) * owned + (head_of & (owned_heads - 1))
+    heads = jnp.concatenate([head_zero, head_one, jnp.zeros((6, HD), f32)], axis=0)
+    spread = contract_columns(heads.astype(bf16), chosen.astype(f32).astype(bf16))
+    small_rows[4:6] = spread[0:2]
+    smalls = remote(
+        small_rows.at[pl.ds(0, 8)], small_take, core_send_sem.at[4], core_recv_sem.at[4], core_dev
+    )
+    smalls.start()
+    smalls.wait_recv()
+    smalls.wait_send()
+    small_rows[0:8] = small_rows[0:8] + small_take[...]
+    attn_grads[0:width, 5 * HD : 5 * HD + 128] = small_rows[...].T
+
+    for block in range(n_dp * 4):
+        attn_blocks[block] = attn_grads[block * owned : (block + 1) * owned, :].astype(bf16)
+
+    def attn_plane(k, place):
+        index = (k - 1) * n_dp + place
+        return remote(
+            attn_blocks.at[place * 4 + plane[k][1]],
+            attn_plane_take.at[index],
+            attn_plane_send_sem.at[index],
+            attn_plane_recv_sem.at[index],
+            plane[k],
+        )
+
+    for place in range(n_dp):
+        for k in (3, 1, 2):
+            attn_plane(k, place).start()
+    move(len(events) - 4)
+    for place in range(n_dp):
+        total = attn_blocks[place * 4 + ctx].astype(f32)
+        for k in (1, 2, 3):
+            attn_plane(k, place).wait_recv()
+            total = total + attn_plane_take[(k - 1) * n_dp + place].astype(f32)
+        attn_sums[place] = total.astype(bf16)
+
+    def attn_hop(way, far, first):
+        source = attn_sums.at[goal(way, far)] if first else attn_slots.at[way * line + far + 1]
+        index = way * line + far
+        return remote(
+            source,
+            attn_slots.at[index],
+            attn_line_send_sem.at[index],
+            attn_line_recv_sem.at[index],
+            line_dev(way),
+        )
+
+    def attn_came(way, far):
+        index = way * line + far
+        block = attn_slots.at[index]
+        remote(
+            block, block, attn_line_send_sem.at[index], attn_line_recv_sem.at[index], line_dev(way)
+        ).wait_recv()
+
+    def attn_start(way):
+        for far in range(last_dp, 0, -1):
+            attn_hop(way, far, True).start()
+
+    def attn_pass(way, far):
+        attn_came(way, far + 1)
+        index = way * line + far + 1
+        total = attn_slots[index].astype(f32) + attn_sums[goal(way, far)].astype(f32)
+        attn_slots[index] = total.astype(bf16)
+        attn_hop(way, far, False).start()
+
+    for way in range(2):
+        if line > 1:
+            pl.when(is_first(way))(functools.partial(attn_start, way))
+    start_first([(1, k) for k in turn[2:]])
+    for far in range(line - 2, 0, -1):
+        for way in range(2):
+            pl.when(not_first(way) & has_goal(way, far))(functools.partial(attn_pass, way, far))
+    move(4)
+    if line == 1:
+        attn_reduced[...] = attn_sums[...]
+    else:
+        total = attn_sums[dp].astype(f32)
+        for way in range(2):
+            pl.when(not_first(way))(functools.partial(attn_came, way, 1))
+            arrived = attn_slots[way * line + 1].astype(f32)
+            total = total + jnp.where(not_first(way), arrived, 0.0)
+        attn_reduced[0] = total.astype(bf16)
+
+    for k in (1, 2, 3):
+        to_owner(k, True).wait_recv()
+        to_owner(k).wait_send()
+    own_done.wait()
+    halves(False).wait_send()
+    to_core.wait_send()
+    pl.when(ctx > 0)(to_past.wait_send)
+    exchange.wait_send()
+    for place in range(n_dp):
+        for k in (1, 2, 3):
+            attn_plane(k, place).wait_send()
+
+    def first_left(way):
+        for far in range(last_dp, 0, -1):
+            attn_hop(way, far, True).wait_send()
+            for k in turn:
+                first_hop(way, far, k).wait_send()
+
+    def left(way, far):
+        attn_hop(way, far, False).wait_send()
+        for k in turn:
+            next_hop(way, far, k).wait_send()
+
+    for way in range(2):
+        if line > 1:
+            pl.when(is_first(way))(functools.partial(first_left, way))
+        for far in range(line - 2, 0, -1):
+            pl.when(not_first(way) & has_goal(way, far))(functools.partial(left, way, far))
+
+
+def retreat_call(n_dp, line, owned_heads, *arrays):
+    tokens, attn_full, keyval = arrays[4], arrays[11], arrays[15]
+    mlp_grads = arrays[18]
+    row_count, width = tokens.shape
+    half = row_count // 2
+    blocks = n_dp * 4
+    owned, hid = mlp_grads.shape[1], mlp_grads.shape[2] // 3
+    attn_cols = attn_full.shape[1]
+    reach = keyval.shape[1]
+    behind = reach - row_count
+    f32, bf16 = jnp.float32, jnp.bfloat16
+    vmem = pl.BlockSpec(memory_space=pltpu.VMEM)
+    anywhere = pl.BlockSpec(memory_space=pl.ANY)
+    dma = pltpu.SemaphoreType.DMA
+    return pl.pallas_call(
+        functools.partial(retreat_kernel, n_dp, line, owned_heads),
+        out_shape=(
+            jax.ShapeDtypeStruct((half, width), f32),
+            jax.ShapeDtypeStruct((4, owned, 3 * hid), bf16),
+            jax.ShapeDtypeStruct((n_dp if line == 1 else 1, owned, attn_cols), bf16),
+        ),
+        in_specs=[
+            anywhere if index < 5 or 11 <= index <= 16 or index == 18 else vmem
+            for index in range(len(arrays))
+        ],
+        out_specs=(vmem, anywhere, vmem),
+        scratch_shapes=[
+            pltpu.VMEM((max(8 * (line - 1), 4), owned, 3 * hid), bf16),
+            pltpu.VMEM((max(width, 3 * half), attn_cols), f32),
+            pltpu.VMEM((blocks, owned, attn_cols), bf16),
+            pltpu.VMEM((3 * n_dp, owned, attn_cols), bf16),
+            pltpu.VMEM((n_dp, owned, attn_cols), bf16),
+            pltpu.VMEM((2 * line, owned, attn_cols), bf16),
+            pltpu.VMEM((row_count, width), bf16),
+            pltpu.VMEM((row_count, 2 * HD), bf16),
+            pltpu.VMEM((row_count, 2 * HD), f32),
+            pltpu.VMEM((row_count, 3 * HD), bf16),
+            pltpu.VMEM((2, reach, HD), f32),
+            pltpu.VMEM((2, reach, HD), bf16),
+            pltpu.VMEM((reach, HD), bf16),
+            pltpu.VMEM((behind, HD), bf16),
+            pltpu.VMEM((half, width), f32),
+            pltpu.VMEM((half, width), bf16),
+            pltpu.VMEM((half, width), bf16),
+            pltpu.VMEM((128, width), f32),
+            pltpu.VMEM((8, width), f32),
+            dma((8 * line,)),
+            dma((8 * line,)),
+            dma((4,)),
+            dma((4,)),
+            dma((4 * n_dp,)),
+            dma((4 * n_dp,)),
+            dma((2 * line,)),
+            dma((2 * line,)),
+            dma((5,)),
+            dma((5,)),
+            dma((12,)),
+            pltpu.VMEM(mlp_grads.shape, bf16),
+        ]
+        + [
+            pltpu.VMEM(arrays[index].shape, arrays[index].dtype)
+            for index in (3, 4, 11, 12, 13, 14, 15, 16)
+        ],
+        compiler_params=pltpu.CompilerParams(
+            collective_id=2, has_side_effects=True, vmem_limit_bytes=63 * 2**20
+        ),
+        cost_estimate=pl.CostEstimate(
+            flops=10**10, bytes_accessed=40 * 2**20, transcendentals=2 * 10**6
+        ),
+        name="retreat",
+    )(*arrays)
 
 
 def on_device(
@@ -947,131 +1527,73 @@
         log_total,
         branch_raw,
         middle,
-        normed_two_half,
+        group_rows,
     ) = attend_call(
         n_dp, owned_heads, behind, tokens, query_cosine, query_sine, lowest, attn_pack, mlp_pack
     )
-    key_count = behind + row_count
-    head_count = cols // HD
-    full_query = attn_full[:, :cols]
-    half_keyval = attn_full[:, cols : cols + HD]
-    full_output = attn_full[:, cols + HD : 2 * cols + HD]
-    query_norm_back = jax.vjp(
-        rms_norm, lin[:, :cols].reshape(row_count, head_count, HD), head_rows[4]
-    )[1]
-    key_norm_back = jax.vjp(rms_norm, lin[:, cols:], head_rows[5])[1]
-    key_all, value_all = keyval_all[0], keyval_all[1]
-    post_one_back = jax.vjp(rms_norm, branch_raw, gain_rows[1])[1]
-    norm_two_back = jax.vjp(rms_norm, middle, gain_rows[2])[1]
-    inputs_half = half_of(tokens, 0).astype(f32)
-    key_index = jnp.arange(key_count, dtype=jnp.int32)[None, :]
-    allowed = (key_index >= lowest) & (key_index <= row_index[:, None] + behind)
-
-    def core_summed(partial):
-        arrived = from_partner(half_not_of(partial, 0).astype(bf16), "tensor", 1)
-        return half_of(partial, 0) + arrived.astype(f32)
-
     cotangent_half = half_of(out_cotangent, 0)
     (
         result_half,
         normed_two_grad,
         gain_three_part,
-        normed_two,
-        mlp_raw_low,
-        hidden_low,
-        gate_grad,
+        mlp_grads,
     ) = mlp_call(
-        normed_two_half,
+        group_rows,
         middle,
         cotangent_half,
         gain_rows[3:4],
         mlp_full.reshape(n_dp * n_ctx * owned, 3 * wide),
     )
-    gain_three_grad = gain_three_part[0]
-    cotangent_half = cotangent_half.astype(f32)
     result = core_ordered(result_half, from_partner(result_half, "tensor", 1))
-    def exchanged(tiles):
-        return lax.all_to_all(tiles, ("dp", "ctx"), split_axis=0, concat_axis=0, tiled=True)
-
-    def to_owners(term):
-        arrived = exchanged(term.astype(bf16).reshape(n_dp * n_ctx, owned, term.shape[1]))
-        return arrived.reshape(n_dp, n_ctx, owned, term.shape[1]).astype(f32).sum(axis=0)
+
+    line = n_dp if n_dp <= 4 else 1
+
+    mlp_grads = mlp_grads.reshape(n_dp, n_ctx, owned, 3 * wide)
+    if line == 1:
+        mlp_grads = lax.psum_scatter(mlp_grads, "dp", scatter_dimension=0, tiled=True)
+    mlp_grads = mlp_grads.reshape(line * n_ctx, owned, 3 * wide)
+    input_half, mlp_reduced, attn_reduced = retreat_call(
+        n_dp,
+        line,
+        owned_heads,
+        normed_two_grad,
+        middle,
+        branch_raw,
+        cotangent_half,
+        tokens,
+        query_cosine,
+        query_sine,
+        lowest,
+        gain_rows,
+        head_rows,
+        gain_three_part,
+        attn_full,
+        normed_one,
+        lin,
+        query_rot,
+        keyval_all,
+        attended_low,
+        log_total,
+        mlp_grads,
+    )
+    input_grad = core_ordered(input_half, from_partner(input_half, "tensor", 1))
+
+    if line == 1:
+        attn_reduced = lax.psum_scatter(attn_reduced, "dp", scatter_dimension=0, tiled=True)
+    attn_reduced = attn_reduced[0].astype(f32)
 
     def from_parts(tiles):
-        return jnp.moveaxis(tiles, 0, 1).reshape(owned, n_ctx * wide)[:, :half_ff]
-
-    down_reduced = from_parts(to_owners(contract_rows(mlp_raw_low, hidden_low)))
-    gate_arrived = to_owners(contract_rows(normed_two, gate_grad))
-    gate_arrived = gate_arrived.reshape(n_ctx, owned, wide // 128, 2, 128)
+        return jnp.moveaxis(tiles, 0, 1).reshape(owned, n_ctx * wide)[:, :half_ff].astype(f32)
+
+    gate_arrived = mlp_reduced[:, :, : 2 * wide].reshape(n_ctx, owned, wide // 128, 2, 128)
     gate_reduced = jnp.stack(
         [from_parts(gate_arrived[:, :, :, side].reshape(n_ctx, owned, wide)) for side in range(2)],
         axis=1,
     )
-
-    middle_part, gain_two_grad = norm_two_back(normed_two_grad)
-    middle_grad = cotangent_half + middle_part
-    branch_pre_grad, gain_one_grad = post_one_back(middle_grad)
-    branch_half = branch_pre_grad.astype(bf16)
-    branch_low = core_ordered(branch_half, from_partner(branch_half, "tensor", 1))
-    output_w_grad = contract_rows(branch_low, attended_low)
-    attended_grad = (
-        jnp.dot(branch_low, full_output, preferred_element_type=f32)
-        .astype(bf16)
-        .reshape(row_count, head_count, HD)
-    )
-    scores_again = (
-        jnp.einsum("hqd,kd->hqk", query_rot, key_all, preferred_element_type=f32) * score_scale
-    )
-    prob_again = jnp.exp(jnp.where(allowed[None], scores_again, -1e30) - log_total)
-    probs_grad = jnp.einsum("qhd,kd->hqk", attended_grad, value_all, preferred_element_type=f32)
-    value_grad_all = jnp.einsum(
-        "hqk,qhd->kd", prob_again.astype(bf16), attended_grad, preferred_element_type=f32
-    )
-    row_delta = jnp.sum(prob_again * probs_grad, axis=-1, keepdims=True)
-    score_grad = (prob_again * (probs_grad - row_delta)).astype(bf16)
-    query_rot_grad = (
-        jnp.einsum("hqk,kd->qhd", score_grad, key_all, preferred_element_type=f32) * score_scale
-    )
-    key_grad_all = (
-        jnp.einsum("hqk,hqd->kd", score_grad, query_rot, preferred_element_type=f32) * score_scale
-    )
-    grad_mine = jnp.where(core_first, key_grad_all, value_grad_all)
-    grad_other = jnp.where(core_first, value_grad_all, key_grad_all)
-    grad_mine = grad_mine + from_partner(grad_other.astype(bf16), "tensor", 1).astype(f32)
-    returned = from_behind(grad_mine[:behind].astype(bf16), "ctx", -1).astype(f32)
-    own_grad = grad_mine[behind:].at[row_count - behind :].add(returned)
-    query_normed_grad = rotate(query_rot_grad, query_cosine[:, None, :], -query_sine[:, None, :])
-    query_pre_grad, head_zero_part = query_norm_back(query_normed_grad)
-    query_lin_grad = query_pre_grad.reshape(row_count, head_count * HD).astype(bf16)
-    key_pre_grad, head_one_part = key_norm_back(rotate(own_grad, query_cosine, -query_sine))
-    keyval_lin_grad = jnp.where(core_first, key_pre_grad, own_grad).astype(bf16)
-    head_one_part = jnp.where(core_first, head_one_part, 0.0)
-    normed_one_grad = core_summed(
-        contract_columns(query_lin_grad, full_query) + contract_columns(keyval_lin_grad, half_keyval)
-    )
-    query_w_grad = contract_rows(normed_one, query_lin_grad)
-    keyval_w_grad = contract_rows(normed_one, keyval_lin_grad)
-    norm_one_back = jax.vjp(rms_norm, inputs_half, gain_rows[0])[1]
-    input_part, gain_zero_grad = norm_one_back(normed_one_grad)
-    input_half = middle_grad + input_part
-    input_grad = core_ordered(input_half, from_partner(input_half, "tensor", 1))
-
-    gains_part = jnp.stack([gain_zero_grad, gain_one_grad, gain_two_grad, gain_three_grad], axis=1)
-    heads_part = jnp.stack([head_zero_part, head_one_part], axis=1)
-    heads_part = jnp.pad(
-        heads_part.reshape(-1, owned_heads, 2), ((0, 0), (0, owned - owned_heads), (0, 0))
-    ).reshape(-1, 2)
-    small_part = jnp.concatenate([gains_part, heads_part], axis=1)
-    small_grad = small_part + from_partner(small_part, "tensor", 1)
-    attn_grad = jnp.concatenate(
-        [query_w_grad, keyval_w_grad, output_w_grad, jnp.pad(small_grad, ((0, 0), (0, 122)))], axis=1
-    ).astype(bf16)
-    attn_grad = jnp.moveaxis(attn_grad.reshape(n_dp, n_ctx, owned, -1), 1, 0)
-    attn_arrived = along_line(attn_grad, "ctx").astype(f32).sum(axis=0).astype(bf16)
-    attn_sum = along_line(attn_arrived, "dp").astype(f32).sum(axis=0)
-    query_reduced = attn_sum[:, :cols]
-    keyval_half = attn_sum[:, cols : cols + HD]
-    output_reduced = attn_sum[:, cols + HD : 2 * cols + HD]
+    down_reduced = from_parts(mlp_reduced[:, :, 2 * wide :])
+    query_reduced = attn_reduced[:, :cols]
+    keyval_half = attn_reduced[:, cols : cols + HD]
+    output_reduced = attn_reduced[:, cols + HD : 2 * cols + HD]
     keyval_not = from_partner(keyval_half, "tensor", 1)
     keyval_reduced = jnp.concatenate(
         [
@@ -1080,8 +1602,8 @@
         ],
         axis=1,
     )
-    gains_reduced = attn_sum[:, 2 * cols + HD : 2 * cols + HD + 4]
-    heads_reduced = attn_sum[:owned_heads, 2 * cols + HD + 4 : 2 * cols + HD + 6]
+    gains_reduced = attn_reduced[:, 2 * cols + HD : 2 * cols + HD + 4]
+    heads_reduced = attn_reduced[:owned_heads, 2 * cols + HD + 4 : 2 * cols + HD + 6]
 
     gains_new, gain_first_new, gain_second_new = adam_step(
         norm_gains, gains_reduced, gain_first, gain_second, 0.5, 0.0

time: 626 us -> 486 us (0.78)
  Pallas kernels: 298 us -> 405 us
  waiting for transfers between devices: 81.9 us -> 0.01 us
  matrix products: 54.5 us -> 0 us
  other arithmetic: 70.8 us -> 28.7 us
  starting transfers between devices: 43.2 us -> 2.75 us
  local copies, waits for them, and re-layouts: 64.7 us -> 39.1 us
    pallas_call x0 -> x1, Pallas kernels: none -> 138 us  [retreat_call(): pl.pallas_call(functools.partial(retreat_kernel, n_dp, line, owned_heads)...]
    ppermute x7 -> x0, waiting for transfers between devices: 81.8 us -> none  [the longest x6 76.8 us: along_line(): lax.ppermute(tile, axis, [(i, (i + shift) % n) for i in range(n)])]
    dot_general x13 -> x0, matrix products: 54.5 us -> none  [the longest x5 37.6 us: contract_rows(): lax.dot_general(left_side, right_side, (((0,), (0,)), ((), ())), preferre...]
    pallas_call x1, Pallas kernels: 155 us -> 130 us  [mlp_call(): pl.pallas_call(mlp_kernel, out_shape=(jax.ShapeDtypeStruct((half, width),...]
    ppermute x7 -> x0, starting transfers between devices: 21 us -> none  [the longest x6 19.7 us: along_line(): lax.ppermute(tile, axis, [(i, (i + shift) % n) for i in range(n)])]
    reduce_sum x14 -> x0, other arithmetic: 20.5 us -> none  [the longest x6 10.2 us: rms_norm(): return values * scale * gain_row]
    all_to_all x2 -> x0, starting transfers between devices: 13.2 us -> none  [exchanged(): lax.all_to_all(tiles, ('dp', 'ctx'), split_axis=0, concat_axis=0, tiled=T...]
    reshape x7 -> x4, local copies, waits for them, and re-layouts: 9.31 us -> 0.36 us  [the longest x1 0.23 us: on_device(): mlp_reduced[:, :, :2 * wide].reshape(n_ctx, owned, wide // 128, 2, 128)]
  transfers between devices with their start and end apart: 16 -> 3, of which waited for: 5 -> 0; matrix products, arithmetic and copies ran while one was open for 21% -> 8% of each run, Pallas kernels for 0% -> 0%
where the time goes in v2:
time: 486 us; the launch traced here: 478 us
  Pallas kernels  405 us (83%)
  local copies, waits for them, and re-layouts  39.1 us (8%)
  other arithmetic  28.7 us (6%)
    pallas_call x1, Pallas kernels, attend_call(): pl.pallas_call(functools.partial(attend_kernel, n_dp, owned_heads), out_s...  138 us
    pallas_call x1, Pallas kernels, retreat_call(): pl.pallas_call(functools.partial(retreat_kernel, n_dp, line, owned_heads)...  138 us
    pallas_call x1, Pallas kernels, mlp_call(): pl.pallas_call(mlp_kernel, out_shape=(jax.ShapeDtypeStruct((half, width),...  130 us
    unnamed x71, local copies, waits for them, and re-layouts  19.4 us
  transfers between devices with their start and end apart: 3, of which 0 were waited for; matrix products, arithmetic and copies ran while one was open for 8% of the time, Pallas kernels for 0%

profile of v2, /device:TPU:9, one launch (start us, length us, event | category | flops | bytes accessed | tf_op | source)
XLA Modules:
  0.0 477.6 jit_solution(2615088054659711700)
XLA Ops:
  2.4 0.9 fusion.7.lowest
  3.3 1.3 broadcast_multiply_fusion.3
  5.4 0.9 convert_element_type.52
  6.3 0.9 convert_element_type.54
  7.3 1.7 copy.287
  10.7 1.6 copy.240
  12.9 0.9 dynamic-slice_convert_fusion
  13.8 2.5 multiply_sine_fusion
  16.3 1.2 maximum_bitcast_fusion.mlp_pack
  18.2 137.9 %attend.1 = (bf16[16,72,2688]{2,1,0:T(8,128)(2,1)}, bf16[1152,1408]{1,0:T(8,128)(2,1)}, f32[8,1152]{1,0:T(8,128)}, f32[8,256]{1,0:T(8,128)}, bf16[768,1152]{1,0:...) custom-call(bf16[768,1152]{1,0:T(8,128)(2,1)} %tokens_in.1, ...), custom_call_target="tpu_custom_call" | custom-call | flops 4000000000 | bytes 31457280 | tf_op jit(solution)/shard_map/attend/pallas_call | solution.py:567
  156.1 1.4 slice.49.gain
  157.4 1.0 constant_dynamic-slice_fusion.cotangent.cotangent_in
  158.4 130.0 %feed_forward.1 = (bf16[384,1152]{1,0:T(8,128)(2,1)}, f32[384,1152]{1,0:T(8,128)}, f32[1,1152]{1,0:T(1,128)}, bf16[1152,2688]{1,0:T(8,128)(2,1)}) custom-call(bf16[4,2,384,1152]{3,2,1,0:T(8,128)(2,1)} %get-tuple-element.43.rows_in, f32[384,1152]{1,0:T(8,128)} %get-tuple-element.44.middle, ...), custom_call_target="tpu_custom_call" | custom-call | flops 57076088832 | bytes 31457280 | tf_op jit(solution)/shard_map/feed_forward/pallas_call | solution.py:833
  288.4 137.6 %retreat.1 = (f32[384,1152]{1,0:T(8,128)}, bf16[4,72,2688]{2,1,0:T(8,128)(2,1)}, bf16[1,72,1408]{2,1,0:T(8,128)(2,1)}) custom-call(f32[384,1152]{1,0:T(8,128)} %get-tuple-element.48.back_sum, f32[384,1152]{1,0:T(8,128)} %get-tuple-element.44.middle, f32[384,1152]{1,0:T(8,128)} %get-tuple-element.49.branch, ...), custom_call_target="tpu_custom_call" | custom-call | flops 10000000000 | bytes 41943040 | tf_op jit(solution)/shard_map/retreat/pallas_call | solution.py:1388
  426.1 1.0 bitcast_convert_fusion
  427.7 2.2 collective-permute-start.2
  430.5 1.3 slice.55
  431.8 1.1 slice_bitcast_fusion
  433.2 5.5 %slice_reduce_fusion.1 = (bf16[4,72,7,128]{3,2,1,0:T(8,128)(2,1)S(1)}, bf16[4,72,7,128]{3,2,1,0:T(8,128)(2,1)S(1)}) fusion(bf16[4,72,7,2,128]{4,3,2,1,0:T(2,128)(2,1)S(1)} %reshape.128), kind=kLoop, calls=%fused_computation.15 | loop fusion | bytes 2064384 | tf_op jit(solution)/shard_map/slice | solution.py:1590
  445.3 1.1 copy-done.9
  446.7 2.1 multiply_subtract_fusion.1
  448.8 1.1 copy-done.4
  450.5 3.5 multiply_subtract_fusion
  454.1 1.1 multiply_subtract_fusion.2
  455.4 4.0 copy.269
  459.4 2.3 copy.270
  461.7 2.3 copy.271
  468.0 0.9 broadcast_select_fusion.5
  469.8 1.6 broadcast_select_fusion.3
  471.4 1.3 pad_maximum_fusion.1
  473.5 1.7 broadcast_select_fusion.1
  475.2 2.0 pad_maximum_fusion
  (115 shorter events, 20.2 us)
Async XLA Ops:
  10.7 2.1 copy-start.2
  18.2 139.2 %copy-start.13 = (bf16[768,1152]{1,0:T(8,128)(2,1)S(1)}, bf16[768,1152]{1,0:T(8,128)(2,1)}, u32[]{:S(2)}) copy-start(bf16[768,1152]{1,0:T(8,128)(2,1)} %param.25) | copy-start | bytes 5308420
  426.0 6.8 %copy-start.26 = (f32[16,2]{0,1:T(2,128)S(1)}, f32[16,2]{0,1:T(2,128)}, u32[]{:S(2)}) copy-start(f32[16,2]{0,1:T(2,128)} %param.30) | copy-start | bytes 388
  427.0 3.4 copy-start.6
  427.7 40.3 %collective-permute-start.2 = (f32[72,256]{1,0:T(8,128)}, f32[72,256]{1,0:T(8,128)}, u32[]{:S(2)}, u32[]{:S(2)}) collective-permute-start(f32[72,256]{1,0:T(8,128)} %slice.67), channel_id=1, source_target_pairs={{1,0},{0,1},{3,2},{2,3},{5,4},{4,5},{7,6},{6,7},{9,8},{8,9},{11,10... | collective-permute-start | bytes 221192 | tf_op jit(solution)/shard_map/ppermute | solution.py:30
  430.0 42.8 %collective-permute-start.1 = (f32[384,1152]{1,0:T(8,128)}, f32[384,1152]{1,0:T(8,128)}, u32[]{:S(2)}, u32[]{:S(2)}) collective-permute-start(f32[384,1152]{1,0:T(8,128)} %get-tuple-element.60), channel_id=1, source_target_pairs={{1,0},{0,1},{3,2},{2,3},{5,4},{4,5},{7,6},{6,7},{9,8},{8,9},{11,10... | collective-permute-start | bytes 5308424 | tf_op jit(solution)/shard_map/ppermute | solution.py:30
  430.0 39.8 %collective-permute-start = (bf16[384,1152]{1,0:T(8,128)(2,1)}, bf16[384,1152]{1,0:T(8,128)(2,1)}, u32[]{:S(2)}, u32[]{:S(2)}) collective-permute-start(bf16[384,1152]{1,0:T(8,128)(2,1)} %get-tuple-element.47), channel_id=1, source_target_pairs={{1,0},{0,1},{3,2},{2,3},{5,4},{4,5},{7,6},{6,7},{9,8},{8,9},{11,10... | collective-permute-start | bytes 2654216 | tf_op jit(solution)/shard_map/ppermute | solution.py:30
  438.7 1.4 copy-start.27
  438.7 1.5 copy-start.28
  438.7 1.6 copy-start.7
  440.1 5.2 %copy-start.3 = (f32[72,3456]{1,0:T(8,128)S(1)}, f32[72,3456]{1,0:T(8,128)}, u32[]{:S(2)}) copy-start(f32[72,3456]{1,0:T(8,128)} %param.45) | copy-start | bytes 2985988
  445.2 1.2 copy-start.9
  445.2 1.5 copy-start.10
  446.7 2.2 copy-start
  446.7 3.2 copy-start.4
  446.7 3.8 copy-start.5
  450.5 3.5 copy-start.11
  450.5 3.5 copy-start.12
  450.5 3.5 copy-start.15
  450.5 3.5 copy-start.16
  450.5 3.5 copy-start.17
  450.5 3.5 copy-start.18
  454.1 1.1 copy-start.21
  454.1 1.1 copy-start.22
  454.1 1.2 copy-start.23
  454.1 1.2 copy-start.24
  454.1 1.2 copy-start.25
  455.4 4.0 copy-start.1
  461.7 7.2 %copy-start.14 = (f32[72,512]{1,0:T(8,128)S(1)}, f32[72,512]{1,0:T(8,128)}, u32[]{:S(2)}) copy-start(f32[72,512]{1,0:T(8,128)} %param.36) | copy-start | bytes 442372
  461.7 7.2 %copy-start.19 = (f32[72,512]{1,0:T(8,128)S(1)}, f32[72,512]{1,0:T(8,128)}, u32[]{:S(2)}) copy-start(f32[72,512]{1,0:T(8,128)} %param.37) | copy-start | bytes 442372
  461.7 7.2 %copy-start.20 = (f32[72,512]{1,0:T(8,128)S(1)}, f32[72,512]{1,0:T(8,128)}, u32[]{:S(2)}) copy-start(f32[72,512]{1,0:T(8,128)} %param.38) | copy-start | bytes 442372
  471.4 2.1 copy-start.8

commit v3 on v2

--- a/solution.py
+++ b/solution.py
@@ -26,22 +26,15 @@
 MESH = pl.DeviceIdType.MESH
 
 
-def from_partner(block, axis, bits):
-    return lax.ppermute(block, axis, [(i ^ bits, i) for i in range(lax.axis_size(axis))])
-
-
-def core_ordered(own, other):
-    first = lax.axis_index("tensor") == 0
-    return jnp.concatenate([jnp.where(first, own, other), jnp.where(first, other, own)], axis=0)
-
-
 def half_of(array, dim):
     size = array.shape[dim] // 2
     return lax.dynamic_slice_in_dim(array, lax.axis_index("tensor") * size, size, axis=dim)
 
 
 def token_layout(lengths, places):
-    stop_at = jnp.cumsum(lengths)
+    count = lengths.shape[0]
+    before = jnp.arange(count)[:, None] <= jnp.arange(count)[None, :]
+    stop_at = jnp.sum(jnp.where(before, lengths[:, None], 0), axis=0)
     start_at = stop_at - lengths
     segment = jnp.sum((places[:, None] >= stop_at[None, :]).astype(jnp.int32), axis=1)
     owned_by = segment[:, None] == jnp.arange(lengths.shape[0], dtype=jnp.int32)[None, :]
@@ -187,17 +180,17 @@
     attn_pack,
     mlp_pack,
     mlp_full,
-    attn_full,
     gain_rows,
     head_rows,
-    normed_out,
-    lin,
-    query_out,
+    log_total,
+    attn_full_out,
+    normed_out_out,
+    lin_out,
+    query_out_out,
     keyval_out,
-    attended,
-    log_total,
-    branch_out,
-    middle_out,
+    attended_out,
+    branch_out_out,
+    middle_out_out,
     rows_out,
     slots,
     wide_slots,
@@ -220,6 +213,14 @@
     rows_send,
     rows_recv,
     rows_sem,
+    attn_full,
+    normed_out,
+    lin,
+    query_out,
+    attended,
+    branch_out,
+    middle_out,
+    out_sem,
 ):
     dp, ctx, core = places()
     x_dev, y_dev, far_dev, core_dev = plane_partners()
@@ -286,16 +287,45 @@
         index = (way * n_dp + step) * 4 + side
         return remote(block, block, attn_plane_send.at[index], attn_plane_recv.at[index], device)
 
+    pending = []
+
+    def give(source, target):
+        copy = pltpu.make_async_copy(source, target, out_sem.at[len(pending)])
+        copy.start()
+        pending.append(copy)
+
+    def first_hop(way, source, blocks, send, recv):
+        return remote(source, blocks.at[dp * 4 + ctx], send, recv, line_dev(way))
+
+    def attn_first(way):
+        index = way * n_dp
+        return first_hop(
+            way, attn_pack, slots, attn_line_send.at[index], attn_line_recv.at[index]
+        )
+
+    def mlp_own(way):
+        index = way * n_dp * 4
+        return first_hop(
+            way, mlp_pack.at[ctx], mlp_full, mlp_line_send.at[index], mlp_line_recv.at[index]
+        )
+
+    def attn_near(side):
+        return remote(
+            attn_pack,
+            slots.at[dp * 4 + ctx],
+            attn_plane_send.at[side],
+            attn_plane_recv.at[side],
+            plane[side],
+        )
+
     own_attn = pltpu.make_async_copy(attn_pack, slots.at[dp * 4 + ctx], own_sem.at[0])
     own_mlp = pltpu.make_async_copy(mlp_pack.at[ctx], mlp_full.at[dp * 4 + ctx], own_sem.at[1])
     own_attn.start()
     own_mlp.start()
-    own_attn.wait()
-    each(0, lambda way: attn_hop(way, 0).start(), True)
+    each(0, lambda way: attn_first(way).start(), True)
     for side in (1, 2):
-        attn_plane(0, 0, side).start()
-    own_mlp.wait()
-    each(0, lambda way: mlp_hop(way, 0, 0).start(), True)
+        attn_near(side).start()
+    each(0, lambda way: mlp_own(way).start(), True)
 
     def mlp_plane(k, came=False):
         return remote(
@@ -350,6 +380,7 @@
         for _ in range(min(count, len(events))):
             events.pop()()
 
+    own_attn.wait()
     for step in range(1, n_dp):
         each(step, lambda way: came(way, step), False)
         each(step, lambda way: attn_hop(way, step).start(), True)
@@ -377,6 +408,7 @@
         return carry
 
     in_rows(width, narrow, 0)
+    give(attn_full, attn_full_out)
     pick = lax.broadcasted_iota(jnp.int32, (8, 128), 0) == lax.broadcasted_iota(
         jnp.int32, (8, 128), 1
     )
@@ -405,7 +437,8 @@
         )
 
     in_columns(3 * HD, project)
-    move(1)
+    give(normed_out, normed_out_out)
+    give(lin, lin_out)
 
     def turn_keyval(first, size, carry):
         at = pl.ds(first, size)
@@ -446,6 +479,7 @@
         return carry
 
     in_rows(row_count, turn_query, 0)
+    give(query_out, query_out_out)
 
     @pl.when(ctx > 0)
     def _():
@@ -458,7 +492,6 @@
         keyval[:, 0:behind] = jnp.zeros((2, behind, HD), bf16)
 
     to_core(True).wait_recv()
-    move(2)
 
     block_rows = 256
     reach = block_rows + behind
@@ -481,7 +514,9 @@
     for block in range(row_count // block_rows):
         for head in range(2):
             attend(block * block_rows, head)
-        move(1)
+    give(attended, attended_out)
+    give(keyval, keyval_out)
+    move(2)
 
     def outward(start, size):
         partial[:, pl.ds(start, size)] = contract_columns(
@@ -498,6 +533,7 @@
     in_rows(half, give_half, 0)
     exchange = remote(core_send, core_take, keyval_send.at[3], keyval_recv.at[3], core_dev)
     exchange.start()
+    move(1)
     exchange.wait_recv()
 
     def finish(first, size, carry):
@@ -512,6 +548,9 @@
 
     in_rows(half, finish, 0)
 
+    give(branch_out, branch_out_out)
+    give(middle_out, middle_out_out)
+
     def remote_rows(source, target, index, device):
         return remote(source, target, rows_send.at[index], rows_recv.at[index], device)
 
@@ -524,12 +563,11 @@
         gather_step(gather, step)
         outs[step].start()
         if step == 0:
-            keyval_out[...] = keyval[...]
-        move(1)
+            move(1)
     move(len(events))
     for copy in gather:
         copy.wait_send()
-    for copy in outs:
+    for copy in outs + pending + [own_mlp]:
         copy.wait()
 
     exchange.wait_send()
@@ -538,14 +576,21 @@
     pl.when(ctx > 0)(past_to_core().wait_send)
     for k in (1, 2, 3):
         mlp_plane(k).wait_send()
+    each(0, lambda way: attn_first(way).wait_send(), True)
+    each(0, lambda way: mlp_own(way).wait_send(), True)
     for step in range(n_dp - 1):
-        each(step, lambda way: attn_hop(way, step).wait_send(), True)
+        if step:
+            each(step, lambda way: attn_hop(way, step).wait_send(), True)
         for k in range(4):
-            each(step, lambda way: mlp_hop(way, step, k).wait_send(), True)
+            if step or k:
+                each(step, lambda way: mlp_hop(way, step, k).wait_send(), True)
 
     def left(way, step):
         for side in (1, 2, 3):
-            attn_plane(way, step, side).wait_send()
+            if step or side == 3:
+                attn_plane(way, step, side).wait_send()
+            else:
+                attn_near(side).wait_send()
 
     for way, step in order:
         where_held(way, step, left)
@@ -568,21 +613,21 @@
         functools.partial(attend_kernel, n_dp, owned_heads),
         out_shape=(
             array(bf16, blocks, owned, mlp_pack.shape[2]),
-            array(bf16, width, attn_cols),
             array(f32, 8, width),
             array(f32, 8, HD),
+            array(f32, 2, row_count, 1),
+            array(bf16, width, attn_cols),
             array(bf16, row_count, width),
             array(f32, row_count, 3 * HD),
             array(bf16, 2, row_count, HD),
             array(bf16, 2, behind + row_count, HD),
             array(bf16, row_count, 2 * HD),
-            array(f32, 2, row_count, 1),
             array(f32, half, width),
             array(f32, half, width),
             array(bf16, 4, 2, half, width),
         ),
         in_specs=[vmem] * 4 + [anywhere] * 2,
-        out_specs=(anywhere,) + (vmem,) * 11 + (anywhere,),
+        out_specs=(anywhere, vmem, vmem, vmem) + (anywhere,) * 9,
         scratch_shapes=[
             pltpu.VMEM((blocks, owned, attn_cols), bf16),
             pltpu.VMEM((width, attn_cols), f32),
@@ -605,6 +650,14 @@
             dma((10,)),
             dma((10,)),
             dma((4,)),
+            pltpu.VMEM((width, attn_cols), bf16),
+            pltpu.VMEM((row_count, width), bf16),
+            pltpu.VMEM((row_count, 3 * HD), f32),
+            pltpu.VMEM((2, row_count, HD), bf16),
+            pltpu.VMEM((row_count, 2 * HD), bf16),
+            pltpu.VMEM((half, width), f32),
+            pltpu.VMEM((half, width), f32),
+            dma((8,)),
         ],
         compiler_params=pltpu.CompilerParams(
             collective_id=1, has_side_effects=True, vmem_limit_bytes=60 * 2**20
@@ -620,12 +673,13 @@
     rows_in,
     middle,
     cotangent,
-    gain,
+    gain_rows,
     weights_in,
-    result,
+    result_out,
     back_sum,
     gain_sum,
     weights_out,
+    result,
     rows,
     grads,
     hidden,
@@ -648,6 +702,8 @@
     step_rows = 2 * half
     part_a, part_b = pl.ds(0, h), pl.ds(h, h)
     x_dev, y_dev, _, core_dev = plane_partners()
+    core = lax.axis_index("tensor")
+    gain = gain_rows.at[pl.ds(3, 1)]
     f32, bf16 = jnp.float32, jnp.bfloat16
 
     loads = [pltpu.make_async_copy(weights_in, weights, load_sem.at[4])] + [
@@ -687,15 +743,22 @@
         if before is not None:
             copies[6 + before].wait_send()
 
-        def body(start, size):
-            product = contract_columns(
-                left[step], weights[pl.ds(start, size), first : first + left.shape[2]]
-            )
-            kept[:, pl.ds(start, size)] = product[:half]
-            slot[:, pl.ds(start, size)] = product[half:].astype(bf16)
-
-        in_columns(width, body)
+        def part(rows, start, size):
+            right = weights[pl.ds(start, size), first : first + left.shape[2]]
+            return contract_columns(left[step, rows], right)
+
+        def give(start, size):
+            slot[:, pl.ds(start, size)] = part(pl.ds(half, half), start, size).astype(bf16)
+
+        def keep(start, size):
+            kept[:, pl.ds(start, size)] = part(pl.ds(0, half), start, size)
+
+        in_columns(width, give)
         copies[6 + step].start()
+        in_columns(width, keep)
+
+    def scatter_rest(copies, step):
+        kept = (total, waiting, back_sum, back_sum)[step]
         copies[6 + step].wait_recv()
         summed = kept[...] + core_take[step].astype(f32)
         if step < 2:
@@ -728,28 +791,28 @@
     for step in (3, 2, 1, 0):
         loads[1 + step].wait()
 
-        def activate(j, carry):
-            at = pl.multiple_of(j * 256, 256)
-            lin = jnp.dot(
-                rows[step].reshape(step_rows, width),
-                weights[:, pl.ds(at, 256)],
-                preferred_element_type=f32,
+        def activate(start, size):
+            def lin(first):
+                return jnp.dot(
+                    rows[step].reshape(step_rows, width),
+                    weights[:, pl.ds(pl.multiple_of(first + start, 128), size)],
+                    preferred_element_type=f32,
+                )
+
+            gate, up = lin(0), lin(hid)
+            square = gate * gate
+            chance = 0.5 + 0.5 * jnp.tanh(gate * (GELU_SCALE + GELU_SCALE * 0.044715 * square))
+            gelu = gate * chance
+            slope = chance + gelu * (1.0 - chance) * (
+                2 * GELU_SCALE + 6 * GELU_SCALE * 0.044715 * square
             )
-            gate, up = lin[:, :128], lin[:, 128:]
-            square = gate * gate
-            curve = jnp.tanh(GELU_SCALE * gate * (1.0 + 0.044715 * square))
-            gelu = 0.5 * gate * (1.0 + curve)
-            slope = 0.5 * (1.0 + curve) + 0.5 * GELU_SCALE * gate * (1.0 - curve * curve) * (
-                1.0 + 3 * 0.044715 * square
-            )
-            at_half = pl.multiple_of(j * 128, 128)
-            hidden[step, :, pl.ds(at_half, 128)] = (gelu * up).astype(bf16)
-            pair[step, :, pl.ds(at, 128)] = (slope * up).astype(bf16)
-            pair[step, :, pl.ds(pl.multiple_of(at + 128, 128), 128)] = gelu.astype(bf16)
-            return carry
-
-        lax.fori_loop(0, hid // 128, activate, 0)
+            hidden[step, :, pl.ds(start, size)] = (gelu * up).astype(bf16)
+            pair[step, :, pl.ds(start, size)] = (slope * up).astype(bf16)
+            pair[step, :, pl.ds(pl.multiple_of(hid + start, 128), size)] = gelu.astype(bf16)
+
+        in_columns(hid, activate)
         scatter_step(scatter, step, step + 2 if step < 2 else None, hidden, 2 * hid)
+        scatter_rest(scatter, step)
         if step == 1:
             scatter_end(scatter)
     scatter_wait(scatter)
@@ -761,7 +824,7 @@
         scale = lax.rsqrt(jnp.mean(raw * raw, axis=1, keepdims=True) + norm_eps)
         normal = raw * scale
         result[at] = (middle[at] + normal * gain[...]).astype(bf16)
-        cotangents = cotangent[at].astype(f32)
+        cotangents = cotangent[pl.ds(pl.multiple_of(core * half + first, 64), size)].astype(f32)
         scaled = cotangents * gain[...]
         inner = jnp.mean(raw * scaled, axis=1, keepdims=True)
         back = scale * scaled - raw * (scale * scale * scale * inner)
@@ -769,6 +832,14 @@
         return gain_total + jnp.sum(cotangents * normal, axis=0, keepdims=True)
 
     gain_sum[...] = in_rows(half, norm_rows, jnp.zeros((1, width), f32))
+
+    def result_rows(place):
+        return result_out.at[pl.ds(pl.multiple_of(place * half, 64), half)]
+
+    own_result = pltpu.make_async_copy(result, result_rows(core), out_sem.at[2])
+    far_result = remote(result, result_rows(core), 30, core_dev)
+    own_result.start()
+    far_result.start()
 
     gather = gather_copies(remote, grads, 10)
     scatter = scatter_copies(20)
@@ -781,14 +852,16 @@
                 weights[:, pl.ds(pl.multiple_of(2 * hid + start, 128), size)],
                 preferred_element_type=f32,
             )
-            for tile in range(size // 128):
-                piece = hidden_grad[:, tile * 128 : (tile + 1) * 128]
-                for side in range(2):
-                    at = pl.ds(pl.multiple_of(2 * start + (2 * tile + side) * 128, 128), 128)
-                    pair[step, :, at] = (pair[step, :, at].astype(f32) * piece).astype(bf16)
+            hidden_grad = hidden_grad.astype(bf16)
+            for first in (0, hid):
+                at = pl.ds(pl.multiple_of(first + start, 128), size)
+                pair[step, :, at] = pair[step, :, at] * hidden_grad
 
         in_columns(hid, unfold)
+        if step:
+            scatter_rest(scatter, step - 1)
         scatter_step(scatter, step, step - 2 if step >= 2 else None, pair, 0)
+    scatter_rest(scatter, 3)
     sent(gather)
 
     def weigh(first, right):
@@ -821,9 +894,12 @@
     sent(scatter[:6] + scatter[8:])
     down_out.wait()
     gate_out.wait()
-
-
-def mlp_call(rows, middle, cotangent, gain, weights):
+    own_result.wait()
+    far_result.wait_send()
+    remote(result, result_rows(1 - core), 30, core_dev).wait_recv()
+
+
+def mlp_call(rows, middle, cotangent, gain_rows, weights):
     half, width = middle.shape
     hid = weights.shape[1] // 3
     count = 8 * half
@@ -833,14 +909,15 @@
     return pl.pallas_call(
         mlp_kernel,
         out_shape=(
-            jax.ShapeDtypeStruct((half, width), bf16),
+            jax.ShapeDtypeStruct(cotangent.shape, bf16),
             jax.ShapeDtypeStruct((half, width), f32),
             jax.ShapeDtypeStruct((1, width), f32),
             jax.ShapeDtypeStruct((width, 3 * hid), bf16),
         ),
         in_specs=[anywhere, vmem, vmem, vmem, anywhere],
-        out_specs=(vmem, vmem, vmem, anywhere),
+        out_specs=(anywhere, vmem, vmem, anywhere),
         scratch_shapes=[
+            pltpu.VMEM((half, width), bf16),
             pltpu.VMEM((4, 2, half, width), bf16),
             pltpu.VMEM((4, 2, half, width), bf16),
             pltpu.VMEM((4, 2 * half, hid), bf16),
@@ -852,10 +929,10 @@
             pltpu.VMEM((4, half, width), bf16),
             pltpu.VMEM((3, half, width), bf16),
             pltpu.VMEM((3, half, width), bf16),
-            pltpu.SemaphoreType.DMA((30,)),
-            pltpu.SemaphoreType.DMA((30,)),
+            pltpu.SemaphoreType.DMA((31,)),
+            pltpu.SemaphoreType.DMA((31,)),
             pltpu.SemaphoreType.DMA((5,)),
-            pltpu.SemaphoreType.DMA((2,)),
+            pltpu.SemaphoreType.DMA((3,)),
         ],
         compiler_params=pltpu.CompilerParams(
             collective_id=0, has_side_effects=True, vmem_limit_bytes=63 * 2**20
@@ -864,7 +941,7 @@
             flops=2 * count * width * hid * 9, bytes_accessed=30 * 2**20, transcendentals=count * hid
         ),
         name="feed_forward",
-    )(rows, middle, cotangent, gain, weights)
+    )(rows, middle, cotangent, gain_rows, weights)
 
 
 def norm_back(values, gains, grads):
@@ -898,9 +975,12 @@
     attended_in,
     log_total,
     mlp_grads,
+    input_whole,
+    gate_reduced,
+    down_reduced,
+    attn_reduced,
+    keyval_reduced,
     input_out,
-    mlp_reduced,
-    attn_reduced,
     line_slots,
     attn_grads,
     attn_blocks,
@@ -1059,13 +1139,25 @@
         for way in range(2):
             pl.when(not_first(way) & has_goal(way, far))(functools.partial(pass_on, way, far, k))
 
+    parts = ((gate_reduced, pl.ds(0, 2 * hid)), (down_reduced, pl.ds(2 * hid, hid)))
+
     def to_owner(k, came=False):
         place = plane[k][1] if came else ctx
-        return remote(
-            line_slots.at[k], mlp_reduced.at[place], plane_send_sem.at[k], plane_recv_sem.at[k], plane[k]
-        )
-
-    own_done = pltpu.make_async_copy(line_slots.at[0], mlp_reduced.at[ctx], plane_send_sem.at[0])
+        return [
+            remote(
+                line_slots.at[k, :, columns],
+                target.at[place],
+                plane_send_sem.at[2 * k + index],
+                plane_recv_sem.at[2 * k + index],
+                plane[k],
+            )
+            for index, (target, columns) in enumerate(parts)
+        ]
+
+    own_done = [
+        pltpu.make_async_copy(line_slots.at[0, :, columns], target.at[ctx], plane_send_sem.at[index])
+        for index, (target, columns) in enumerate(parts)
+    ]
 
     def mlp_last(k):
         if line > 1:
@@ -1077,10 +1169,8 @@
                 arrived = line_slots[slot_of(way, 1, k)].astype(f32)
                 total = total + jnp.where(not_first(way), arrived, 0.0)
         line_slots[k] = total.astype(bf16)
-        if k:
-            to_owner(k).start()
-        else:
-            own_done.start()
+        for copy in to_owner(k) if k else own_done:
+            copy.start()
 
     events = [
         functools.partial(mlp_step, far, k) for far in range(line - 2, 0, -1) for k in turn
@@ -1100,10 +1190,11 @@
     def norms(first, size, carry):
         at = pl.ds(first, size)
         part, gain_two = norm_back(loaded(0, first, size), gain_rows[2:3], loaded(2, first, size))
-        middle_grad = cotangent[at].astype(f32) + part
+        whole_at = pl.ds(pl.multiple_of(core * half + first, 64), size)
+        middle_grad = cotangent[whole_at].astype(f32) + part
         input_out[at] = middle_grad
         grad, gain_one = norm_back(loaded(1, first, size), gain_rows[1:2], middle_grad)
-        branch_low[pl.ds(pl.multiple_of(core * half + first, 64), size)] = grad.astype(bf16)
+        branch_low[whole_at] = grad.astype(bf16)
         return (
             carry[0] + jnp.sum(gain_one, axis=0, keepdims=True),
             carry[1] + jnp.sum(gain_two, axis=0, keepdims=True),
@@ -1253,6 +1344,19 @@
         return carry + jnp.sum(gain, axis=0, keepdims=True)
 
     small_rows[0:1] = in_rows(half, finish, nothing)
+
+    def input_rows(place):
+        return input_whole.at[pl.ds(pl.multiple_of(place * half, 64), half)]
+
+    own_input = pltpu.make_async_copy(input_out, input_rows(core), load_sem.at[0])
+    own_input.start()
+
+    def far_input(place):
+        return remote(
+            input_out, input_rows(place), core_send_sem.at[5], core_recv_sem.at[5], core_dev
+        )
+
+    far_input(core).start()
 
     row_of = lax.broadcasted_iota(jnp.int32, (width, HD), 0)
     head_of = lax.broadcasted_iota(jnp.int32, (width, HD), 1)
@@ -1340,11 +1444,30 @@
             arrived = attn_slots[way * line + 1].astype(f32)
             total = total + jnp.where(not_first(way), arrived, 0.0)
         attn_reduced[0] = total.astype(bf16)
+        columns = attn_reduced.at[0, :, pl.ds(2 * HD, HD)]
+        own_keyval = pltpu.make_async_copy(columns, keyval_reduced.at[core], load_sem.at[1])
+        own_keyval.start()
+
+        def far_keyval(place):
+            return remote(
+                columns, keyval_reduced.at[place], core_send_sem.at[6], core_recv_sem.at[6], core_dev
+            )
+
+        far_keyval(core).start()
+        far_keyval(core).wait_send()
+        far_keyval(1 - core).wait_recv()
+        own_keyval.wait()
 
     for k in (1, 2, 3):
-        to_owner(k, True).wait_recv()
-        to_owner(k).wait_send()
-    own_done.wait()
+        for copy in to_owner(k, True):
+            copy.wait_recv()
+        for copy in to_owner(k):
+            copy.wait_send()
+    for copy in own_done:
+        copy.wait()
+    own_input.wait()
+    far_input(core).wait_send()
+    far_input(1 - core).wait_recv()
     halves(False).wait_send()
     to_core.wait_send()
     pl.when(ctx > 0)(to_past.wait_send)
@@ -1388,16 +1511,19 @@
     return pl.pallas_call(
         functools.partial(retreat_kernel, n_dp, line, owned_heads),
         out_shape=(
-            jax.ShapeDtypeStruct((half, width), f32),
-            jax.ShapeDtypeStruct((4, owned, 3 * hid), bf16),
+            jax.ShapeDtypeStruct((row_count, width), f32),
+            jax.ShapeDtypeStruct((4, owned, 2 * hid), bf16),
+            jax.ShapeDtypeStruct((4, owned, hid), bf16),
             jax.ShapeDtypeStruct((n_dp if line == 1 else 1, owned, attn_cols), bf16),
+            jax.ShapeDtypeStruct((2, owned, HD), bf16),
         ),
         in_specs=[
             anywhere if index < 5 or 11 <= index <= 16 or index == 18 else vmem
             for index in range(len(arrays))
         ],
-        out_specs=(vmem, anywhere, vmem),
+        out_specs=(anywhere, anywhere, anywhere, vmem, anywhere),
         scratch_shapes=[
+            pltpu.VMEM((half, width), f32),
             pltpu.VMEM((max(8 * (line - 1), 4), owned, 3 * hid), bf16),
             pltpu.VMEM((max(width, 3 * half), attn_cols), f32),
             pltpu.VMEM((blocks, owned, attn_cols), bf16),
@@ -1419,14 +1545,14 @@
             pltpu.VMEM((8, width), f32),
             dma((8 * line,)),
             dma((8 * line,)),
-            dma((4,)),
-            dma((4,)),
+            dma((8,)),
+            dma((8,)),
             dma((4 * n_dp,)),
             dma((4 * n_dp,)),
             dma((2 * line,)),
             dma((2 * line,)),
-            dma((5,)),
-            dma((5,)),
+            dma((7,)),
+            dma((7,)),
             dma((12,)),
             pltpu.VMEM(mlp_grads.shape, bf16),
         ]
@@ -1442,6 +1568,65 @@
         ),
         name="retreat",
     )(*arrays)
+
+
+def update_call(wide, passed, small_grads, attn_grads, keyval_grads, gate_grads, down_grads, *states):
+    owned = states[0].shape[0]
+    cols = states[0].shape[1]
+    blocks = down_grads.shape[0]
+
+    def whole(array):
+        return pl.BlockSpec(array.shape, lambda i: (0,) * array.ndim)
+
+    def step(state, new, gradient, rate, decay=decay_rate):
+        results = adam_step(
+            state[0][...], gradient.astype(jnp.float32), state[1][...], state[2][...], rate, decay
+        )
+        for target, result in zip(new, results):
+            target[...] = result
+
+    def kernel(first_in, second_in, small_ref, attn_ref, keyval_ref, gate_ref, down_ref, *refs):
+        olds, news, first_out, second_out = refs[:21], refs[21:42], *refs[42:]
+        first_out[...] = first_in[...]
+        second_out[...] = second_in[...]
+        step(olds[9:12], news[9:12], gate_ref[...], D ** (-0.5))
+        step(olds[12:15], news[12:15], down_ref[0], FF ** (-0.5))
+
+        @pl.when(pl.program_id(0) == 0)
+        def _():
+            step(olds[0:3], news[0:3], attn_ref[0, :, 0:cols], D ** (-0.5))
+            keyval = jnp.concatenate([keyval_ref[0], keyval_ref[1]], axis=1)
+            step(olds[3:6], news[3:6], keyval, D ** (-0.5))
+            output = attn_ref[0, :, cols + HD : 2 * cols + HD]
+            step(olds[6:9], news[6:9], output, (HQ * HD) ** (-0.5))
+            step(olds[15:18], news[15:18], small_ref[0:4], 0.5, 0.0)
+            step(olds[18:21], news[18:21], small_ref[4:6, 0 : olds[18].shape[1]], 0.5, 0.0)
+
+    gate_block = pl.BlockSpec((owned, 2, wide), lambda i: (0, 0, i))
+    down_block = pl.BlockSpec((owned, wide), lambda i: (0, i))
+    state_blocks = [whole(array) for array in states[:9]] + [gate_block] * 3 + [down_block] * 3
+    state_blocks += [whole(array) for array in states[15:]]
+    passed_blocks = [
+        pl.BlockSpec((array.shape[0] // blocks, array.shape[1]), lambda i: (i, 0))
+        for array in passed
+    ]
+    return pl.pallas_call(
+        kernel,
+        grid=(blocks,),
+        in_specs=[
+            *passed_blocks,
+            whole(small_grads),
+            whole(attn_grads),
+            whole(keyval_grads),
+            gate_block,
+            pl.BlockSpec((1, owned, wide), lambda i: (i, 0, 0)),
+        ]
+        + state_blocks,
+        out_specs=tuple(state_blocks + passed_blocks),
+        out_shape=tuple(jax.ShapeDtypeStruct(array.shape, array.dtype) for array in states + passed),
+        compiler_params=pltpu.CompilerParams(vmem_limit_bytes=63 * 2**20 + 900 * 2**10),
+        name="update",
+    )(*passed, small_grads, attn_grads, keyval_grads, gate_grads, down_grads, *states)
 
 
 def on_device(
@@ -1497,15 +1682,10 @@
 
     def in_parts(array):
         padded = jnp.pad(array.astype(bf16), ((0, 0), (0, n_ctx * wide - half_ff)))
-        return padded.reshape(owned, n_ctx, wide // 128, 128)
-
-    gate_parts = jnp.stack([in_parts(gate_up[:, side]) for side in range(2)], axis=3)
+        return padded.reshape(owned, n_ctx, wide)
+
     mlp_pack = jnp.concatenate(
-        [
-            gate_parts.reshape(owned, n_ctx, 2 * wide),
-            in_parts(down_weight).reshape(owned, n_ctx, wide),
-        ],
-        axis=2,
+        [in_parts(gate_up[:, 0]), in_parts(gate_up[:, 1]), in_parts(down_weight)], axis=2
     )
     mlp_pack = jnp.moveaxis(mlp_pack, 1, 0)
 
@@ -1516,35 +1696,28 @@
     lowest = jnp.maximum(row_index - query_position + behind, row_index + 1)[:, None]
     (
         mlp_full,
-        attn_full,
         gain_rows,
         head_rows,
+        log_total,
+        attn_full,
         normed_one,
         lin,
         query_rot,
         keyval_all,
         attended_low,
-        log_total,
         branch_raw,
         middle,
         group_rows,
     ) = attend_call(
         n_dp, owned_heads, behind, tokens, query_cosine, query_sine, lowest, attn_pack, mlp_pack
     )
-    cotangent_half = half_of(out_cotangent, 0)
-    (
-        result_half,
-        normed_two_grad,
-        gain_three_part,
-        mlp_grads,
-    ) = mlp_call(
+    result, normed_two_grad, gain_three_part, mlp_grads = mlp_call(
         group_rows,
         middle,
-        cotangent_half,
-        gain_rows[3:4],
+        out_cotangent,
+        gain_rows,
         mlp_full.reshape(n_dp * n_ctx * owned, 3 * wide),
     )
-    result = core_ordered(result_half, from_partner(result_half, "tensor", 1))
 
     line = n_dp if n_dp <= 4 else 1
 
@@ -1552,14 +1725,14 @@
     if line == 1:
         mlp_grads = lax.psum_scatter(mlp_grads, "dp", scatter_dimension=0, tiled=True)
     mlp_grads = mlp_grads.reshape(line * n_ctx, owned, 3 * wide)
-    input_half, mlp_reduced, attn_reduced = retreat_call(
+    input_grad, gate_arrived, down_arrived, attn_reduced, keyval_both = retreat_call(
         n_dp,
         line,
         owned_heads,
         normed_two_grad,
         middle,
         branch_raw,
-        cotangent_half,
+        out_cotangent,
         tokens,
         query_cosine,
         query_sine,
@@ -1576,56 +1749,72 @@
         log_total,
         mlp_grads,
     )
-    input_grad = core_ordered(input_half, from_partner(input_half, "tensor", 1))
-
     if line == 1:
         attn_reduced = lax.psum_scatter(attn_reduced, "dp", scatter_dimension=0, tiled=True)
-    attn_reduced = attn_reduced[0].astype(f32)
-
-    def from_parts(tiles):
-        return jnp.moveaxis(tiles, 0, 1).reshape(owned, n_ctx * wide)[:, :half_ff].astype(f32)
-
-    gate_arrived = mlp_reduced[:, :, : 2 * wide].reshape(n_ctx, owned, wide // 128, 2, 128)
-    gate_reduced = jnp.stack(
-        [from_parts(gate_arrived[:, :, :, side].reshape(n_ctx, owned, wide)) for side in range(2)],
-        axis=1,
+        keyval_half = attn_reduced[0, :, cols : cols + HD]
+        first, second = jnp.where(core_first, 0, 1), jnp.where(core_first, 1, 0)
+        keyval_both = jnp.stack([keyval_half, lax.ppermute(keyval_half, "tensor", [(0, 1), (1, 0)])])
+        keyval_both = jnp.stack([keyval_both[first], keyval_both[second]])
+    gate_reduced = gate_arrived.reshape(n_ctx, owned, 2, wide)
+    gate_reduced = gate_reduced.transpose(1, 2, 0, 3).reshape(owned, 2, n_ctx * wide)
+    gate_reduced = lax.optimization_barrier(gate_reduced)
+    (
+        query_new,
+        query_first_new,
+        query_second_new,
+        keyval_new,
+        keyval_first_new,
+        keyval_second_new,
+        output_new,
+        output_first_new,
+        output_second_new,
+        gate_new,
+        gate_first_new,
+        gate_second_new,
+        down_new,
+        down_first_new,
+        down_second_new,
+        *gains_updated,
+        result,
+        input_grad,
+    ) = update_call(
+        wide,
+        (result, input_grad),
+        attn_reduced[0, :, 2 * cols + HD :].astype(f32).T,
+        attn_reduced,
+        keyval_both,
+        gate_reduced,
+        down_arrived,
+        query_weight,
+        query_first,
+        query_second,
+        keyval_weight,
+        keyval_first,
+        keyval_second,
+        output_weight,
+        output_first,
+        output_second,
+        gate_up,
+        gate_first,
+        gate_second,
+        down_weight,
+        down_first,
+        down_second,
+        norm_gains.T,
+        gain_first.T,
+        gain_second.T,
+        head_gains.T,
+        head_first.T,
+        head_second.T,
     )
-    down_reduced = from_parts(mlp_reduced[:, :, 2 * wide :])
-    query_reduced = attn_reduced[:, :cols]
-    keyval_half = attn_reduced[:, cols : cols + HD]
-    output_reduced = attn_reduced[:, cols + HD : 2 * cols + HD]
-    keyval_not = from_partner(keyval_half, "tensor", 1)
-    keyval_reduced = jnp.concatenate(
-        [
-            jnp.where(core_first, keyval_half, keyval_not),
-            jnp.where(core_first, keyval_not, keyval_half),
-        ],
-        axis=1,
-    )
-    gains_reduced = attn_reduced[:, 2 * cols + HD : 2 * cols + HD + 4]
-    heads_reduced = attn_reduced[:owned_heads, 2 * cols + HD + 4 : 2 * cols + HD + 6]
-
-    gains_new, gain_first_new, gain_second_new = adam_step(
-        norm_gains, gains_reduced, gain_first, gain_second, 0.5, 0.0
-    )
-    heads_new, head_first_new, head_second_new = adam_step(
-        head_gains, heads_reduced, head_first, head_second, 0.5, 0.0
-    )
-    query_new, query_first_new, query_second_new = adam_step(
-        query_weight, query_reduced, query_first, query_second, D ** (-0.5), decay_rate
-    )
-    keyval_new, keyval_first_new, keyval_second_new = adam_step(
-        keyval_weight, keyval_reduced, keyval_first, keyval_second, D ** (-0.5), decay_rate
-    )
-    output_new, output_first_new, output_second_new = adam_step(
-        output_weight, output_reduced, output_first, output_second, (HQ * HD) ** (-0.5), decay_rate
-    )
-    gate_new, gate_first_new, gate_second_new = adam_step(
-        gate_up, gate_reduced, gate_first, gate_second, D ** (-0.5), decay_rate
-    )
-    down_new, down_first_new, down_second_new = adam_step(
-        down_weight, down_reduced, down_first, down_second, FF ** (-0.5), decay_rate
-    )
+    (
+        gains_new,
+        gain_first_new,
+        gain_second_new,
+        heads_new,
+        head_first_new,
+        head_second_new,
+    ) = (new.T for new in gains_updated)
     return (
         result,
         input_grad,

time: 486 us -> 404 us (0.83)
  local copies, waits for them, and re-layouts: 39.1 us -> 6.72 us
  Pallas kernels: 405 us -> 380 us
  other arithmetic: 28.7 us -> 10.9 us
    unnamed x71 -> x5, local copies, waits for them, and re-layouts: 19.4 us -> 0.12 us
    pallas_call x1, Pallas kernels: 138 us -> 119 us  [attend_call(): pl.pallas_call(functools.partial(attend_kernel, n_dp, owned_heads), out_s...]
    pallas_call x1, Pallas kernels: 138 us -> 123 us  [retreat_call(): pl.pallas_call(functools.partial(retreat_kernel, n_dp, line, owned_heads)...]
    slice x4 -> x0, local copies, waits for them, and re-layouts: 8.84 us -> none  [the longest x1 5.51 us: on_device(): gate_arrived[:, :, :, side].reshape(n_ctx, owned, wide)]
    pallas_call x1 -> x2, Pallas kernels: 130 us -> 138 us  [the longest x1 125 us: mlp_call(): pl.pallas_call(mlp_kernel, out_shape=(jax.ShapeDtypeStruct(cotangent.shap...]
    sub x6 -> x0, other arithmetic: 7.57 us -> none  [adam_step(): weight_value - step_rate * (update + decay_factor * weight_value)]
  transfers between devices with their start and end apart: 3 -> 0, of which waited for: 0 -> 0; matrix products, arithmetic and copies ran while one was open for 8% -> 0% of each run, Pallas kernels for 0% -> 0%
where the time goes in v3:
time: 404 us; the launch traced here: 398 us
  Pallas kernels  380 us (94%)
  other arithmetic  10.9 us (3%)
  local copies, waits for them, and re-layouts  6.72 us (2%)
    pallas_call x1, Pallas kernels, mlp_call(): pl.pallas_call(mlp_kernel, out_shape=(jax.ShapeDtypeStruct(cotangent.shap...  125 us
    pallas_call x1, Pallas kernels, retreat_call(): pl.pallas_call(functools.partial(retreat_kernel, n_dp, line, owned_heads)...  123 us
    pallas_call x1, Pallas kernels, attend_call(): pl.pallas_call(functools.partial(attend_kernel, n_dp, owned_heads), out_s...  119 us
    pallas_call x1, Pallas kernels, update_call(): pl.pallas_call(kernel, grid=(blocks,), in_specs=[*passed_blocks, whole(sm...  12.9 us

profile of v3, /device:TPU:9, one launch (start us, length us, event | category | flops | bytes accessed | tf_op | source)
XLA Modules:
  0.0 398.5 jit_solution(16043956635640118875)
XLA Ops:
  0.7 0.0 copy-start.1
  0.7 0.8 select_reduce_fusion.1
  1.5 0.7 fusion.7
  2.2 0.7 convert.15
  2.8 0.7 convert.14
  3.6 0.1 convert_reduce_fusion
  3.6 0.1 select_reduce_fusion
  3.7 0.1 copy.78
  3.9 0.9 dynamic-slice_convert_fusion
  4.7 0.9 convert_element_type.45
  5.7 0.9 convert_element_type.47
  6.6 0.0 copy-start
  6.6 0.7 fusion.4.attn_pack
  7.3 0.9 fusion.3.lowest
  8.2 0.0 copy-done.1
  8.2 0.1 convert_element_type.50
  8.3 2.5 multiply_sine_fusion
  10.8 0.0 copy-done
  10.8 0.1 copy.93
  11.0 0.1 slice_bitcast_fusion.1
  11.2 0.1 copy_bitcast_fusion.1
  11.3 1.2 maximum_bitcast_fusion.mlp_pack
  12.5 118.9 %attend.1 = (bf16[16,72,2688]{2,1,0:T(8,128)(2,1)}, f32[8,1152]{1,0:T(8,128)}, f32[8,256]{1,0:T(8,128)}, f32[2,768,1]{2,1,0:T(8,128)}, bf16[1152,1408]{1,0:T(8,1...) custom-call(bf16[768,1152]{1,0:T(8,128)(2,1)} %tokens_in.1, ...), custom_call_target="tpu_custom_call" | custom-call | flops 4000000000 | bytes 31457280 | tf_op jit(solution)/shard_map/attend/pallas_call | solution.py:612
  131.4 124.9 %feed_forward.1 = (bf16[768,1152]{1,0:T(8,128)(2,1)}, f32[384,1152]{1,0:T(8,128)}, f32[1,1152]{1,0:T(1,128)}, bf16[1152,2688]{1,0:T(8,128)(2,1)}) custom-call(bf16[4,2,384,1152]{3,2,1,0:T(8,128)(2,1)} %get-tuple-element.68.rows_in, f32[384,1152]{1,0:T(8,128)} %get-tuple-element.69.middle, bf16[768,1152]{1,0:T(8,128)(2,1)} %cotangent_in.1, ...), custom_call_target="tpu_custom_call" | custom-call | flops 57076088832 | bytes 31457280 | tf_op jit(solution)/shard_map/feed_forward/pallas_call | solution.py:909
  256.4 122.8 %retreat.1 = (f32[768,1152]{1,0:T(8,128)}, bf16[4,72,1792]{2,1,0:T(8,128)(2,1)}, bf16[4,72,896]{2,1,0:T(8,128)(2,1)}, bf16[1,72,1408]{2,1,0:T(8,128)(2,1)}, bf16[2,72,256]{2,1,0:T(8,128)(2,1)}) custom-call(f32[384,1152]{1,0:T(8,128)} %get-tuple-element.73.back_sum, f32[384,1152]{1,0:T(8,128)} %get-tuple-element.69.middle, ...), custom_call_target="tpu_custom_call" | custom-call | flops 10000000000 | bytes 41943040 | tf_op jit(solution)/shard_map/retreat/pallas_call | solution.py:1511
  379.2 1.1 copy.83
  380.3 0.6 convert_bitcast_fusion.small_ref
  380.9 2.4 reshape.121
  383.3 0.4 copy.94
  383.7 1.3 reshape.122.gate_ref
  385.1 12.9 %update.1 = (f32[72,512]{1,0:T(8,128)}, f32[72,512]{1,0:T(8,128)}, f32[72,512]{1,0:T(8,128)}, f32[72,512]{1,0:T(8,128)}, f32[72,512]{1,0:T(8,128)}, /*index=5*/f...) custom-call(bf16[768,1152]{1,0:T(8,128)(2,1)} %get-tuple-element.72., ...), custom_call_target="tpu_custom_call" | custom-call | tf_op jit(solution)/shard_map/update/pallas_call | solution.py:1613
  (8 shorter events, 0.2 us)
Async XLA Ops:
  0.7 7.6 %copy-start.1 = (f32[72,3456]{1,0:T(8,128)S(1)}, f32[72,3456]{1,0:T(8,128)}, u32[]{:S(2)}) copy-start(f32[72,3456]{1,0:T(8,128)} %refs_12_.1) | copy-start | bytes 2985988
  6.6 4.2 %copy-start = (f32[72,2,3456]{2,1,0:T(2,128)S(1)}, f32[72,2,3456]{2,1,0:T(2,128)}, u32[]{:S(2)}) copy-start(f32[72,2,3456]{2,1,0:T(2,128)} %refs_9_.1) | copy-start | bytes 5971972

commit v4 on v3

--- a/solution.py
+++ b/solution.py
@@ -29,25 +29,6 @@
 def half_of(array, dim):
     size = array.shape[dim] // 2
     return lax.dynamic_slice_in_dim(array, lax.axis_index("tensor") * size, size, axis=dim)
-
-
-def token_layout(lengths, places):
-    count = lengths.shape[0]
-    before = jnp.arange(count)[:, None] <= jnp.arange(count)[None, :]
-    stop_at = jnp.sum(jnp.where(before, lengths[:, None], 0), axis=0)
-    start_at = stop_at - lengths
-    segment = jnp.sum((places[:, None] >= stop_at[None, :]).astype(jnp.int32), axis=1)
-    owned_by = segment[:, None] == jnp.arange(lengths.shape[0], dtype=jnp.int32)[None, :]
-    seg_begin = jnp.sum(jnp.where(owned_by, start_at[None, :], 0), axis=1)
-    return (segment, places - seg_begin)
-
-
-def rope_tables(position):
-    half_dim = HD // 2
-    exponent = jnp.arange(half_dim, dtype=jnp.float32) * (2.0 / HD)
-    inverse = jnp.power(jnp.float32(rope_base), -exponent)
-    angles = position.astype(jnp.float32)[:, None] * inverse[None, :]
-    return (jnp.cos(angles), jnp.sin(angles))
 
 
 def contract_rows(left_side, right_side):
@@ -173,16 +154,18 @@
 def attend_kernel(
     n_dp,
     owned_heads,
-    tokens,
-    cosine,
-    sine,
-    lowest,
+    tokens_in,
+    lengths,
+    inverse,
     attn_pack,
     mlp_pack,
     mlp_full,
     gain_rows,
     head_rows,
     log_total,
+    cosine,
+    sine,
+    lowest,
     attn_full_out,
     normed_out_out,
     lin_out,
@@ -221,6 +204,7 @@
     branch_out,
     middle_out,
     out_sem,
+    tokens,
 ):
     dp, ctx, core = places()
     x_dev, y_dev, far_dev, core_dev = plane_partners()
@@ -319,6 +303,7 @@
         )
 
     own_attn = pltpu.make_async_copy(attn_pack, slots.at[dp * 4 + ctx], own_sem.at[0])
+    own_tokens = pltpu.make_async_copy(tokens_in, tokens, own_sem.at[2])
     own_mlp = pltpu.make_async_copy(mlp_pack.at[ctx], mlp_full.at[dp * 4 + ctx], own_sem.at[1])
     own_attn.start()
     own_mlp.start()
@@ -338,6 +323,25 @@
 
     for k in (1, 2):
         mlp_plane(k).start()
+
+    own_tokens.start()
+
+    def place_rows(first, size, carry):
+        at = pl.ds(first, size)
+        row = first + lax.broadcasted_iota(jnp.int32, (size, 1), 0)
+        position = ctx * row_count + row
+        stop, begin = 0, jnp.zeros((size, 1), jnp.int32)
+        for index in range(lengths.shape[1]):
+            stop = stop + lengths[0, index]
+            begin = begin + jnp.where(position >= stop, lengths[0, index], 0)
+        position = position - begin
+        lowest[at] = jnp.maximum(row - position + behind, row + 1)
+        angles = position.astype(f32) * inverse[...]
+        cosine[at] = jnp.cos(angles)
+        sine[at] = jnp.sin(angles)
+        return carry
+
+    in_rows(row_count, place_rows, 0)
 
     def came(way, step):
         attn_came(way, step).wait_recv()
@@ -429,6 +433,7 @@
         normed_out[at] = (values * scale_of(values) * gain_rows[0:1]).astype(bf16)
         return carry
 
+    own_tokens.wait()
     in_rows(row_count, normalize, 0)
 
     def project(start, size):
@@ -596,7 +601,7 @@
         where_held(way, step, left)
 
 
-def attend_call(n_dp, owned_heads, behind, tokens, cosine, sine, lowest, attn_pack, mlp_pack):
+def attend_call(n_dp, owned_heads, behind, tokens, lengths, inverse, attn_pack, mlp_pack):
     row_count, width = tokens.shape
     half = row_count // 2
     owned, attn_cols = attn_pack.shape
@@ -616,6 +621,9 @@
             array(f32, 8, width),
             array(f32, 8, HD),
             array(f32, 2, row_count, 1),
+            array(f32, row_count, HD // 2),
+            array(f32, row_count, HD // 2),
+            array(jnp.int32, row_count, 1),
             array(bf16, width, attn_cols),
             array(bf16, row_count, width),
             array(f32, row_count, 3 * HD),
@@ -626,8 +634,14 @@
             array(f32, half, width),
             array(bf16, 4, 2, half, width),
         ),
-        in_specs=[vmem] * 4 + [anywhere] * 2,
-        out_specs=(anywhere, vmem, vmem, vmem) + (anywhere,) * 9,
+        in_specs=[
+            anywhere,
+            pl.BlockSpec(memory_space=pltpu.SMEM),
+            vmem,
+            anywhere,
+            anywhere,
+        ],
+        out_specs=(anywhere,) + (vmem,) * 6 + (anywhere,) * 9,
         scratch_shapes=[
             pltpu.VMEM((blocks, owned, attn_cols), bf16),
             pltpu.VMEM((width, attn_cols), f32),
@@ -635,7 +649,7 @@
             pltpu.VMEM((row_count, width), f32),
             pltpu.VMEM((half, width), bf16),
             pltpu.VMEM((half, width), bf16),
-            dma((2,)),
+            dma((3,)),
             dma((4,)),
             dma((4,)),
             dma((8 * n_dp,)),
@@ -658,6 +672,7 @@
             pltpu.VMEM((half, width), f32),
             pltpu.VMEM((half, width), f32),
             dma((8,)),
+            pltpu.VMEM((row_count, width), bf16),
         ],
         compiler_params=pltpu.CompilerParams(
             collective_id=1, has_side_effects=True, vmem_limit_bytes=60 * 2**20
@@ -666,19 +681,22 @@
             flops=4 * 10**9, bytes_accessed=30 * 2**20, transcendentals=2 * 10**6
         ),
         name="attend",
-    )(tokens, cosine, sine, lowest, attn_pack, mlp_pack)
+    )(tokens, lengths, inverse, attn_pack, mlp_pack)
 
 
 def mlp_kernel(
+    n_dp,
+    line,
     rows_in,
-    middle,
-    cotangent,
+    middle_in,
+    cotangent_in,
     gain_rows,
     weights_in,
     result_out,
     back_sum,
     gain_sum,
     weights_out,
+    early,
     result,
     rows,
     grads,
@@ -695,6 +713,8 @@
     recv_sem,
     load_sem,
     out_sem,
+    middle,
+    cotangent,
 ):
     half, width = middle.shape
     h = half // 2
@@ -710,9 +730,13 @@
         pltpu.make_async_copy(rows_in.at[step], rows.at[step], load_sem.at[step])
         for step in range(4)
     ]
-    for load in (loads[0], loads[4], loads[3], loads[2], loads[1]):
+    norm_loads = [
+        pltpu.make_async_copy(middle_in, middle, load_sem.at[5]),
+        pltpu.make_async_copy(cotangent_in, cotangent, load_sem.at[6]),
+    ]
+    for load in [loads[0], loads[4], loads[3], loads[2], loads[1]] + norm_loads:
         load.start()
-    enter(1, False)
+    enter(n_dp, line > 1)
 
     def remote(source, target, index, device):
         return pltpu.make_async_remote_copy(
@@ -817,6 +841,8 @@
             scatter_end(scatter)
     scatter_wait(scatter)
     sent(scatter[:8])
+    for load in norm_loads:
+        load.wait()
 
     def norm_rows(first, size, gain_total):
         at = pl.ds(first, size)
@@ -881,6 +907,25 @@
         return copy
 
     down_out = weigh(2 * hid, hidden)
+
+    dp, ctx, _ = places()
+    last_dp = line - 1
+    group = width // line
+
+    def early_copy(way, index):
+        place = last_dp - index if way == 0 else index
+        first = pl.multiple_of(place * group, 8)
+        device = (dp + 1, ctx, core) if way == 0 else (dp - 1, ctx, core)
+        source = weights.at[pl.ds(first, group), pl.ds(2 * hid, hid)]
+        item = 2 * index + way
+        return remote(source, early.at[item], 31 + item, device)
+
+    def sends_early(way):
+        return dp == 0 if way == 0 else dp == last_dp
+
+    if line > 1:
+        for way, index in early_items(line):
+            pl.when(sends_early(way))(early_copy(way, index).start)
     scatter_end(scatter)
     gate_out = weigh(0, pair)
     scatter_wait(scatter)
@@ -892,6 +937,10 @@
 
     in_rows(half, finish_rows, 0)
     sent(scatter[:6] + scatter[8:])
+    if line > 1:
+        for way, index in early_items(line):
+            pl.when(sends_early(way))(early_copy(way, index).wait_send)
+            pl.when(takes_early(way, dp, last_dp))(early_copy(way, index).wait_recv)
     down_out.wait()
     gate_out.wait()
     own_result.wait()
@@ -899,7 +948,15 @@
     remote(result, result_rows(1 - core), 30, core_dev).wait_recv()
 
 
-def mlp_call(rows, middle, cotangent, gain_rows, weights):
+def early_items(line):
+    return [(way, index) for index in range(min(2, line - 1)) for way in range(2)]
+
+
+def takes_early(way, dp, last_dp):
+    return dp == 1 if way == 0 else dp == last_dp - 1
+
+
+def mlp_call(n_dp, line, rows, middle, cotangent, gain_rows, weights):
     half, width = middle.shape
     hid = weights.shape[1] // 3
     count = 8 * half
@@ -907,15 +964,16 @@
     vmem = pl.BlockSpec(memory_space=pltpu.VMEM)
     anywhere = pl.BlockSpec(memory_space=pl.ANY)
     return pl.pallas_call(
-        mlp_kernel,
+        functools.partial(mlp_kernel, n_dp, line),
         out_shape=(
             jax.ShapeDtypeStruct(cotangent.shape, bf16),
             jax.ShapeDtypeStruct((half, width), f32),
             jax.ShapeDtypeStruct((1, width), f32),
             jax.ShapeDtypeStruct((width, 3 * hid), bf16),
+            jax.ShapeDtypeStruct((max(2, len(early_items(line))), width // line, hid), bf16),
         ),
-        in_specs=[anywhere, vmem, vmem, vmem, anywhere],
-        out_specs=(anywhere, vmem, vmem, anywhere),
+        in_specs=[anywhere, anywhere, anywhere, vmem, anywhere],
+        out_specs=(anywhere, vmem, vmem, anywhere, anywhere),
         scratch_shapes=[
             pltpu.VMEM((half, width), bf16),
             pltpu.VMEM((4, 2, half, width), bf16),
@@ -929,10 +987,12 @@
             pltpu.VMEM((4, half, width), bf16),
             pltpu.VMEM((3, half, width), bf16),
             pltpu.VMEM((3, half, width), bf16),
-            pltpu.SemaphoreType.DMA((31,)),
-            pltpu.SemaphoreType.DMA((31,)),
-            pltpu.SemaphoreType.DMA((5,)),
+            pltpu.SemaphoreType.DMA((35,)),
+            pltpu.SemaphoreType.DMA((35,)),
+            pltpu.SemaphoreType.DMA((7,)),
             pltpu.SemaphoreType.DMA((3,)),
+            pltpu.VMEM((half, width), f32),
+            pltpu.VMEM(cotangent.shape, bf16),
         ],
         compiler_params=pltpu.CompilerParams(
             collective_id=0, has_side_effects=True, vmem_limit_bytes=63 * 2**20
@@ -975,6 +1035,7 @@
     attended_in,
     log_total,
     mlp_grads,
+    early,
     input_whole,
     gate_reduced,
     down_reduced,
@@ -1011,6 +1072,7 @@
     core_send_sem,
     core_recv_sem,
     load_sem,
+    early_sem,
     mlp_own,
     cotangent,
     tokens,
@@ -1031,6 +1093,7 @@
     behind = keyval.shape[1] - row_count
     last_dp = line - 1
     here_dp = dp if line > 1 else 0
+    early_count = len(early_items(line)) // 2
     sources = (
         (cotangent_in, cotangent),
         (attn_full_in, attn_full),
@@ -1091,9 +1154,10 @@
 
     def first_hop(way, far, k):
         slot = slot_of(way, far, k)
+        columns = pl.ds(0, 2 * hid if last_dp - far < early_count else 3 * hid)
         return remote(
-            mlp_grads.at[goal(way, far) * 4 + plane[k][1]],
-            line_slots.at[slot],
+            mlp_grads.at[goal(way, far) * 4 + plane[k][1], :, columns],
+            line_slots.at[slot, :, columns],
             line_send_sem.at[slot],
             line_recv_sem.at[slot],
             line_dev(way),
@@ -1111,10 +1175,41 @@
 
     def came(way, far, k):
         slot = slot_of(way, far, k)
-        block = line_slots.at[slot]
-        remote(
-            block, block, line_send_sem.at[slot], line_recv_sem.at[slot], line_dev(way)
-        ).wait_recv()
+
+        def wait(count):
+            block = line_slots.at[slot, :, pl.ds(0, count)]
+            remote(
+                block, block, line_send_sem.at[slot], line_recv_sem.at[slot], line_dev(way)
+            ).wait_recv()
+
+        def wait_both():
+            wait(2 * hid)
+            early_load(way, last_dp - far, k).wait()
+
+        if far == last_dp:
+            wait_both()
+        elif last_dp - far < early_count:
+            beside_first = takes_early(way, dp, last_dp)
+            pl.when(beside_first)(wait_both)
+            pl.when(jnp.logical_not(beside_first))(functools.partial(wait, 3 * hid))
+        else:
+            wait(3 * hid)
+
+    def early_load(way, index, k):
+        return pltpu.make_async_copy(
+            early.at[2 * index + way, plane[k][1]],
+            line_slots.at[slot_of(way, last_dp - index, k), :, pl.ds(2 * hid, hid)],
+            early_sem.at[(2 * index + way) * 4 + k],
+        )
+
+    def load_early(way):
+        for index in range(early_count):
+            for k in range(4):
+                early_load(way, index, k).start()
+
+    if line > 1:
+        for way in range(2):
+            pl.when(takes_early(way, dp, last_dp))(functools.partial(load_early, way))
 
     turn = (3, 1, 2, 0)
 
@@ -1320,8 +1415,33 @@
         )
 
     in_columns(3 * HD, weigh)
+
+    attn_parts = ((0, 5 * HD), (5 * HD, 128))
+
+    def attn_plane(k, place, part):
+        index = (k - 1) * n_dp + place
+        columns = pl.ds(*attn_parts[part])
+        return remote(
+            attn_blocks.at[place * 4 + plane[k][1], :, columns],
+            attn_plane_take.at[index, :, columns],
+            attn_plane_send_sem.at[2 * index + part],
+            attn_plane_recv_sem.at[2 * index + part],
+            plane[k],
+        )
+
+    def give_attn(part):
+        first, count = attn_parts[part]
+        for block in range(n_dp * 4):
+            attn_blocks[block, :, first : first + count] = attn_grads[
+                block * owned : (block + 1) * owned, first : first + count
+            ].astype(bf16)
+        for place in range(n_dp):
+            for k in (3, 1, 2):
+                attn_plane(k, place, part).start()
+
+    give_attn(0)
     move(1)
-    start_first([(1, k) for k in turn[:2]])
+    start_first([(1, k) for k in turn])
 
     def back(start, size):
         columns = pl.ds(start, size)
@@ -1374,27 +1494,13 @@
     small_rows[0:8] = small_rows[0:8] + small_take[...]
     attn_grads[0:width, 5 * HD : 5 * HD + 128] = small_rows[...].T
 
-    for block in range(n_dp * 4):
-        attn_blocks[block] = attn_grads[block * owned : (block + 1) * owned, :].astype(bf16)
-
-    def attn_plane(k, place):
-        index = (k - 1) * n_dp + place
-        return remote(
-            attn_blocks.at[place * 4 + plane[k][1]],
-            attn_plane_take.at[index],
-            attn_plane_send_sem.at[index],
-            attn_plane_recv_sem.at[index],
-            plane[k],
-        )
-
-    for place in range(n_dp):
-        for k in (3, 1, 2):
-            attn_plane(k, place).start()
+    give_attn(1)
     move(len(events) - 4)
     for place in range(n_dp):
         total = attn_blocks[place * 4 + ctx].astype(f32)
         for k in (1, 2, 3):
-            attn_plane(k, place).wait_recv()
+            attn_plane(k, place, 0).wait_recv()
+            attn_plane(k, place, 1).wait_recv()
             total = total + attn_plane_take[(k - 1) * n_dp + place].astype(f32)
         attn_sums[place] = total.astype(bf16)
 
@@ -1430,11 +1536,10 @@
     for way in range(2):
         if line > 1:
             pl.when(is_first(way))(functools.partial(attn_start, way))
-    start_first([(1, k) for k in turn[2:]])
+    move(4)
     for far in range(line - 2, 0, -1):
         for way in range(2):
             pl.when(not_first(way) & has_goal(way, far))(functools.partial(attn_pass, way, far))
-    move(4)
     if line == 1:
         attn_reduced[...] = attn_sums[...]
     else:
@@ -1474,7 +1579,8 @@
     exchange.wait_send()
     for place in range(n_dp):
         for k in (1, 2, 3):
-            attn_plane(k, place).wait_send()
+            attn_plane(k, place, 0).wait_send()
+            attn_plane(k, place, 1).wait_send()
 
     def first_left(way):
         for far in range(last_dp, 0, -1):
@@ -1518,7 +1624,7 @@
             jax.ShapeDtypeStruct((2, owned, HD), bf16),
         ),
         in_specs=[
-            anywhere if index < 5 or 11 <= index <= 16 or index == 18 else vmem
+            anywhere if index < 5 or 11 <= index <= 16 or index >= 18 else vmem
             for index in range(len(arrays))
         ],
         out_specs=(anywhere, anywhere, anywhere, vmem, anywhere),
@@ -1547,13 +1653,14 @@
             dma((8 * line,)),
             dma((8,)),
             dma((8,)),
-            dma((4 * n_dp,)),
-            dma((4 * n_dp,)),
+            dma((6 * n_dp,)),
+            dma((6 * n_dp,)),
             dma((2 * line,)),
             dma((2 * line,)),
             dma((7,)),
             dma((7,)),
             dma((12,)),
+            dma((16,)),
             pltpu.VMEM(mlp_grads.shape, bf16),
         ]
         + [
@@ -1663,6 +1770,7 @@
     half_ff = gate_up.shape[2]
     wide = -(-half_ff // (n_ctx * 128)) * 128
     behind = WIN
+    line = n_dp if n_dp <= 4 else 1
     ctx_place = lax.axis_index("ctx")
     core_first = lax.axis_index("tensor") == 0
     score_scale = HD ** (-0.5)
@@ -1689,16 +1797,16 @@
     )
     mlp_pack = jnp.moveaxis(mlp_pack, 1, 0)
 
-    start_row = ctx_place * row_count
-    row_index = jnp.arange(row_count, dtype=jnp.int32)
-    query_position = token_layout(lengths[0], start_row + row_index)[1]
-    query_cosine, query_sine = rope_tables(query_position)
-    lowest = jnp.maximum(row_index - query_position + behind, row_index + 1)[:, None]
+    exponent = np.arange(HD // 2, dtype=np.float32) * np.float32(2.0 / HD)
+    inverse = jnp.power(jnp.float32(rope_base), -jnp.asarray(exponent))[None]
     (
         mlp_full,
         gain_rows,
         head_rows,
         log_total,
+        query_cosine,
+        query_sine,
+        lowest,
         attn_full,
         normed_one,
         lin,
@@ -1708,10 +1816,10 @@
         branch_raw,
         middle,
         group_rows,
-    ) = attend_call(
-        n_dp, owned_heads, behind, tokens, query_cosine, query_sine, lowest, attn_pack, mlp_pack
-    )
-    result, normed_two_grad, gain_three_part, mlp_grads = mlp_call(
+    ) = attend_call(n_dp, owned_heads, behind, tokens, lengths, inverse, attn_pack, mlp_pack)
+    result, normed_two_grad, gain_three_part, mlp_grads, early = mlp_call(
+        n_dp,
+        line,
         group_rows,
         middle,
         out_cotangent,
@@ -1719,7 +1827,6 @@
         mlp_full.reshape(n_dp * n_ctx * owned, 3 * wide),
     )
 
-    line = n_dp if n_dp <= 4 else 1
 
     mlp_grads = mlp_grads.reshape(n_dp, n_ctx, owned, 3 * wide)
     if line == 1:
@@ -1748,6 +1855,7 @@
         attended_low,
         log_total,
         mlp_grads,
+        early.reshape(early.shape[0], -1, owned, wide),
     )
     if line == 1:
         attn_reduced = lax.psum_scatter(attn_reduced, "dp", scatter_dimension=0, tiled=True)

time: 404 us -> 382 us (0.946)
  Pallas kernels: 380 us -> 359 us
    pallas_call x1, Pallas kernels: 123 us -> 101 us  [retreat_call(): pl.pallas_call(functools.partial(retreat_kernel, n_dp, line, owned_heads)...]
where the time goes in v4:
time: 382 us; the launch traced here: 374 us
  Pallas kernels  359 us (94%)
  other arithmetic  7.21 us (2%)
  local copies, waits for them, and re-layouts  6.71 us (2%)
    pallas_call x1, Pallas kernels, mlp_call(): pl.pallas_call(functools.partial(mlp_kernel, n_dp, line), out_shape=(jax....  127 us
    pallas_call x1, Pallas kernels, attend_call(): pl.pallas_call(functools.partial(attend_kernel, n_dp, owned_heads), out_s...  118 us
    pallas_call x1, Pallas kernels, retreat_call(): pl.pallas_call(functools.partial(retreat_kernel, n_dp, line, owned_heads)...  101 us
    pallas_call x1, Pallas kernels, update_call(): pl.pallas_call(kernel, grid=(blocks,), in_specs=[*passed_blocks, whole(sm...  12.9 us

profile of v4, /device:TPU:9, one launch (start us, length us, event | category | flops | bytes accessed | tf_op | source)
XLA Modules:
  0.0 374.4 jit_solution(3997198328800685356)
XLA Ops:
  0.7 0.0 copy-start
  0.7 0.8 convert.15
  1.5 0.7 convert.14
  2.2 0.1 copy.60
  2.3 0.9 dynamic-slice_convert_fusion
  3.2 0.9 convert_element_type.33
  4.1 0.9 convert_element_type.35
  5.1 0.7 fusion.1.attn_pack
  5.8 1.3 convert_element_type.38
  7.1 0.0 copy-done
  7.1 0.1 copy.75
  7.2 0.1 slice_bitcast_fusion.1
  7.4 0.1 copy_bitcast_fusion.1
  7.5 1.2 maximum_bitcast_fusion.mlp_pack
  8.8 118.3 %attend.1 = (bf16[16,72,2688]{2,1,0:T(8,128)(2,1)}, f32[8,1152]{1,0:T(8,128)}, f32[8,256]{1,0:T(8,128)}, f32[2,768,1]{2,1,0:T(8,128)}, f32[768,128]{1,0:T(8,128)...) custom-call(bf16[768,1152]{1,0:T(8,128)(2,1)} %tokens_in.3, ...), custom_call_target="tpu_custom_call" | custom-call | flops 4000000000 | bytes 31457280 | tf_op jit(solution)/shard_map/attend/pallas_call | solution.py:617
  127.1 127.5 %feed_forward.1 = (bf16[768,1152]{1,0:T(8,128)(2,1)}, f32[384,1152]{1,0:T(8,128)}, f32[1,1152]{1,0:T(1,128)}, bf16[1152,2688]{1,0:T(8,128)(2,1)}, bf16[4,288,896]{2,1,0:T(8,128)(2,1)}) custom-call(bf16[4,2,384,1152]{3,2,1,0:T(8,128)(2,1)} %get-tuple-element.72.rows_in, f32[384,1152]{1,0:T(8,128)} %get-tuple-element.73.middle_in.middle, ...), custom_call_target="tpu_custom_call" | custom-call | flops 57076088832 | bytes 31457280 | tf_op jit(solution)/shard_map/feed_forward/pallas_call | solution.py:966
  254.5 100.6 %retreat.1 = (f32[768,1152]{1,0:T(8,128)}, bf16[4,72,1792]{2,1,0:T(8,128)(2,1)}, bf16[4,72,896]{2,1,0:T(8,128)(2,1)}, bf16[1,72,1408]{2,1,0:T(8,128)(2,1)}, bf16[2,72,256]{2,1,0:T(8,128)(2,1)}) custom-call(f32[384,1152]{1,0:T(8,128)} %get-tuple-element.77.back_sum, f32[384,1152]{1,0:T(8,128)} %get-tuple-element.73.middle_in.middle, ...), custom_call_target="tpu_custom_call" | custom-call | flops 10000000000 | bytes 41943040 | tf_op jit(solution)/shard_map/retreat/pallas_call | solution.py:1617
  355.1 1.1 copy.65
  356.3 0.6 convert_bitcast_fusion.small_ref
  356.9 2.4 reshape.76
  359.3 0.4 copy.76
  359.7 1.3 reshape.77.gate_ref
  361.0 12.9 %update.1 = (f32[72,512]{1,0:T(8,128)}, f32[72,512]{1,0:T(8,128)}, f32[72,512]{1,0:T(8,128)}, f32[72,512]{1,0:T(8,128)}, f32[72,512]{1,0:T(8,128)}, /*index=5*/f...) custom-call(bf16[768,1152]{1,0:T(8,128)(2,1)} %get-tuple-element.76., ...), custom_call_target="tpu_custom_call" | custom-call | tf_op jit(solution)/shard_map/update/pallas_call | solution.py:1720
  (5 shorter events, 0.2 us)
Async XLA Ops:
  0.7 6.4 %copy-start = (f32[72,2,3456]{2,1,0:T(2,128)S(1)}, f32[72,2,3456]{2,1,0:T(2,128)}, u32[]{:S(2)}) copy-start(f32[72,2,3456]{2,1,0:T(2,128)} %refs_9_.1) | copy-start | bytes 5971972

commit v5 on v4

--- a/solution.py
+++ b/solution.py
@@ -890,27 +890,28 @@
     scatter_rest(scatter, 3)
     sent(gather)
 
-    def weigh(first, right):
-        def one(i, carry):
-            at = pl.ds(pl.multiple_of(i * 384, 128), 384)
-            left = (rows if right is pair else grads)[:, :, :, at].reshape(8 * half, 384)
-            product = contract_rows(left, right[...].reshape(8 * half, right.shape[2]))
-            weights[at, first : first + right.shape[2]] = product.astype(bf16)
-            return carry
-
-        lax.fori_loop(0, width // 384, one, 0)
-        columns = pl.ds(first, right.shape[2])
-        copy = pltpu.make_async_copy(
-            weights.at[:, columns], weights_out.at[:, columns], out_sem.at[first // (2 * hid)]
-        )
-        copy.start()
-        return copy
-
-    down_out = weigh(2 * hid, hidden)
-
     dp, ctx, _ = places()
     last_dp = line - 1
     group = width // line
+    chunk_rows = 384
+    chunks = width // chunk_rows
+
+    def weigh(first, left, right, i):
+        chunk = jnp.where(2 * dp < n_dp, chunks - 1 - i, i)
+        at = pl.ds(pl.multiple_of(chunk * chunk_rows, 128), chunk_rows)
+        product = contract_rows(
+            left[:, :, :, at].reshape(8 * half, chunk_rows),
+            right[...].reshape(8 * half, right.shape[2]),
+        )
+        weights[at, first : first + right.shape[2]] = product.astype(bf16)
+
+    def leave(first, count, index):
+        columns = pl.ds(first, count)
+        copy = pltpu.make_async_copy(
+            weights.at[:, columns], weights_out.at[:, columns], out_sem.at[index]
+        )
+        copy.start()
+        return copy
 
     def early_copy(way, index):
         place = last_dp - index if way == 0 else index
@@ -923,11 +924,17 @@
     def sends_early(way):
         return dp == 0 if way == 0 else dp == last_dp
 
-    if line > 1:
+    for i in range(chunks):
+        weigh(2 * hid, grads, hidden, i)
         for way, index in early_items(line):
-            pl.when(sends_early(way))(early_copy(way, index).start)
+            if i * chunk_rows < (index + 1) * group <= (i + 1) * chunk_rows:
+                pl.when(sends_early(way))(early_copy(way, index).start)
+    down_out = leave(2 * hid, hid, 1)
+    weigh(0, rows, pair, 0)
     scatter_end(scatter)
-    gate_out = weigh(0, pair)
+    for i in range(1, chunks):
+        weigh(0, rows, pair, i)
+    gate_out = leave(0, 2 * hid, 0)
     scatter_wait(scatter)
 
     def finish_rows(first, size, carry):

time: 382 us -> 378 us (0.990)
  Pallas kernels: 359 us -> 355 us
    pallas_call x1, Pallas kernels: 127 us -> 123 us  [mlp_call(): pl.pallas_call(functools.partial(mlp_kernel, n_dp, line), out_shape=(jax....]
where the time goes in v5:
time: 378 us; the launch traced here: 370 us
  Pallas kernels  355 us (94%)
  other arithmetic  7.21 us (2%)
  local copies, waits for them, and re-layouts  6.71 us (2%)
    pallas_call x1, Pallas kernels, mlp_call(): pl.pallas_call(functools.partial(mlp_kernel, n_dp, line), out_shape=(jax....  123 us
    pallas_call x1, Pallas kernels, attend_call(): pl.pallas_call(functools.partial(attend_kernel, n_dp, owned_heads), out_s...  118 us
    pallas_call x1, Pallas kernels, retreat_call(): pl.pallas_call(functools.partial(retreat_kernel, n_dp, line, owned_heads)...  101 us
    pallas_call x1, Pallas kernels, update_call(): pl.pallas_call(kernel, grid=(blocks,), in_specs=[*passed_blocks, whole(sm...  12.9 us

profile of v5, /device:TPU:9, one launch (start us, length us, event | category | flops | bytes accessed | tf_op | source)
XLA Modules:
  0.0 370.4 jit_solution(11697337346429039298)
XLA Ops:
  0.7 0.0 copy-start
  0.7 0.8 convert.15
  1.5 0.7 convert.14
  2.2 0.1 copy.60
  2.3 0.9 dynamic-slice_convert_fusion
  3.2 0.9 convert_element_type.33
  4.1 0.9 convert_element_type.35
  5.1 0.7 fusion.1.attn_pack
  5.8 1.3 convert_element_type.38
  7.1 0.0 copy-done
  7.1 0.1 copy.75
  7.2 0.1 slice_bitcast_fusion.1
  7.4 0.1 copy_bitcast_fusion.1
  7.5 1.2 maximum_bitcast_fusion.mlp_pack
  8.8 118.3 %attend.1 = (bf16[16,72,2688]{2,1,0:T(8,128)(2,1)}, f32[8,1152]{1,0:T(8,128)}, f32[8,256]{1,0:T(8,128)}, f32[2,768,1]{2,1,0:T(8,128)}, f32[768,128]{1,0:T(8,128)...) custom-call(bf16[768,1152]{1,0:T(8,128)(2,1)} %tokens_in.3, ...), custom_call_target="tpu_custom_call" | custom-call | flops 4000000000 | bytes 31457280 | tf_op jit(solution)/shard_map/attend/pallas_call | solution.py:617
  127.1 122.8 %feed_forward.1 = (bf16[768,1152]{1,0:T(8,128)(2,1)}, f32[384,1152]{1,0:T(8,128)}, f32[1,1152]{1,0:T(1,128)}, bf16[1152,2688]{1,0:T(8,128)(2,1)}, bf16[4,288,896]{2,1,0:T(8,128)(2,1)}) custom-call(bf16[4,2,384,1152]{3,2,1,0:T(8,128)(2,1)} %get-tuple-element.72.rows_in, f32[384,1152]{1,0:T(8,128)} %get-tuple-element.73.middle_in.middle, ...), custom_call_target="tpu_custom_call" | custom-call | flops 57076088832 | bytes 31457280 | tf_op jit(solution)/shard_map/feed_forward/pallas_call | solution.py:973
  249.9 101.2 %retreat.1 = (f32[768,1152]{1,0:T(8,128)}, bf16[4,72,1792]{2,1,0:T(8,128)(2,1)}, bf16[4,72,896]{2,1,0:T(8,128)(2,1)}, bf16[1,72,1408]{2,1,0:T(8,128)(2,1)}, bf16[2,72,256]{2,1,0:T(8,128)(2,1)}) custom-call(f32[384,1152]{1,0:T(8,128)} %get-tuple-element.77.back_sum, f32[384,1152]{1,0:T(8,128)} %get-tuple-element.73.middle_in.middle, ...), custom_call_target="tpu_custom_call" | custom-call | flops 10000000000 | bytes 41943040 | tf_op jit(solution)/shard_map/retreat/pallas_call | solution.py:1624
  351.1 1.1 copy.65
  352.2 0.6 convert_bitcast_fusion.small_ref
  352.9 2.4 reshape.76
  355.3 0.4 copy.76
  355.7 1.3 reshape.77.gate_ref
  357.0 12.9 %update.1 = (f32[72,512]{1,0:T(8,128)}, f32[72,512]{1,0:T(8,128)}, f32[72,512]{1,0:T(8,128)}, f32[72,512]{1,0:T(8,128)}, f32[72,512]{1,0:T(8,128)}, /*index=5*/f...) custom-call(bf16[768,1152]{1,0:T(8,128)(2,1)} %get-tuple-element.76., ...), custom_call_target="tpu_custom_call" | custom-call | tf_op jit(solution)/shard_map/update/pallas_call | solution.py:1727
  (5 shorter events, 0.2 us)
Async XLA Ops:
  0.7 6.4 %copy-start = (f32[72,2,3456]{2,1,0:T(2,128)S(1)}, f32[72,2,3456]{2,1,0:T(2,128)}, u32[]{:S(2)}) copy-start(f32[72,2,3456]{2,1,0:T(2,128)} %refs_9_.1) | copy-start | bytes 5971972

commit v6 on v5

--- a/solution.py
+++ b/solution.py
@@ -1317,6 +1317,8 @@
 
     halves(False).start()
     halves(True).wait_recv()
+    held[4].wait()
+    move(1)
 
     def inward(start, size):
         grad = jnp.dot(
@@ -1328,11 +1330,12 @@
 
     held[1].wait()
     in_columns(2 * HD, inward)
+    move(1)
 
     block_rows = 256
     reach = block_rows + behind
     keyval_grad[...] = jnp.zeros_like(keyval_grad)
-    for load in held[2:5]:
+    for load in held[2:4]:
         load.wait()
 
     def retreat(first, head):
@@ -1436,19 +1439,22 @@
             plane[k],
         )
 
+    def place_at(i):
+        return jnp.where(2 * dp < n_dp, n_dp - 1 - i, i)
+
     def give_attn(part):
         first, count = attn_parts[part]
         for block in range(n_dp * 4):
             attn_blocks[block, :, first : first + count] = attn_grads[
                 block * owned : (block + 1) * owned, first : first + count
             ].astype(bf16)
-        for place in range(n_dp):
+        for i in range(n_dp):
             for k in (3, 1, 2):
-                attn_plane(k, place, part).start()
+                attn_plane(k, place_at(i), part).start()
 
     give_attn(0)
     move(1)
-    start_first([(1, k) for k in turn])
+    start_first([(1, k) for k in turn[:2]])
 
     def back(start, size):
         columns = pl.ds(start, size)
@@ -1503,14 +1509,6 @@
 
     give_attn(1)
     move(len(events) - 4)
-    for place in range(n_dp):
-        total = attn_blocks[place * 4 + ctx].astype(f32)
-        for k in (1, 2, 3):
-            attn_plane(k, place, 0).wait_recv()
-            attn_plane(k, place, 1).wait_recv()
-            total = total + attn_plane_take[(k - 1) * n_dp + place].astype(f32)
-        attn_sums[place] = total.astype(bf16)
-
     def attn_hop(way, far, first):
         source = attn_sums.at[goal(way, far)] if first else attn_slots.at[way * line + far + 1]
         index = way * line + far
@@ -1529,9 +1527,22 @@
             block, block, attn_line_send_sem.at[index], attn_line_recv_sem.at[index], line_dev(way)
         ).wait_recv()
 
-    def attn_start(way):
-        for far in range(last_dp, 0, -1):
-            attn_hop(way, far, True).start()
+    def attn_leave(way, far):
+        attn_hop(way, far, True).start()
+
+    for i in range(n_dp):
+        place = place_at(i)
+        total = attn_blocks[place * 4 + ctx].astype(f32)
+        for k in (1, 2, 3):
+            attn_plane(k, place, 0).wait_recv()
+            attn_plane(k, place, 1).wait_recv()
+            total = total + attn_plane_take[(k - 1) * n_dp + place].astype(f32)
+        attn_sums[place] = total.astype(bf16)
+        if i < last_dp:
+            for way in range(2):
+                pl.when(is_first(way))(functools.partial(attn_leave, way, last_dp - i))
+        if i < 2:
+            start_first([(1, turn[2 + i])])
 
     def attn_pass(way, far):
         attn_came(way, far + 1)
@@ -1540,13 +1551,11 @@
         attn_slots[index] = total.astype(bf16)
         attn_hop(way, far, False).start()
 
-    for way in range(2):
-        if line > 1:
-            pl.when(is_first(way))(functools.partial(attn_start, way))
-    move(4)
     for far in range(line - 2, 0, -1):
         for way in range(2):
             pl.when(not_first(way) & has_goal(way, far))(functools.partial(attn_pass, way, far))
+        move(2)
+    move(len(events))
     if line == 1:
         attn_reduced[...] = attn_sums[...]
     else:

time: 378 us -> 373 us (0.987)
  no operation moved by 1% of the time
where the time goes in v6:
time: 373 us; the launch traced here: 368 us
  Pallas kernels  353 us (95%)
  other arithmetic  7.21 us (2%)
  local copies, waits for them, and re-layouts  6.71 us (2%)
    pallas_call x1, Pallas kernels, mlp_call(): pl.pallas_call(functools.partial(mlp_kernel, n_dp, line), out_shape=(jax....  123 us
    pallas_call x1, Pallas kernels, attend_call(): pl.pallas_call(functools.partial(attend_kernel, n_dp, owned_heads), out_s...  118 us
    pallas_call x1, Pallas kernels, retreat_call(): pl.pallas_call(functools.partial(retreat_kernel, n_dp, line, owned_heads)...  98.8 us
    pallas_call x1, Pallas kernels, update_call(): pl.pallas_call(kernel, grid=(blocks,), in_specs=[*passed_blocks, whole(sm...  12.9 us

profile of v6, /device:TPU:9, one launch (start us, length us, event | category | flops | bytes accessed | tf_op | source)
XLA Modules:
  0.0 368.0 jit_solution(2598946470016757464)
XLA Ops:
  0.7 0.0 copy-start
  0.7 0.8 convert.15
  1.5 0.7 convert.14
  2.2 0.1 copy.60
  2.3 0.9 dynamic-slice_convert_fusion
  3.2 0.9 convert_element_type.33
  4.1 0.9 convert_element_type.35
  5.1 0.7 fusion.1.attn_pack
  5.8 1.3 convert_element_type.38
  7.1 0.0 copy-done
  7.1 0.1 copy.75
  7.2 0.1 slice_bitcast_fusion.1
  7.4 0.1 copy_bitcast_fusion.1
  7.5 1.2 maximum_bitcast_fusion.mlp_pack
  8.8 118.3 %attend.1 = (bf16[16,72,2688]{2,1,0:T(8,128)(2,1)}, f32[8,1152]{1,0:T(8,128)}, f32[8,256]{1,0:T(8,128)}, f32[2,768,1]{2,1,0:T(8,128)}, f32[768,128]{1,0:T(8,128)...) custom-call(bf16[768,1152]{1,0:T(8,128)(2,1)} %tokens_in.3, ...), custom_call_target="tpu_custom_call" | custom-call | flops 4000000000 | bytes 31457280 | tf_op jit(solution)/shard_map/attend/pallas_call | solution.py:617
  127.1 122.8 %feed_forward.1 = (bf16[768,1152]{1,0:T(8,128)(2,1)}, f32[384,1152]{1,0:T(8,128)}, f32[1,1152]{1,0:T(1,128)}, bf16[1152,2688]{1,0:T(8,128)(2,1)}, bf16[4,288,896]{2,1,0:T(8,128)(2,1)}) custom-call(bf16[4,2,384,1152]{3,2,1,0:T(8,128)(2,1)} %get-tuple-element.72.rows_in, f32[384,1152]{1,0:T(8,128)} %get-tuple-element.73.middle_in.middle, ...), custom_call_target="tpu_custom_call" | custom-call | flops 57076088832 | bytes 31457280 | tf_op jit(solution)/shard_map/feed_forward/pallas_call | solution.py:973
  249.9 98.8 %retreat.1 = (f32[768,1152]{1,0:T(8,128)}, bf16[4,72,1792]{2,1,0:T(8,128)(2,1)}, bf16[4,72,896]{2,1,0:T(8,128)(2,1)}, bf16[1,72,1408]{2,1,0:T(8,128)(2,1)}, bf16[2,72,256]{2,1,0:T(8,128)(2,1)}) custom-call(f32[384,1152]{1,0:T(8,128)} %get-tuple-element.77.back_sum, f32[384,1152]{1,0:T(8,128)} %get-tuple-element.73.middle_in.middle, ...), custom_call_target="tpu_custom_call" | custom-call | flops 10000000000 | bytes 41943040 | tf_op jit(solution)/shard_map/retreat/pallas_call | solution.py:1633
  348.7 1.1 copy.65
  349.8 0.6 convert_bitcast_fusion.small_ref
  350.5 2.4 reshape.76
  352.8 0.4 copy.76
  353.3 1.3 reshape.77.gate_ref
  354.6 12.9 %update.1 = (f32[72,512]{1,0:T(8,128)}, f32[72,512]{1,0:T(8,128)}, f32[72,512]{1,0:T(8,128)}, f32[72,512]{1,0:T(8,128)}, f32[72,512]{1,0:T(8,128)}, /*index=5*/f...) custom-call(bf16[768,1152]{1,0:T(8,128)(2,1)} %get-tuple-element.76., ...), custom_call_target="tpu_custom_call" | custom-call | tf_op jit(solution)/shard_map/update/pallas_call | solution.py:1736
  (5 shorter events, 0.2 us)
Async XLA Ops:
  0.7 6.4 %copy-start = (f32[72,2,3456]{2,1,0:T(2,128)S(1)}, f32[72,2,3456]{2,1,0:T(2,128)}, u32[]{:S(2)}) copy-start(f32[72,2,3456]{2,1,0:T(2,128)} %refs_9_.1) | copy-start | bytes 5971972
